TPU v7x, 32 devices: a whole 2x2x4 slice. The times are simulated.
32 devices in a mesh: fix: 16 (over z, x, core), subj: 2 (over y).
Axes of the slice: x: 2, y: 2, z: 4, core: 2. Of those that a mesh axis runs over, the one named last changes fastest.
Arguments:
- fixels: float32 [16384, 256], P('fix', 'subj'), may hold values from -6 to 6
- conn_tiles: float32 [128, 4, 128, 128], P('fix'), may hold values from -0.25 to 0.25
- columns: int32 [128, 4], P('fix'), may hold values from 0 to 127, as said below
- nuisance: float32 [4, 256], P(None, 'subj'), may hold values from -5 to 5
- nuisance_pinv: float32 [4, 256], P(None, 'subj'), may hold values from -0.375 to 0.375
- contrast: float32 [4, 256], replicated, may hold values from -0.375 to 0.375
- perm_table: int32 [128, 256], P(None, 'subj'), may hold values from 0 to 255, each once within a row
Outputs:
- projections: float32 [512, 16384], P('subj', 'fix')
Inputs may be any that keep to these rules, and one draw needn't show every extreme that they name: `columns`: device j of fix holds blocks j * 8 to (j + 1) * 8 - 1. The 32 entries of one device's rows name blocks of any one device at most 2 times, and in every draw some device's blocks are named exactly 2 times by the rows of every device. `perm_table`: each row is a permutation of the 256 subjects.
All inputs are finite; a program needn't handle non-finite values.
Results may differ from a plain program's by a relative error of at most 0.000071.
Values sent between devices are 32-bit elements; how exact they have to be, the bound alone decides.
No kernel may reach another device: no remote copies, remote signals or barrier semaphores. Data moves between devices by JAX's collectives and lax.ppermute only.
A program may use at most 64 MiB of HBM per device.

v0:
```python
import jax
import jax.numpy as jnp
from jax import lax
from jax.sharding import PartitionSpec as P


def design_rows(contrast, perm_table):
    picked = jnp.take(contrast, perm_table, axis=1)
    return jnp.transpose(picked, (1, 0, 2)).reshape(-1, perm_table.shape[1])


def per_device(fixels, conn_tiles, columns, nuisance, nuisance_pinv, contrast, perm_table):
    fix_count = lax.axis_size("fix")
    block_count, per_row = columns.shape
    block_size = conn_tiles.shape[2]
    subj_count = fixels.shape[1]
    tile_total = block_count * per_row
    wanted = columns.reshape(tile_total)
    owners = wanted // block_count
    local_index = wanted % block_count
    capacity = (tile_total + fix_count - 1) // fix_count
    positions = jnp.arange(tile_total)
    earlier = positions[:, None] > positions[None, :]
    same_owner = owners[:, None] == owners[None, :]
    ranks = jnp.sum(jnp.logical_and(same_owner, earlier), axis=1)
    slots = owners * capacity + ranks
    request = jnp.zeros((fix_count * capacity,), jnp.int32).at[slots].set(local_index)
    asked = lax.all_to_all(
        request.reshape(fix_count, capacity), "fix", split_axis=0, concat_axis=0, tiled=True
    ).reshape(-1)
    design = design_rows(contrast, perm_table)
    own_blocks = fixels.reshape(block_count, block_size, subj_count)
    outgoing = jnp.take(own_blocks, asked, axis=0).reshape(
        fix_count, capacity, block_size, subj_count
    )
    arrived = lax.all_to_all(outgoing, "fix", split_axis=0, concat_axis=0, tiled=True).reshape(
        fix_count * capacity, block_size, subj_count
    )
    needed = jnp.take(arrived, slots, axis=0).reshape(block_count, per_row, block_size, subj_count)
    smoothed = jnp.einsum(
        "bkij,bkjs->bis", conn_tiles, needed, precision=lax.Precision.HIGHEST
    ).reshape(block_count * block_size, subj_count)
    fitted_part = jnp.einsum("ns,fs->nf", nuisance_pinv, smoothed, precision=lax.Precision.HIGHEST)
    fitted = lax.psum(fitted_part, "subj")
    residual = smoothed - jnp.einsum("nf,ns->fs", fitted, nuisance, precision=lax.Precision.HIGHEST)
    partial_value = jnp.einsum("cs,fs->cf", design, residual, precision=lax.Precision.HIGHEST)
    return lax.psum_scatter(partial_value, "subj", scatter_dimension=0, tiled=True)


def solution(mesh):
    placed = (
        P("fix", "subj"),
        P("fix", None, None, None),
        P("fix", None),
        P(None, "subj"),
        P(None, "subj"),
        P(),
        P(None, "subj"),
    )
    return jax.shard_map(
        per_device, mesh=mesh, in_specs=placed, out_specs=P("subj", "fix"), check_vma=False
    )
```

profile of v0, /device:TPU:0, one launch (start us, length us, event | category | flops | bytes accessed | tf_op | source)
XLA Modules:
  0.0 154.6 jit_solution(3575122768907073975)
XLA Ops:
  6.5 0.9 copy.40
  7.4 0.1 reshape.209
  7.5 0.1 reshape.210
  7.6 0.2 convert_reduce_fusion
  7.8 0.7 scatter_custom_fusion
  8.5 0.1 all_to_all.9
  8.6 13.6 %all_to_all.14 = s32[16,1,2]{2,1,0:T(1,128)S(1)} all-to-all(s32[16,1,2]{2,1,0:T(1,128)S(1)} %bitcast.43), channel_id=1, replica_groups=mesh['fix'=16,'subj'=2] {'fix'}, dimensions={0} | all-to-all | bytes 256 | tf_op jit(solution)/shard_map/all_to_all | solution.py:28
  22.1 0.5 broadcast.245
  22.7 0.7 reduce.3
  23.3 0.1 reshape.213
  23.4 0.1 copy.47
  23.5 0.1 copy.48
  23.6 3.1 %gather_fusion.1 = f32[32,128,128]{2,1,0:T(8,128)} fusion(f32[8,128,128]{2,1,0:T(8,128)} %bitcast.39, s32[1024]{0:T(1024)S(1)} %pad_clamp_fusion.1), kind=kCustom, calls=%fused_computation.1 | custom fusion | bytes 4194432 | tf_op jit(solution)/shard_map/jit(_take)/gather | solution.py:33
  26.7 3.1 %broadcast_select_fusion = f32[16,2,128,128]{3,2,1,0:T(8,128)} fusion(f32[16,2,128,128]{3,2,1,0:T(8,128)} %bitcast.38, pred[16,2]{1,0:T(8,128)(4,1)S(1)} %copy.48), kind=kLoop, calls=%fused_computation.9 | loop fusion | flops 524288 | bytes 4194336 | tf_op jit(solution)/shard_map/jit(_take)/select_n | solution.py:33
  29.8 4.6 %all-to-all-start.1 = ((f32[16,2,128,128]{3,2,1,0:T(8,128)}), f32[16,2,128,128]{3,2,1,0:T(8,128)}, u32[]{:S(2)}, u32[]{:S(2)}) async-start(f32[16,2,128,128]{3,2,1,0:T(8,128)} %broadcast_select_fusion), calls=%async_computation.1 | async-start | bytes 4194304 | tf_op jit(solution)/shard_map/all_to_all | solution.py:36
  34.4 0.0 reduce-scatter.2.cloned.1.call-start
  34.4 0.1 reduce_sum.14
  34.5 0.1 copy.38
  34.7 0.0 copy-done.1
  34.7 54.4 %gather_fusion = f32[16384,4]{1,0:T(8,128)} fusion(f32[4,256]{0,1:T(8,128)S(1)} %copy.38, s32[16384]{0:T(1024)S(1)} %bitcast_clamp_fusion), kind=kCustom, calls=%fused_computation | custom fusion | bytes 589824 | tf_op jit(solution)/shard_map/jit(_take)/gather | solution.py:8
  89.1 5.5 %copy.39 = f32[128,128,4]{1,2,0:T(4,128)S(1)} copy(f32[128,128,4]{2,1,0:T(8,128)} %bitcast.36) | data formatting | bytes 524288 | tf_op jit(solution)/shard_map/jit(_take)/gather | solution.py:8
  94.7 0.1 broadcast_select_fusion.1
  94.8 0.0 all-to-all-done.1
  94.8 3.6 %gather_fusion.2 = f32[32,128,128]{2,1,0:T(8,128)} fusion(f32[32,128,128]{2,1,0:T(8,128)} %bitcast.11, s32[1024]{0:T(1024)S(1)} %pad_clamp_fusion), kind=kCustom, calls=%fused_computation.2 | custom fusion | bytes 4194432 | tf_op jit(solution)/shard_map/jit(_take)/gather | solution.py:39
  98.4 4.1 %fusion = f32[8,128,128,1]{1,2,3,0:T(8,128)S(1)} fusion(f32[8,4,128,128]{3,2,1,0:T(8,128)S(1)} %copy-done, f32[8,4,128,128]{3,2,1,0:T(8,128)} %bitcast.37, pred[8,4]{1,0:T(8,128)(4,1)S(1)} %compare_and_fusion.1), kind=kOutput, calls=%fused_computation.4 | convolution fusion | flops 805830656 | bytes 4718624 | tf_op jit(solution)/shard_map/bkij,bkjs->bis/dot_general | solution.py:40
  102.6 0.0 copy-done.3
  102.6 0.5 convolution_bitcast_fusion
  103.1 8.2 %psum.7 = f32[4,1024]{1,0:T(4,128)S(1)} all-reduce(f32[4,1024]{1,0:T(4,128)S(1)} %convolution_bitcast_fusion), channel_id=1, replica_groups=mesh['fix'=16,'subj'=2] {'subj'}, use_global_device_ids=true, to_apply=%region_2.3 | all-reduce | flops 4096 | bytes 32768 | tf_op jit(solution)/shard_map/psum | solution.py:44
  111.3 1.0 convolution_subtract_fusion
  112.3 3.2 %fusion.14 = f32[512,1024]{1,0:T(8,128)} fusion(f32[512,128]{1,0:T(8,128)S(1)} %bitcast.42, f32[1024,128]{1,0:T(8,128)S(1)} %convolution_subtract_fusion), kind=kOutput, calls=%fused_computation.50 | convolution fusion | flops 805306368 | bytes 2883584 | tf_op jit(solution)/shard_map/cs,fs->cf/dot_general | solution.py:46
  115.5 0.0 reduce-scatter.2.cloned.1.call-update
  115.5 32.3 %reduce-scatter.2.cloned.1.call-done = f32[256,1024]{1,0:T(8,128)} async-done(((f32[512,1024]{1,0:T(8,128)}), f32[256,1024]{1,0:T(8,128)}) %reduce-scatter.2.cloned.1.call-update) | async-done | bytes 1048592 | tf_op jit(solution)/shard_map/reduce_scatter | solution.py:47
  (17 shorter events, 0.1 us)
Async XLA Ops:
  6.5 91.9 %copy-start = (f32[8,4,128,128]{3,2,1,0:T(8,128)S(1)}, f32[8,4,128,128]{3,2,1,0:T(8,128)}, u32[]{:S(2)}) copy-start(f32[8,4,128,128]{3,2,1,0:T(8,128)} %param.8) | copy-start | bytes 6291460
  29.8 4.7 %copy-start.2 = (f32[4,256]{1,0:T(4,128)S(1)}, f32[4,256]{1,0:T(4,128)}, u32[]{:S(2)}) copy-start(f32[4,256]{1,0:T(4,128)} %param.12) | copy-start | bytes 12292
  29.8 4.9 %copy-start.1 = (s32[128,128]{1,0:T(8,128)S(1)}, s32[128,128]{1,0:T(8,128)}, u32[]{:S(2)}) copy-start(s32[128,128]{1,0:T(8,128)} %param.13) | copy-start | bytes 196612
  29.8 65.0 %all-to-all-start.1 = ((f32[16,2,128,128]{3,2,1,0:T(8,128)}), f32[16,2,128,128]{3,2,1,0:T(8,128)}, u32[]{:S(2)}, u32[]{:S(2)}) async-start(f32[16,2,128,128]{3,2,1,0:T(8,128)} %broadcast_select_fusion), calls=%async_computation.1 | async-start | bytes 4194304 | tf_op jit(solution)/shard_map/all_to_all | solution.py:36
  34.4 113.4 %reduce-scatter.2.cloned.1.call-start = ((), (), s32[]{:S(2)}) async-start(), calls=%async_computation.3 | async-start | bytes 3145728 | tf_op jit(solution)/shard_map/reduce_scatter | solution.py:47
  98.4 4.1 %copy-start.3 = (f32[4,128]{1,0:T(4,128)S(1)}, f32[4,128]{1,0:T(4,128)}, u32[]{:S(2)}) copy-start(f32[4,128]{1,0:T(4,128)} %param.11) | copy-start | bytes 6148
  98.4 12.9 %copy-start.4 = (f32[4,128]{1,0:T(4,128)S(1)}, f32[4,128]{1,0:T(4,128)}, u32[]{:S(2)}) copy-start(f32[4,128]{1,0:T(4,128)} %param.10) | copy-start | bytes 6148
Sparse Core Ops, SparseCore 0:
  115.6 32.1 reduce-scatter.1
where the time goes:
time: 155 us
  local copies, waits for them, and re-layouts  69.4 us (45%)
  waiting for transfers between devices  32.3 us (21%)
  blocking collectives  21.8 us (14%)
  between operations  13.6 us (9%)
  matrix products  8.82 us (6%)
  starting transfers between devices  4.61 us (3%)
  other arithmetic  4.15 us (3%)
    gather x2, local copies, waits for them, and re-layouts, design_rows(): picked = jnp.take(contrast, perm_table, axis=1)  59.9 us
    reduce_scatter x1, waiting for transfers between devices, per_device(): lax.psum_scatter(partial_value, 'subj', scatter_dimension=0, tiled=True)  32.3 us
    all_to_all x1, blocking collectives, per_device(): lax.all_to_all(request.reshape(fix_count, capacity), 'fix', split_axis=0,...  13.6 us
    psum x1, blocking collectives, per_device(): fitted = lax.psum(fitted_part, 'subj')  8.19 us
    all_to_all x1, starting transfers between devices, per_device(): lax.all_to_all(outgoing, 'fix', split_axis=0, concat_axis=0, tiled=True)  4.57 us
    dot_general x1, matrix products, per_device(): jnp.einsum('bkij,bkjs->bis', conn_tiles, needed, precision=lax.Precision....  4.12 us
    gather x1, local copies, waits for them, and re-layouts, per_device(): jnp.take(arrived, slots, axis=0)  3.62 us
    dot_general x1, matrix products, per_device(): jnp.einsum('cs,fs->cf', design, residual, precision=lax.Precision.HIGHEST)  3.15 us
  transfers between devices with their start and end apart: 2, of which 1 were waited for; matrix products, arithmetic and copies ran while one was open for 39% of the time, Pallas kernels for 0%

commit v1 on v0

v1 whole, which is shorter than its diff:
```python
import functools

import jax
import jax.numpy as jnp
from jax import lax
from jax.experimental import pallas as pl
from jax.experimental.pallas import tpu as pltpu
from jax.sharding import PartitionSpec as P

GROUP = 4
LANES = 128
HIGHEST = lax.Precision.HIGHEST
ANY = pl.BlockSpec(memory_space=pl.ANY)
SMEM = pl.BlockSpec(memory_space=pltpu.SMEM)
VMEM = pl.BlockSpec(memory_space=pltpu.VMEM)


def pack_kernel(plan, piece_count, local_ref, line_ref, *refs):
    pieces = refs[:piece_count]
    outs = refs[piece_count:-1]
    sems = refs[-1]

    def copies(choice):
        return [
            pltpu.make_async_copy(
                pieces[choice if piece is None else piece].at[local_ref[entry]],
                outs[partner].at[place],
                sems.at[entry],
            )
            for entry, (piece, partner, place) in enumerate(plan)
        ]

    def run(choice):
        todo = copies(choice)
        for copy in todo:
            copy.start()
        for copy in todo:
            copy.wait()

    if plan[0][0] is None:
        upper = line_ref[0] != 0
        pl.when(upper)(lambda: run(0))
        pl.when(jnp.logical_not(upper))(lambda: run(1))
    else:
        run(0)


def pack(pieces, local, upper, cap, merged):
    groups, partners, _ = local.shape
    shape = pieces[0].shape[1:]
    plan = [
        (None if merged else piece, partner, piece * cap + rank)
        for piece in range(groups)
        for partner in range(partners)
        for rank in range(cap)
    ]
    size = groups * cap * partners * shape[0] * shape[1] * 4
    return pl.pallas_call(
        functools.partial(pack_kernel, plan, len(pieces)),
        out_shape=[jax.ShapeDtypeStruct((groups * cap,) + shape, jnp.float32)] * partners,
        in_specs=[SMEM, SMEM] + [ANY] * len(pieces),
        out_specs=[ANY] * partners,
        scratch_shapes=[pltpu.SemaphoreType.DMA((len(plan),))],
        cost_estimate=pl.CostEstimate(flops=0, bytes_accessed=2 * size, transcendentals=0),
    )(local.reshape(-1), upper, *pieces)


def split(value):
    high = value.astype(jnp.bfloat16)
    return high, (value - high.astype(jnp.float32)).astype(jnp.bfloat16)


def smooth_kernel(plan, per_row, source_count, first, tile_ref, local_ref, *refs):
    sources = refs[:source_count]
    conn = refs[source_count]
    before = None if first else refs[source_count + 1]
    out, blocks, tiles, here, sems = refs[source_count + (1 if first else 2) :]
    tile_total = blocks.shape[0]
    for t in range(tile_total):
        here[t] = 0
    for slot, (source, place) in enumerate(plan):
        tile = tile_ref[slot]

        @pl.when(tile >= 0)
        def _():
            index = local_ref[slot] if place is None else place
            here[tile] = 1
            pltpu.make_async_copy(
                sources[source].at[index], blocks.at[tile], sems.at[0, tile]
            ).start()
            pltpu.make_async_copy(conn.at[tile], tiles.at[tile], sems.at[1, tile]).start()

    if first:
        out[...] = jnp.zeros_like(out)
    else:
        out[...] = before[...]

    @pl.loop(0, tile_total)
    def _(t):
        @pl.when(here[t] != 0)
        def _():
            pltpu.make_async_copy(tiles.at[t], tiles.at[t], sems.at[1, t]).wait()
            pltpu.make_async_copy(blocks.at[t], blocks.at[t], sems.at[0, t]).wait()
            left_high, left_low = split(tiles[t])
            right_high, right_low = split(blocks[t])
            left = jnp.concatenate([left_high, left_low], axis=1)
            right = jnp.concatenate([right_high, right_low], axis=1)
            both = jnp.dot(
                left,
                jnp.concatenate([right, right], axis=0),
                preferred_element_type=jnp.float32,
            )
            width = blocks.shape[2]
            row = t // per_row
            out[row] += both[:, :width] + both[:, width:]


def smooth(plan, tile, local, sources, conn, before, block_count):
    tile_total, size, _ = conn.shape
    width = sources[0].shape[2]
    first = before is None
    extra = () if first else (before,)
    steps = min(tile_total, len(plan))
    return pl.pallas_call(
        functools.partial(
            smooth_kernel, plan, tile_total // block_count, len(sources), first
        ),
        out_shape=jax.ShapeDtypeStruct((block_count, size, width), jnp.float32),
        in_specs=[SMEM, SMEM] + [ANY] * (len(sources) + 1) + [VMEM] * len(extra),
        out_specs=VMEM,
        scratch_shapes=[
            pltpu.VMEM((tile_total, size, width), jnp.float32),
            pltpu.VMEM((tile_total, size, size), jnp.float32),
            pltpu.SMEM((tile_total,), jnp.int32),
            pltpu.SemaphoreType.DMA((2, tile_total)),
        ],
        compiler_params=pltpu.CompilerParams(vmem_limit_bytes=32 * 1024 * 1024),
        cost_estimate=pl.CostEstimate(
            flops=8 * steps * size * size * width,
            bytes_accessed=2 * steps * size * width * 4,
            transcendentals=0,
        ),
    )(tile, local, *sources, conn, *extra)


def design_kernel(perm_ref, contrast_ref, nuisance_ref, pinv_ref, out_ref, rows_ref):
    perms, subjects = perm_ref.shape
    regressors = contrast_ref.shape[0]
    for start in range(0, subjects, LANES):
        want = perm_ref[:, start : start + LANES].astype(jnp.int32)
        lane, part = want % LANES, want // LANES
        for r in range(regressors):
            value = jnp.zeros((perms, LANES), jnp.float32)
            for base in range(0, subjects, LANES):
                table = jnp.broadcast_to(
                    contrast_ref[r : r + 1, base : base + LANES], (perms, LANES)
                )
                found = jnp.take_along_axis(table, lane, axis=1, mode="promise_in_bounds")
                value = jnp.where(part == base // LANES, found, value)
            rows_ref[start // LANES, pl.ds(r, perms, stride=regressors), :] = value
    design = jnp.concatenate([rows_ref[i] for i in range(rows_ref.shape[0])], axis=1)
    result = design
    for n in range(nuisance_ref.shape[0]):
        weight = jnp.sum(design * nuisance_ref[n : n + 1, :], axis=1, keepdims=True)
        result = result - weight * pinv_ref[n : n + 1, :]
    out_ref[...] = result


def reduced_design(perm, contrast, nuisance, pinv):
    rows = perm.shape[0] * contrast.shape[0]
    subjects = perm.shape[1]
    return pl.pallas_call(
        design_kernel,
        out_shape=jax.ShapeDtypeStruct((rows, subjects), jnp.float32),
        in_specs=[VMEM] * 4,
        out_specs=VMEM,
        scratch_shapes=[pltpu.VMEM((subjects // LANES, rows, LANES), jnp.float32)],
        compiler_params=pltpu.CompilerParams(vmem_limit_bytes=32 * 1024 * 1024),
        cost_estimate=pl.CostEstimate(
            flops=32 * rows * subjects, bytes_accessed=8 * rows * subjects, transcendentals=0
        ),
    )(perm, contrast, nuisance, pinv)


def project(design, smoothed):
    return lax.dot_general(
        design, smoothed, (((1,), (1,)), ((), ())), precision=HIGHEST
    )


def per_device(fixels, conn_tiles, columns, nuisance, nuisance_pinv, contrast, perm_table):
    fix_count = lax.axis_size("fix")
    subj_count = lax.axis_size("subj")
    group = GROUP if fix_count % GROUP == 0 else 1
    lines = fix_count // group
    block_count, per_row = columns.shape
    size = conn_tiles.shape[2]
    width = fixels.shape[1]
    tile_total = block_count * per_row
    cap = (tile_total + fix_count - 1) // fix_count
    me = lax.axis_index("fix")
    line, member = me // group, me % group
    part = lax.axis_index("subj")

    own = fixels.reshape(block_count, size, width)
    up, down = {0: own}, {0: own}
    for hop in range(1, lines):
        up[hop] = lax.ppermute(
            up[hop - 1],
            "fix",
            [(i, i + group) for i in range(fix_count - group) if i // group >= hop - 1],
        )
        down[hop] = lax.ppermute(
            down[hop - 1],
            "fix",
            [(i, i - group) for i in range(group, fix_count) if i // group <= lines - hop],
        )

    named = [columns.reshape(-1)] + [
        lax.ppermute(columns, "fix", [(i, i ^ m) for i in range(fix_count)]).reshape(-1)
        for m in range(1, group)
    ]
    named = jnp.stack(named)
    owners, locals_ = named // block_count, named % block_count
    positions = jnp.arange(tile_total)
    earlier = positions[:, None] > positions[None, :]
    same = owners[:, :, None] == owners[:, None, :]
    ranks = jnp.sum(jnp.logical_and(same, earlier[None]).astype(jnp.int32), axis=2)
    rank_of = jnp.arange(cap)

    def lookup(who, owner_list, values):
        owner_list = jnp.asarray(owner_list)
        hit = jnp.logical_and(
            owners[who] == owner_list[..., None, None],
            ranks[who] == rank_of[:, None],
        )
        return jnp.sum(jnp.where(hit, values, 0), axis=-1)

    stages = []
    for hop in range(lines):
        if hop == 0:
            stages.append((hop, [own], [line], False))
        elif 2 * hop > lines - 1:
            far = jnp.where(line >= hop, line - hop, line + hop)
            stages.append((hop, [up[hop], down[hop]], [far], True))
        else:
            stages.append((hop, [up[hop], down[hop]], [line - hop, line + hop], False))

    early, late = ([], [], [], []), ([], [], [], [])
    for hop, pieces, origins, merged in stages:
        plan, tile, local, sources = late if hop == lines - 1 and hop > 0 else early
        upper = (line >= hop).astype(jnp.int32).reshape(1)
        asked = jnp.stack(
            [
                jnp.stack(
                    [lookup(m, origin * group + member, locals_[m]) for m in range(1, group)]
                )
                for origin in origins
            ]
        )
        packs = pack(pieces, asked, upper, cap, merged)
        sides = [z for z in range(lines) if z >= hop or z <= lines - 1 - hop]
        pairs = [(i, i) for i in range(fix_count) if i // group in sides]
        got = [
            lax.ppermute(packs[m - 1], "fix", [(i, i ^ m) for i, _ in pairs])
            for m in range(1, group)
        ]
        base = len(sources)
        sources.extend(pieces)
        sources.extend(got)
        own_tile = [lookup(0, origin * group + member, positions + 1) - 1 for origin in origins]
        own_local = [lookup(0, origin * group + member, locals_[0]) for origin in origins]
        for place, origin in enumerate(origins):
            for choice in range(2 if merged else 1):
                source = base + (choice if merged else place)
                for rank in range(cap):
                    plan.append((source, None))
                if merged:
                    mine = (line >= hop) if choice == 0 else (line < hop)
                    tile.append(jnp.where(mine, own_tile[place], -1))
                else:
                    tile.append(own_tile[place])
                local.append(own_local[place])
            for m in range(1, group):
                for rank in range(cap):
                    plan.append((base + len(pieces) + m - 1, place * cap + rank))
                tile.append(lookup(0, origin * group + (member ^ m), positions + 1) - 1)
                local.append(jnp.zeros((cap,), jnp.int32))

    conn = conn_tiles.reshape(tile_total, size, size)
    smoothed = None
    for plan, tile, local, sources in (early, late):
        if plan:
            smoothed = smooth(
                tuple(plan),
                jnp.concatenate(tile).astype(jnp.int32),
                jnp.concatenate(local).astype(jnp.int32),
                sources,
                conn,
                smoothed,
                block_count,
            )
    smoothed = smoothed.reshape(block_count * size, width)

    rows = perm_table.shape[0] // subj_count
    shares, halves = [], []
    for shift in range(subj_count):
        to = (part + shift) % subj_count
        share = jnp.concatenate(
            [
                lax.dynamic_slice_in_dim(perm_table, to * rows, rows, 0).astype(jnp.float32),
                nuisance,
                nuisance_pinv,
            ]
        )
        half = smoothed
        if shift:
            pairs = [(i, (i + shift) % subj_count) for i in range(subj_count)]
            share = lax.ppermute(share, "subj", pairs)
            half = lax.ppermute(half, "subj", pairs)
        shares.append(share)
        halves.append(half)
    shares = jnp.concatenate(shares, axis=1)
    count = nuisance.shape[0]
    design = reduced_design(
        shares[:rows],
        contrast,
        shares[rows : rows + count],
        shares[rows + count :],
    )
    total = None
    for shift, half in enumerate(halves):
        term = project(design[:, shift * width : (shift + 1) * width], half)
        total = term if total is None else total + term
    return total


def solution(mesh):
    placed = (
        P("fix", "subj"),
        P("fix", None, None, None),
        P("fix", None),
        P(None, "subj"),
        P(None, "subj"),
        P(),
        P(None, "subj"),
    )
    return jax.shard_map(
        per_device, mesh=mesh, in_specs=placed, out_specs=P("subj", "fix"), check_vma=False
    )
```

time: 155 us -> 150 us (0.968)
  Pallas kernels: 0 us -> 80.6 us
  local copies, waits for them, and re-layouts: 69.4 us -> 9.43 us
  starting transfers between devices: 4.61 us -> 29.7 us
  blocking collectives: 21.8 us -> 0 us
  waiting for transfers between devices: 32.3 us -> 13.2 us
  between operations: 13.6 us -> 0.47 us
  other arithmetic: 4.15 us -> 12.8 us
  matrix products: 8.82 us -> 2.95 us
    pallas_call x0 -> x7, Pallas kernels: none -> 80.6 us  [the longest x4 66.9 us: pack(): pl.pallas_call(functools.partial(pack_kernel, plan, len(pieces)), out_sha...]
    gather x4 -> x0, local copies, waits for them, and re-layouts: 66.6 us -> none  [the longest x2 59.9 us: design_rows(): picked = jnp.take(contrast, perm_table, axis=1)]
    reduce_scatter x1 -> x0, waiting for transfers between devices: 32.3 us -> none  [per_device(): lax.psum_scatter(partial_value, 'subj', scatter_dimension=0, tiled=True)]
    ppermute x0 -> x23, starting transfers between devices: none -> 29.7 us  [the longest x12 13.9 us: per_device(): lax.ppermute(packs[m - 1], 'fix', [(i, i ^ m) for i, _ in pairs])]
    all_to_all x1 -> x0, blocking collectives: 13.6 us -> none  [per_device(): lax.all_to_all(request.reshape(fix_count, capacity), 'fix', split_axis=0,...]
    ppermute x0 -> x23, waiting for transfers between devices: none -> 13.2 us  [the longest x1 13.1 us: per_device(): share = lax.ppermute(share, 'subj', pairs)]
    psum x1 -> x0, blocking collectives: 8.19 us -> none  [per_device(): fitted = lax.psum(fitted_part, 'subj')]
    sub x0 -> x11, other arithmetic: none -> 7.39 us  [per_device(): tile.append(lookup(0, origin * group + (member ^ m), positions + 1) - 1)]
  transfers between devices with their start and end apart: 2 -> 23, of which waited for: 1 -> 1; matrix products, arithmetic and copies ran while one was open for 39% -> 13% of each run, Pallas kernels for 0% -> 51%
where the time goes in v1:
time: 150 us; the launch traced here: 149 us
  Pallas kernels  80.6 us (54%)
  starting transfers between devices  29.7 us (20%)
  waiting for transfers between devices  13.2 us (9%)
  other arithmetic  12.8 us (9%)
  local copies, waits for them, and re-layouts  9.43 us (6%)
  matrix products  2.95 us (2%)
    pallas_call x4, Pallas kernels, pack(): pl.pallas_call(functools.partial(pack_kernel, plan, len(pieces)), out_sha...  66.9 us
    ppermute x12, starting transfers between devices, per_device(): lax.ppermute(packs[m - 1], 'fix', [(i, i ^ m) for i, _ in pairs])  13.9 us
    ppermute x1, waiting for transfers between devices, per_device(): share = lax.ppermute(share, 'subj', pairs)  13.1 us
    pallas_call x2, Pallas kernels, smooth(): pl.pallas_call(functools.partial(smooth_kernel, plan, tile_total // block...  13 us
    sub x11, other arithmetic, per_device(): tile.append(lookup(0, origin * group + (member ^ m), positions + 1) - 1)  7.39 us
    ppermute x3, starting transfers between devices, per_device(): lax.ppermute(up[hop - 1], 'fix', [(i, i + group) for i in range(fix_count...  6.65 us
    unnamed x23, local copies, waits for them, and re-layouts  3.92 us
    ppermute x3, starting transfers between devices, per_device(): lax.ppermute(down[hop - 1], 'fix', [(i, i - group) for i in range(group,...  3.85 us
  transfers between devices with their start and end apart: 23, of which 1 were waited for; matrix products, arithmetic and copies ran while one was open for 13% of the time, Pallas kernels for 51%

profile of v1, /device:TPU:0, one launch (start us, length us, event | category | flops | bytes accessed | tf_op | source)
XLA Modules:
  0.0 149.1 jit_solution(4571609807900376794)
XLA Ops:
  0.5 2.5 %collective-permute-start.2 = (s32[8,4]{0,1:T(4,128)}, s32[8,4]{0,1:T(4,128)S(1)}, u32[]{:S(2)}, u32[]{:S(2)}) collective-permute-start(s32[8,4]{0,1:T(4,128)} %param.9), channel_id=1, source_target_pairs={{0,4},{2,6},{4,0},{6,2},{8,12},{10,14},{12,8},{14,10},{16,20},{18,... | collective-permute-start | bytes 392 | tf_op jit(solution)/shard_map/ppermute | solution.py:220
  3.1 4.5 %collective-permute-start.4 = (f32[8,128,128]{2,1,0:T(8,128)}, f32[8,128,128]{2,1,0:T(8,128)}, u32[]{:S(2)}, u32[]{:S(2)}) collective-permute-start(f32[8,128,128]{2,1,0:T(8,128)} %bitcast.114), channel_id=1, source_target_pairs={{0,8},{2,10},{4,12},{6,14},{8,16},{10,18},{12,20},{14,22},{16,24},... | collective-permute-start | bytes 1572872 | tf_op jit(solution)/shard_map/ppermute | solution.py:208
  7.6 1.3 collective-permute-start.7
  10.7 0.8 fusion.41
  11.5 0.8 fusion.5
  12.3 0.9 fusion.13
  14.4 13.7 %shard_map.75 = (f32[2,128,128]{2,1,0:T(8,128)}, f32[2,128,128]{2,1,0:T(8,128)}, f32[2,128,128]{2,1,0:T(8,128)}) custom-call(s32[6]{0:T(128)} %reshape_stack.10.local_ref, s32[1]{0:T(128)} %bitcast.43.line_ref, f32[8,128,128]{2,1,0:T(8,128)} %bitcast.116), custom_call_target="tpu_custom_call" | custom-call | bytes 786432 | tf_op jit(solution)/shard_map/pallas_call | solution.py:58
  28.3 1.6 %collective-permute-start.14 = (f32[2,128,128]{2,1,0:T(8,128)}, f32[2,128,128]{2,1,0:T(8,128)}, u32[]{:S(2)}, u32[]{:S(2)}) collective-permute-start(f32[2,128,128]{2,1,0:T(8,128)} %get-tuple-element.21), channel_id=1, source_target_pairs={{0,4},{2,6},{4,0},{6,2},{8,12},{10,14},{12,8},{14,10},{16,20},{18,... | collective-permute-start | bytes 393224 | tf_op jit(solution)/shard_map/ppermute | solution.py:265
  35.2 1.3 collective-permute-start.8
  38.2 25.7 %shard_map.76 = (f32[4,128,128]{2,1,0:T(8,128)}, f32[4,128,128]{2,1,0:T(8,128)}, f32[4,128,128]{2,1,0:T(8,128)}) custom-call(s32[12]{0:T(128)} %reshape.348.local_ref, s32[1]{0:T(128)} %bitcast.58.line_ref, f32[8,128,128]{2,1,0:T(8,128)} %collective-permute-done.4.refs_0_.refs_4_, f32[8,128,128]{2,1,0:T(8,128)} %collective-permute-done.7.refs_1_.refs_5_), custom_call_target="tpu_custom_call" | custom-call | bytes 1572864 | tf_op jit(solution)/shard_map/pallas_call | solution.py:58
  64.2 1.5 collective-permute-start.6
  65.7 1.3 collective-permute-start.9
  68.7 1.2 broadcast_add_fusion.15
  69.9 13.7 %shard_map.77 = (f32[2,128,128]{2,1,0:T(8,128)}, f32[2,128,128]{2,1,0:T(8,128)}, f32[2,128,128]{2,1,0:T(8,128)}) custom-call(s32[6]{0:T(128)} %reshape_stack.11.local_ref, s32[1]{0:T(128)} %bitcast.65.line_ref, f32[8,128,128]{2,1,0:T(8,128)} %copy-done.1, f32[8,128,128]{2,1,0:T(8,128)} %copy-done.3), custom_call_target="tpu_custom_call" | custom-call | bytes 786432 | tf_op jit(solution)/shard_map/pallas_call | solution.py:58
  83.7 1.6 %collective-permute-start.17 = (f32[4,128,128]{2,1,0:T(8,128)}, f32[4,128,128]{2,1,0:T(8,128)}, u32[]{:S(2)}, u32[]{:S(2)}) collective-permute-start(f32[4,128,128]{2,1,0:T(8,128)} %get-tuple-element.24), channel_id=1, source_target_pairs={{0,4},{2,6},{4,0},{6,2},{8,12},{10,14},{12,8},{14,10},{16,20},{18,... | collective-permute-start | bytes 786440 | tf_op jit(solution)/shard_map/ppermute | solution.py:265
  85.9 1.1 broadcast_add_fusion.16
  87.1 1.5 %collective-permute-start.20 = (f32[2,128,128]{2,1,0:T(8,128)}, f32[2,128,128]{2,1,0:T(8,128)S(1)}, u32[]{:S(2)}, u32[]{:S(2)}) collective-permute-start(f32[2,128,128]{2,1,0:T(8,128)} %get-tuple-element.27), channel_id=1, source_target_pairs={{0,4},{2,6},{4,0},{6,2},{8,12},{10,14},{12,8},{14,10},{16,20},{18,... | collective-permute-start | bytes 393224 | tf_op jit(solution)/shard_map/ppermute | solution.py:265
  89.8 0.8 concatenate.50.tile_ref
  91.3 0.8 concatenate.52.tile_ref
  92.1 13.8 %shard_map.74 = (f32[2,128,128]{2,1,0:T(8,128)}, f32[2,128,128]{2,1,0:T(8,128)}, f32[2,128,128]{2,1,0:T(8,128)}) custom-call(s32[6]{0:T(128)} %reshape_stack.9.local_ref, s32[1]{0:T(128)} %bitcast.19.line_ref, f32[8,128,128]{2,1,0:T(8,128)} %collective-permute-done.6.refs_0_, f32[8,128,128]{2,1,0:T(8,128)} %collective-permute-done.9.refs_1_), custom_call_target="tpu_custom_call" | custom-call | bytes 786432 | tf_op jit(solution)/shard_map/pallas_call | solution.py:58
  105.9 2.6 %collective-permute-start.10 = (f32[2,128,128]{2,1,0:T(8,128)}, f32[2,128,128]{2,1,0:T(8,128)S(1)}, u32[]{:S(2)}, u32[]{:S(2)}) collective-permute-start(f32[2,128,128]{2,1,0:T(8,128)} %get-tuple-element.17), channel_id=1, source_target_pairs={{0,2},{2,0},{4,6},{6,4},{24,26},{26,24},{28,30},{30,28},{1,3},{3,1... | collective-permute-start | bytes 393224 | tf_op jit(solution)/shard_map/ppermute | solution.py:265
  108.4 3.4 %collective-permute-start.11 = (f32[2,128,128]{2,1,0:T(8,128)}, f32[2,128,128]{2,1,0:T(8,128)S(1)}, u32[]{:S(2)}, u32[]{:S(2)}) collective-permute-start(f32[2,128,128]{2,1,0:T(8,128)} %get-tuple-element.18), channel_id=1, source_target_pairs={{0,4},{2,6},{4,0},{6,2},{24,28},{26,30},{28,24},{30,26},{1,5},{3,7... | collective-permute-start | bytes 393224 | tf_op jit(solution)/shard_map/ppermute | solution.py:265
  111.8 1.9 %collective-permute-start.12 = (f32[2,128,128]{2,1,0:T(8,128)}, f32[2,128,128]{2,1,0:T(8,128)S(1)}, u32[]{:S(2)}, u32[]{:S(2)}) collective-permute-start(f32[2,128,128]{2,1,0:T(8,128)} %get-tuple-element.19), channel_id=1, source_target_pairs={{0,6},{2,4},{4,2},{6,0},{24,30},{26,28},{28,26},{30,24},{1,7},{3,5... | collective-permute-start | bytes 393224 | tf_op jit(solution)/shard_map/ppermute | solution.py:265
  113.9 1.0 copy-done.2
  114.9 1.0 copy-done.4
  116.0 1.0 copy-done.5
  117.0 8.8 %shard_map.78.refs_6_ = f32[8,128,128]{2,1,0:T(8,128)S(1)} custom-call(s32[34]{0:T(128)S(1)} %concatenate.52.tile_ref, s32[34]{0:T(128)S(1)} %concatenate.53.local_ref, f32[8,128,128]{2,1,0:T(8,128)S(1)} %bitcast.117, f32[2,128,128]{2,1,0:T(8,128)S(1)} %collective-permute-done.13.refs_1_, f32[2,128,128]{2,1,0:T(8,128)} %collective-permute-done.14.refs_2_, ...), custom_call_target="tpu_custom_call" | custom-call | flops 536870912 | bytes 4194304 | tf_op jit(solution)/shard_map/pallas_call | solution.py:124
  125.9 4.1 %shard_map.79 = f32[8,128,128]{2,1,0:T(8,128)S(1)} custom-call(s32[10]{0:T(128)S(1)} %concatenate.50.tile_ref, s32[10]{0:T(128)S(1)} %pad_add_fusion.7.local_ref, f32[8,128,128]{2,1,0:T(8,128)} %collective-permute-done.6.refs_0_, f32[8,128,128]{2,1,0:T(8,128)} %collective-permute-done.9.refs_1_, f32[2,128,128]{2,1,0:T(8,128)S(1)} %collective-permute-done.10.refs_2_, ...), custom_call_target="tpu_custom_call" | custom-call | flops 167772160 | bytes 1310720 | tf_op jit(solution)/shard_map/pallas_call | solution.py:124
  130.1 1.6 %collective-permute-start.22 = (f32[1024,128]{1,0:T(8,128)S(1)}, f32[1024,128]{1,0:T(8,128)S(1)}, u32[]{:S(2)}, u32[]{:S(2)}) collective-permute-start(f32[1024,128]{1,0:T(8,128)S(1)} %bitcast.118), channel_id=1, source_target_pairs={{0,1},{1,0},{2,3},{3,2},{4,5},{5,4},{6,7},{7,6},{8,9},{9,8},{10,11... | collective-permute-start | bytes 1572872 | tf_op jit(solution)/shard_map/ppermute | solution.py:320
  132.3 13.1 %collective-permute-done = f32[72,128]{1,0:T(8,128)S(1)} collective-permute-done((f32[72,128]{1,0:T(8,128)S(1)}, f32[72,128]{1,0:T(8,128)S(1)}, u32[]{:S(2)}, u32[]{:S(2)}) %collective-permute-start) | collective-permute-done | bytes 36896 | tf_op jit(solution)/shard_map/ppermute | solution.py:319
  146.1 1.0 fusion
  147.1 2.0 %convolution_add_fusion = f32[256,1024]{1,0:T(8,128)} fusion(f32[256,1024]{1,0:T(8,128)S(1)} %fusion, f32[1024,128]{1,0:T(8,128)S(1)} %bitcast.119, f32[256,256]{1,0:T(8,128)S(1)} %shard_map.73), kind=kOutput, calls=%fused_computation | convolution fusion | flops 402915328 | bytes 2752512 | tf_op jit(solution)/shard_map/dot_general | solution.py:186
  (103 shorter events, 16.7 us)
Async XLA Ops:
  0.0 9.8 %collective-permute-start.1 = (s32[8,4]{0,1:T(4,128)}, s32[8,4]{0,1:T(4,128)S(1)}, u32[]{:S(2)}, u32[]{:S(2)}) collective-permute-start(s32[8,4]{0,1:T(4,128)} %param.9), channel_id=1, source_target_pairs={{0,2},{2,0},{4,6},{6,4},{8,10},{10,8},{12,14},{14,12},{16,18},{18,... | collective-permute-start | bytes 392 | tf_op jit(solution)/shard_map/ppermute | solution.py:220
  0.5 9.5 %collective-permute-start.2 = (s32[8,4]{0,1:T(4,128)}, s32[8,4]{0,1:T(4,128)S(1)}, u32[]{:S(2)}, u32[]{:S(2)}) collective-permute-start(s32[8,4]{0,1:T(4,128)} %param.9), channel_id=1, source_target_pairs={{0,4},{2,6},{4,0},{6,2},{8,12},{10,14},{12,8},{14,10},{16,20},{18,... | collective-permute-start | bytes 392 | tf_op jit(solution)/shard_map/ppermute | solution.py:220
  2.9 7.2 %collective-permute-start.3 = (s32[8,4]{0,1:T(4,128)}, s32[8,4]{0,1:T(4,128)S(1)}, u32[]{:S(2)}, u32[]{:S(2)}) collective-permute-start(s32[8,4]{0,1:T(4,128)} %param.9), channel_id=1, source_target_pairs={{0,6},{2,4},{4,2},{6,0},{8,14},{10,12},{12,10},{14,8},{16,22},{18,... | collective-permute-start | bytes 392 | tf_op jit(solution)/shard_map/ppermute | solution.py:220
  3.1 31.4 %collective-permute-start.4 = (f32[8,128,128]{2,1,0:T(8,128)}, f32[8,128,128]{2,1,0:T(8,128)}, u32[]{:S(2)}, u32[]{:S(2)}) collective-permute-start(f32[8,128,128]{2,1,0:T(8,128)} %bitcast.114), channel_id=1, source_target_pairs={{0,8},{2,10},{4,12},{6,14},{8,16},{10,18},{12,20},{14,22},{16,24},... | collective-permute-start | bytes 1572872 | tf_op jit(solution)/shard_map/ppermute | solution.py:208
  7.6 27.6 %collective-permute-start.7 = (f32[8,128,128]{2,1,0:T(8,128)}, f32[8,128,128]{2,1,0:T(8,128)}, u32[]{:S(2)}, u32[]{:S(2)}) collective-permute-start(f32[8,128,128]{2,1,0:T(8,128)} %bitcast.115), channel_id=1, source_target_pairs={{8,0},{10,2},{12,4},{14,6},{16,8},{18,10},{20,12},{22,14},{24,16},... | collective-permute-start | bytes 1572872 | tf_op jit(solution)/shard_map/ppermute | solution.py:213
  9.7 104.2 %copy-start = (f32[8,4,128,128]{3,2,1,0:T(8,128)S(1)}, f32[8,4,128,128]{3,2,1,0:T(8,128)}, u32[]{:S(2)}) copy-start(f32[8,4,128,128]{3,2,1,0:T(8,128)} %param.8) | copy-start | bytes 6291460
  28.2 40.1 %collective-permute-start.13 = (f32[2,128,128]{2,1,0:T(8,128)}, f32[2,128,128]{2,1,0:T(8,128)S(1)}, u32[]{:S(2)}, u32[]{:S(2)}) collective-permute-start(f32[2,128,128]{2,1,0:T(8,128)} %get-tuple-element.20), channel_id=1, source_target_pairs={{0,2},{2,0},{4,6},{6,4},{8,10},{10,8},{12,14},{14,12},{16,18},{18,... | collective-permute-start | bytes 393224 | tf_op jit(solution)/shard_map/ppermute | solution.py:265
  28.3 55.4 %collective-permute-start.14 = (f32[2,128,128]{2,1,0:T(8,128)}, f32[2,128,128]{2,1,0:T(8,128)}, u32[]{:S(2)}, u32[]{:S(2)}) collective-permute-start(f32[2,128,128]{2,1,0:T(8,128)} %get-tuple-element.21), channel_id=1, source_target_pairs={{0,4},{2,6},{4,0},{6,2},{8,12},{10,14},{12,8},{14,10},{16,20},{18,... | collective-permute-start | bytes 393224 | tf_op jit(solution)/shard_map/ppermute | solution.py:265
  34.5 29.7 %collective-permute-start.5 = (f32[8,128,128]{2,1,0:T(8,128)}, f32[8,128,128]{2,1,0:T(8,128)S(1)}, u32[]{:S(2)}, u32[]{:S(2)}) collective-permute-start(f32[8,128,128]{2,1,0:T(8,128)} %collective-permute-done.4.refs_0_.refs_4_), channel_id=1, source_target_pairs={{8,16},{10,18},{12,20},{14,22},{16,24},{18,26},{20,28},{22,30},{9,... | collective-permute-start | bytes 1572872 | tf_op jit(solution)/shard_map/ppermute | solution.py:208
  35.2 30.5 %collective-permute-start.8 = (f32[8,128,128]{2,1,0:T(8,128)}, f32[8,128,128]{2,1,0:T(8,128)S(1)}, u32[]{:S(2)}, u32[]{:S(2)}) collective-permute-start(f32[8,128,128]{2,1,0:T(8,128)} %collective-permute-done.7.refs_1_.refs_5_), channel_id=1, source_target_pairs={{8,0},{10,2},{12,4},{14,6},{16,8},{18,10},{20,12},{22,14},{9,1},{1... | collective-permute-start | bytes 1572872 | tf_op jit(solution)/shard_map/ppermute | solution.py:213
  64.0 21.4 %collective-permute-start.16 = (f32[4,128,128]{2,1,0:T(8,128)}, f32[4,128,128]{2,1,0:T(8,128)S(1)}, u32[]{:S(2)}, u32[]{:S(2)}) collective-permute-start(f32[4,128,128]{2,1,0:T(8,128)} %get-tuple-element.23), channel_id=1, source_target_pairs={{0,2},{2,0},{4,6},{6,4},{8,10},{10,8},{12,14},{14,12},{16,18},{18,... | collective-permute-start | bytes 786440 | tf_op jit(solution)/shard_map/ppermute | solution.py:265
  64.2 5.7 %copy-start.1 = (f32[8,128,128]{2,1,0:T(8,128)}, f32[8,128,128]{2,1,0:T(8,128)S(1)}, u32[]{:S(2)}) copy-start(f32[8,128,128]{2,1,0:T(8,128)S(1)} %collective-permute-done.5.refs_0_.refs_9_) | copy-start | bytes 1572868
  64.2 22.9 %collective-permute-start.6 = (f32[8,128,128]{2,1,0:T(8,128)S(1)}, f32[8,128,128]{2,1,0:T(8,128)}, u32[]{:S(2)}, u32[]{:S(2)}) collective-permute-start(f32[8,128,128]{2,1,0:T(8,128)S(1)} %collective-permute-done.5.refs_0_.refs_9_), channel_id=1, source_target_pairs={{16,24},{18,26},{20,28},{22,30},{17,25},{19,27},{21,29},{23,31}} | collective-permute-start | bytes 1572872 | tf_op jit(solution)/shard_map/ppermute | solution.py:208
  65.7 4.3 %copy-start.3 = (f32[8,128,128]{2,1,0:T(8,128)}, f32[8,128,128]{2,1,0:T(8,128)S(1)}, u32[]{:S(2)}) copy-start(f32[8,128,128]{2,1,0:T(8,128)S(1)} %collective-permute-done.8.refs_1_.refs_10_) | copy-start | bytes 1572868
  65.7 22.9 %collective-permute-start.9 = (f32[8,128,128]{2,1,0:T(8,128)S(1)}, f32[8,128,128]{2,1,0:T(8,128)}, u32[]{:S(2)}, u32[]{:S(2)}) collective-permute-start(f32[8,128,128]{2,1,0:T(8,128)S(1)} %collective-permute-done.8.refs_1_.refs_10_), channel_id=1, source_target_pairs={{8,0},{10,2},{12,4},{14,6},{9,1},{11,3},{13,5},{15,7}} | collective-permute-start | bytes 1572872 | tf_op jit(solution)/shard_map/ppermute | solution.py:213
  68.2 45.5 %copy-start.10 = (s32[2]{0:T(128)S(1)}, s32[2]{0:T(128)}, u32[]{:S(2)}) copy-start(s32[2]{0:T(128)} %get-tuple-element.64) | copy-start | bytes 28
  68.2 17.0 %collective-permute-start.15 = (f32[2,128,128]{2,1,0:T(8,128)}, f32[2,128,128]{2,1,0:T(8,128)}, u32[]{:S(2)}, u32[]{:S(2)}) collective-permute-start(f32[2,128,128]{2,1,0:T(8,128)} %get-tuple-element.22), channel_id=1, source_target_pairs={{0,6},{2,4},{4,2},{6,0},{8,14},{10,12},{12,10},{14,8},{16,22},{18,... | collective-permute-start | bytes 393224 | tf_op jit(solution)/shard_map/ppermute | solution.py:265
  83.7 22.1 %collective-permute-start.17 = (f32[4,128,128]{2,1,0:T(8,128)}, f32[4,128,128]{2,1,0:T(8,128)}, u32[]{:S(2)}, u32[]{:S(2)}) collective-permute-start(f32[4,128,128]{2,1,0:T(8,128)} %get-tuple-element.24), channel_id=1, source_target_pairs={{0,4},{2,6},{4,0},{6,2},{8,12},{10,14},{12,8},{14,10},{16,20},{18,... | collective-permute-start | bytes 786440 | tf_op jit(solution)/shard_map/ppermute | solution.py:265
  85.3 23.2 %collective-permute-start.18 = (f32[4,128,128]{2,1,0:T(8,128)}, f32[4,128,128]{2,1,0:T(8,128)}, u32[]{:S(2)}, u32[]{:S(2)}) collective-permute-start(f32[4,128,128]{2,1,0:T(8,128)} %get-tuple-element.25), channel_id=1, source_target_pairs={{0,6},{2,4},{4,2},{6,0},{8,14},{10,12},{12,10},{14,8},{16,22},{18,... | collective-permute-start | bytes 786440 | tf_op jit(solution)/shard_map/ppermute | solution.py:265
  85.3 26.5 %collective-permute-start.19 = (f32[2,128,128]{2,1,0:T(8,128)}, f32[2,128,128]{2,1,0:T(8,128)}, u32[]{:S(2)}, u32[]{:S(2)}) collective-permute-start(f32[2,128,128]{2,1,0:T(8,128)} %get-tuple-element.26), channel_id=1, source_target_pairs={{0,2},{2,0},{4,6},{6,4},{8,10},{10,8},{12,14},{14,12},{16,18},{18,... | collective-permute-start | bytes 393224 | tf_op jit(solution)/shard_map/ppermute | solution.py:265
  87.1 26.8 %collective-permute-start.20 = (f32[2,128,128]{2,1,0:T(8,128)}, f32[2,128,128]{2,1,0:T(8,128)S(1)}, u32[]{:S(2)}, u32[]{:S(2)}) collective-permute-start(f32[2,128,128]{2,1,0:T(8,128)} %get-tuple-element.27), channel_id=1, source_target_pairs={{0,4},{2,6},{4,0},{6,2},{8,12},{10,14},{12,8},{14,10},{16,20},{18,... | collective-permute-start | bytes 393224 | tf_op jit(solution)/shard_map/ppermute | solution.py:265
  88.6 25.3 %collective-permute-start.21 = (f32[2,128,128]{2,1,0:T(8,128)}, f32[2,128,128]{2,1,0:T(8,128)S(1)}, u32[]{:S(2)}, u32[]{:S(2)}) collective-permute-start(f32[2,128,128]{2,1,0:T(8,128)} %get-tuple-element.28), channel_id=1, source_target_pairs={{0,6},{2,4},{4,2},{6,0},{8,14},{10,12},{12,10},{14,8},{16,22},{18,... | collective-permute-start | bytes 393224 | tf_op jit(solution)/shard_map/ppermute | solution.py:265
  105.9 20.1 %collective-permute-start.10 = (f32[2,128,128]{2,1,0:T(8,128)}, f32[2,128,128]{2,1,0:T(8,128)S(1)}, u32[]{:S(2)}, u32[]{:S(2)}) collective-permute-start(f32[2,128,128]{2,1,0:T(8,128)} %get-tuple-element.17), channel_id=1, source_target_pairs={{0,2},{2,0},{4,6},{6,4},{24,26},{26,24},{28,30},{30,28},{1,3},{3,1... | collective-permute-start | bytes 393224 | tf_op jit(solution)/shard_map/ppermute | solution.py:265
  108.4 17.5 %collective-permute-start.11 = (f32[2,128,128]{2,1,0:T(8,128)}, f32[2,128,128]{2,1,0:T(8,128)S(1)}, u32[]{:S(2)}, u32[]{:S(2)}) collective-permute-start(f32[2,128,128]{2,1,0:T(8,128)} %get-tuple-element.18), channel_id=1, source_target_pairs={{0,4},{2,6},{4,0},{6,2},{24,28},{26,30},{28,24},{30,26},{1,5},{3,7... | collective-permute-start | bytes 393224 | tf_op jit(solution)/shard_map/ppermute | solution.py:265
  111.8 14.1 %collective-permute-start.12 = (f32[2,128,128]{2,1,0:T(8,128)}, f32[2,128,128]{2,1,0:T(8,128)S(1)}, u32[]{:S(2)}, u32[]{:S(2)}) collective-permute-start(f32[2,128,128]{2,1,0:T(8,128)} %get-tuple-element.19), channel_id=1, source_target_pairs={{0,6},{2,4},{4,2},{6,0},{24,30},{26,28},{28,26},{30,24},{1,7},{3,5... | collective-permute-start | bytes 393224 | tf_op jit(solution)/shard_map/ppermute | solution.py:265
  113.9 1.0 copy-start.2
  125.9 5.8 %copy-start.7 = (s32[128,128]{1,0:T(8,128)S(1)}, s32[128,128]{1,0:T(8,128)}, u32[]{:S(2)}) copy-start(s32[128,128]{1,0:T(8,128)} %param.13) | copy-start | bytes 196612
  125.9 5.8 %copy-start.8 = (f32[4,128]{1,0:T(4,128)S(1)}, f32[4,128]{1,0:T(4,128)}, u32[]{:S(2)}) copy-start(f32[4,128]{1,0:T(4,128)} %param.11) | copy-start | bytes 6148
  125.9 5.8 %copy-start.9 = (f32[4,128]{1,0:T(4,128)S(1)}, f32[4,128]{1,0:T(4,128)}, u32[]{:S(2)}) copy-start(f32[4,128]{1,0:T(4,128)} %param.10) | copy-start | bytes 6148
  125.9 19.6 %copy-start.6 = (f32[4,256]{1,0:T(4,128)S(1)}, f32[4,256]{1,0:T(4,128)}, u32[]{:S(2)}) copy-start(f32[4,256]{1,0:T(4,128)} %contrast_ref.1) | copy-start | bytes 12292
  130.1 16.0 %collective-permute-start.22 = (f32[1024,128]{1,0:T(8,128)S(1)}, f32[1024,128]{1,0:T(8,128)S(1)}, u32[]{:S(2)}, u32[]{:S(2)}) collective-permute-start(f32[1024,128]{1,0:T(8,128)S(1)} %bitcast.118), channel_id=1, source_target_pairs={{0,1},{1,0},{2,3},{3,2},{4,5},{5,4},{6,7},{7,6},{8,9},{9,8},{10,11... | collective-permute-start | bytes 1572872 | tf_op jit(solution)/shard_map/ppermute | solution.py:320
  131.7 13.7 %collective-permute-start = (f32[72,128]{1,0:T(8,128)S(1)}, f32[72,128]{1,0:T(8,128)S(1)}, u32[]{:S(2)}, u32[]{:S(2)}) collective-permute-start(f32[72,128]{1,0:T(8,128)S(1)} %pad_maximum_fusion.1), channel_id=1, source_target_pairs={{0,1},{1,0},{2,3},{3,2},{4,5},{5,4},{6,7},{7,6},{8,9},{9,8},{10,11... | collective-permute-start | bytes 110600 | tf_op jit(solution)/shard_map/ppermute | solution.py:319
  (2 other events, 2.1 us)

commit v2 on v0

v2 whole, which is shorter than its diff:
```python
import functools

import jax
import jax.numpy as jnp
from jax import lax
from jax.experimental import pallas as pl
from jax.experimental.pallas import tpu as pltpu
from jax.sharding import PartitionSpec as P

GROUP = 8
CHUNKS = 2
LANES = 128
ANY = pl.BlockSpec(memory_space=pl.ANY)
SMEM = pl.BlockSpec(memory_space=pltpu.SMEM)
VMEM = pl.BlockSpec(memory_space=pltpu.VMEM)
PARAMS = pltpu.CompilerParams(vmem_limit_bytes=32 * 1024 * 1024)


def cost(flops, bytes_accessed):
    return pl.CostEstimate(flops=flops, bytes_accessed=bytes_accessed, transcendentals=0)


def split(value):
    high = value.astype(jnp.bfloat16)
    return high, (value - high.astype(jnp.float32)).astype(jnp.bfloat16)


def turn_kernel(fixels_ref, *outs):
    block_count, sub, size = outs[0].shape
    for b in range(block_count):
        turned = fixels_ref[b * size : (b + 1) * size, :].T
        for c, out in enumerate(outs):
            out[b] = turned[c * sub : (c + 1) * sub, :]


def turn(fixels, block_count, sub):
    rows, width = fixels.shape
    shape = jax.ShapeDtypeStruct((block_count, sub, rows // block_count), jnp.float32)
    return pl.pallas_call(
        turn_kernel,
        out_shape=[shape] * (width // sub),
        in_specs=[VMEM],
        out_specs=[VMEM] * (width // sub),
        compiler_params=PARAMS,
        cost_estimate=cost(0, 8 * rows * width),
    )(fixels)


def tiles_kernel(conn_ref, out_ref):
    size = conn_ref.shape[1]

    @pl.loop(0, conn_ref.shape[0])
    def _(t):
        high, low = split(conn_ref[t])
        out_ref[t, :size, :] = high
        out_ref[t, size:, :] = low


def split_tiles(conn):
    total, size, _ = conn.shape
    return pl.pallas_call(
        tiles_kernel,
        out_shape=jax.ShapeDtypeStruct((total, 2 * size, size), jnp.bfloat16),
        in_specs=[VMEM],
        out_specs=VMEM,
        compiler_params=PARAMS,
        cost_estimate=cost(4 * total * size * size, 8 * total * size * size),
    )(conn)


def code_of(table_ref, place_ref, sizes, who, piece, other, rank):
    group, lines, cap = sizes
    line = lax.rem(lax.div(place_ref[0], group) + lines - piece, lines)
    member = jnp.bitwise_xor(lax.rem(place_ref[0], group), other)
    return table_ref[((who * lines + line) * group + member) * cap + rank]


def pack_kernel(piece_of, sizes, table_ref, place_ref, *refs):
    group, _, cap = sizes
    pieces = refs[: len(piece_of)]
    outs = refs[len(piece_of) : -1]
    sems = refs[-1]
    block_count = pieces[0].shape[0]
    todo = []
    for m in range(1, group):
        for item, piece in enumerate(piece_of):
            for rank in range(cap):
                code = code_of(table_ref, place_ref, sizes, m, piece, 0, rank)
                place = item * cap + rank
                copy = pltpu.make_async_copy(
                    pieces[item].at[lax.rem(jnp.maximum(code, 0), block_count)],
                    outs[m - 1].at[place],
                    sems.at[m - 1, place],
                )
                copy.start()
                todo.append(copy)
    for copy in todo:
        copy.wait()


def pack(items, table, place, sizes):
    group, _, cap = sizes
    piece_of, pieces = zip(*items)
    shape = pieces[0].shape[1:]
    count = cap * len(items)
    size = count * (group - 1) * shape[0] * shape[1] * 4
    return pl.pallas_call(
        functools.partial(pack_kernel, piece_of, sizes),
        out_shape=[jax.ShapeDtypeStruct((count,) + shape, jnp.float32)] * (group - 1),
        in_specs=[SMEM, SMEM] + [ANY] * len(items),
        out_specs=[VMEM] * (group - 1),
        scratch_shapes=[pltpu.SemaphoreType.DMA((group - 1, count))],
        compiler_params=PARAMS,
        cost_estimate=cost(0, 2 * size),
    )(table, place, *pieces)


def smooth_kernel(plan, sizes, per_row, source_count, table_ref, place_ref, *refs):
    sources = refs[:source_count]
    tiles_ref, out_ref, blocks, sems = refs[source_count:]
    tile_total, sub, size = blocks.shape
    block_count = tile_total // per_row
    for piece, m, source, base in plan:
        for rank in range(sizes[2]):
            code = code_of(table_ref, place_ref, sizes, 0, piece, m, rank)

            @pl.when(code >= 0)
            def _():
                tile, local = lax.div(code, block_count), lax.rem(code, block_count)
                pltpu.make_async_copy(
                    sources[source].at[local if m == 0 else base + rank],
                    blocks.at[tile],
                    sems.at[tile],
                ).start()

    for row in range(block_count):
        highs, lows = [], []
        for tile in range(row * per_row, (row + 1) * per_row):
            pltpu.make_async_copy(blocks.at[tile], blocks.at[tile], sems.at[tile]).wait()
            high, low = split(blocks[tile])
            highs.append(high)
            lows.append(low)
        left = jnp.concatenate(
            [jnp.concatenate(highs, axis=1), jnp.concatenate(lows, axis=1)], axis=0
        )
        right = jnp.concatenate(
            [tiles_ref[tile] for tile in range(row * per_row, (row + 1) * per_row)], axis=1
        )
        terms = lax.dot_general(
            left, right, (((1,), (1,)), ((), ())), preferred_element_type=jnp.float32
        )
        value = (terms[:sub, :size] + terms[sub:, :size]) + (
            terms[:sub, size:] + terms[sub:, size:]
        )
        out_ref[:, row * size : (row + 1) * size] = value


def smooth(plan, sizes, table, place, sources, tiles, block_count):
    tile_total, _, size = tiles.shape
    sub = sources[0].shape[1]
    return pl.pallas_call(
        functools.partial(
            smooth_kernel, plan, sizes, tile_total // block_count, len(sources)
        ),
        out_shape=jax.ShapeDtypeStruct((sub, block_count * size), jnp.float32),
        in_specs=[SMEM, SMEM] + [ANY] * len(sources) + [VMEM],
        out_specs=VMEM,
        scratch_shapes=[
            pltpu.VMEM((tile_total, sub, size), jnp.float32),
            pltpu.SemaphoreType.DMA((tile_total,)),
        ],
        compiler_params=PARAMS,
        cost_estimate=cost(
            8 * tile_total * size * size * sub, 4 * tile_total * size * (sub + size)
        ),
    )(table, place, *sources, tiles)


def design_kernel(sub, perm_ref, contrast_ref, nuisance_ref, pinv_ref, out_ref, rows_ref):
    perms, subjects = perm_ref.shape
    regressors = contrast_ref.shape[0]
    for start in range(0, subjects, LANES):
        want = perm_ref[:, start : start + LANES].astype(jnp.int32)
        lane, part = want % LANES, want // LANES
        for r in range(regressors):
            value = jnp.zeros((perms, LANES), jnp.float32)
            for base in range(0, subjects, LANES):
                table = jnp.broadcast_to(
                    contrast_ref[r : r + 1, base : base + LANES], (perms, LANES)
                )
                found = jnp.take_along_axis(table, lane, axis=1, mode="promise_in_bounds")
                value = jnp.where(part == base // LANES, found, value)
            rows_ref[start // LANES, pl.ds(r, perms, stride=regressors), :] = value
    design = jnp.concatenate([rows_ref[i] for i in range(rows_ref.shape[0])], axis=1)
    result = design
    for n in range(nuisance_ref.shape[0]):
        weight = jnp.sum(design * nuisance_ref[n : n + 1, :], axis=1, keepdims=True)
        result = result - weight * pinv_ref[n : n + 1, :]
    high, low = split(result)
    for q in range(subjects // sub):
        columns = slice(q * sub, (q + 1) * sub)
        out_ref[q] = jnp.concatenate(
            [high[:, columns], high[:, columns], low[:, columns], low[:, columns]], axis=1
        )


def reduced_design(perm, contrast, nuisance, pinv, sub):
    rows = perm.shape[0] * contrast.shape[0]
    subjects = perm.shape[1]
    return pl.pallas_call(
        functools.partial(design_kernel, sub),
        out_shape=jax.ShapeDtypeStruct((subjects // sub, rows, 4 * sub), jnp.bfloat16),
        in_specs=[VMEM] * 4,
        out_specs=VMEM,
        scratch_shapes=[pltpu.VMEM((subjects // LANES, rows, LANES), jnp.float32)],
        compiler_params=PARAMS,
        cost_estimate=cost(32 * rows * subjects, 8 * rows * subjects),
    )(perm, contrast, nuisance, pinv)


def project_kernel(chunks, first, design_ref, *refs):
    parts = refs[: len(chunks)]
    before = None if first else refs[len(chunks)]
    out_ref = refs[-1]
    total = None if first else before[...]
    for q, part in zip(chunks, parts):
        high, low = split(part[...])
        term = jnp.dot(
            design_ref[q],
            jnp.concatenate([high, low, high, low], axis=0),
            preferred_element_type=jnp.float32,
        )
        total = term if total is None else total + term
    out_ref[...] = total


def project(design, chunks, parts, before):
    _, rows, _ = design.shape
    sub, fixels = parts[0].shape
    step = 256
    first = before is None
    wide = pl.BlockSpec((sub, step), lambda i: (0, i))
    tall = pl.BlockSpec((rows, step), lambda i: (0, i))
    return pl.pallas_call(
        functools.partial(project_kernel, tuple(chunks), first),
        grid=(fixels // step,),
        out_shape=jax.ShapeDtypeStruct((rows, fixels), jnp.float32),
        in_specs=[pl.BlockSpec(design.shape, lambda i: (0, 0, 0))]
        + [wide] * len(parts)
        + ([] if first else [tall]),
        out_specs=tall,
        compiler_params=PARAMS,
        cost_estimate=cost(
            8 * len(parts) * rows * sub * fixels, 4 * fixels * (rows + sub * len(parts))
        ),
    )(design, *parts, *(() if first else (before,)))


def per_device(fixels, conn_tiles, columns, nuisance, nuisance_pinv, contrast, perm_table):
    fix_count = lax.axis_size("fix")
    subj_count = lax.axis_size("subj")
    group = GROUP if fix_count % GROUP == 0 else 1
    lines = fix_count // group
    block_count, per_row = columns.shape
    size = conn_tiles.shape[2]
    width = fixels.shape[1]
    sub = width // CHUNKS
    tile_total = block_count * per_row
    cap = (tile_total + fix_count - 1) // fix_count
    sizes = (group, lines, cap)
    me = lax.axis_index("fix")
    part = lax.axis_index("subj")
    place = me.astype(jnp.int32).reshape(1)

    own = turn(fixels, block_count, sub)
    pieces = [
        [own[c]]
        + [
            lax.ppermute(
                own[c],
                "fix",
                [(i, (i + k * group) % fix_count) for i in range(fix_count)],
            )
            for k in range(1, lines)
        ]
        for c in range(CHUNKS)
    ]

    named = columns.reshape(1, tile_total)
    step = 1
    while step < group:
        pairs = [(i, i ^ step) for i in range(fix_count)]
        named = jnp.concatenate([named, lax.ppermute(named, "fix", pairs)])
        step *= 2
    owners = named // block_count
    positions = jnp.arange(tile_total)
    earlier = positions[:, None] > positions[None, :]
    same = owners[:, :, None] == owners[:, None, :]
    ranks = jnp.sum(jnp.logical_and(same, earlier[None]).astype(jnp.int32), axis=2)
    slots = (owners * cap + ranks)[:, None, :] == jnp.arange(fix_count * cap)[:, None]
    codes = (positions * block_count + named % block_count + 1)[:, None, :]
    table = (jnp.sum(jnp.where(slots, codes, 0), axis=2) - 1).astype(jnp.int32).reshape(-1)

    rows = perm_table.shape[0] // subj_count
    count = nuisance.shape[0]
    shares = []
    for shift in range(subj_count):
        to = (part + shift) % subj_count
        share = jnp.concatenate(
            [
                lax.dynamic_slice_in_dim(perm_table, to * rows, rows, 0).astype(jnp.float32),
                nuisance,
                nuisance_pinv,
            ]
        )
        if shift:
            pairs = [(i, (i + shift) % subj_count) for i in range(subj_count)]
            share = lax.ppermute(share, "subj", pairs)
        shares.append(share)
    shares = jnp.concatenate(shares, axis=1)
    design = reduced_design(
        shares[:rows], contrast, shares[rows : rows + count], shares[rows + count :], sub
    )

    tiles = split_tiles(conn_tiles.reshape(tile_total, size, size))
    smoothed = []
    for c in range(CHUNKS):
        packs = pack(list(enumerate(pieces[c])), table, place, sizes)
        got = [
            lax.ppermute(packs[m - 1], "fix", [(i, i ^ m) for i in range(fix_count)])
            for m in range(1, group)
        ]
        plan = []
        for k in range(lines):
            plan.append((k, 0, k, 0))
            plan.extend((k, m, lines + m - 1, k * cap) for m in range(1, group))
        smoothed.append(
            smooth(tuple(plan), sizes, table, place, pieces[c] + got, tiles, block_count)
        )

    total = project(design, range(CHUNKS), smoothed, None)
    for shift in range(1, subj_count):
        pairs = [(i, (i + shift) % subj_count) for i in range(subj_count)]
        halves = [lax.ppermute(value, "subj", pairs) for value in smoothed]
        chunks = range(shift * CHUNKS, (shift + 1) * CHUNKS)
        total = project(design, chunks, halves, total)
    return total


def solution(mesh):
    placed = (
        P("fix", "subj"),
        P("fix", None, None, None),
        P("fix", None),
        P(None, "subj"),
        P(None, "subj"),
        P(),
        P(None, "subj"),
    )
    return jax.shard_map(
        per_device, mesh=mesh, in_specs=placed, out_specs=P("subj", "fix"), check_vma=False
    )
```

time: 155 us -> 73.4 us (0.47)
  local copies, waits for them, and re-layouts: 69.4 us -> 3.57 us
  blocking collectives: 21.8 us -> 0 us
  Pallas kernels: 0 us -> 20.1 us
  starting transfers between devices: 4.61 us -> 23.6 us
  between operations: 13.6 us -> 0.19 us
  matrix products: 8.82 us -> 0 us
  waiting for transfers between devices: 32.3 us -> 24.3 us
  other arithmetic: 4.15 us -> 1.39 us
    gather x4 -> x0, local copies, waits for them, and re-layouts: 66.6 us -> none  [the longest x2 59.9 us: design_rows(): picked = jnp.take(contrast, perm_table, axis=1)]
    reduce_scatter x1 -> x0, waiting for transfers between devices: 32.3 us -> none  [per_device(): lax.psum_scatter(partial_value, 'subj', scatter_dimension=0, tiled=True)]
    ppermute x0 -> x22, waiting for transfers between devices: none -> 24.3 us  [the longest x3 8.12 us: per_device(): named = jnp.concatenate([named, lax.ppermute(named, 'fix', pairs)])]
    ppermute x0 -> x22, starting transfers between devices: none -> 23.6 us  [the longest x14 11.9 us: per_device(): lax.ppermute(packs[m - 1], 'fix', [(i, i ^ m) for i in range(fix_count)])]
    pallas_call x0 -> x9, Pallas kernels: none -> 20.1 us  [the longest x2 10.5 us: smooth(): pl.pallas_call(functools.partial(smooth_kernel, plan, sizes, tile_total /...]
    all_to_all x1 -> x0, blocking collectives: 13.6 us -> none  [per_device(): lax.all_to_all(request.reshape(fix_count, capacity), 'fix', split_axis=0,...]
    dot_general x4 -> x0, matrix products: 8.82 us -> none  [the longest x1 4.12 us: per_device(): jnp.einsum('bkij,bkjs->bis', conn_tiles, needed, precision=lax.Precision....]
    psum x1 -> x0, blocking collectives: 8.19 us -> none  [per_device(): fitted = lax.psum(fitted_part, 'subj')]
  transfers between devices with their start and end apart: 2 -> 22, of which waited for: 1 -> 9; matrix products, arithmetic and copies ran while one was open for 39% -> 2% of each run, Pallas kernels for 0% -> 24%
where the time goes in v2:
time: 73.4 us; the launch traced here: 73.1 us
  waiting for transfers between devices  24.3 us (33%)
  starting transfers between devices  23.6 us (32%)
  Pallas kernels  20.1 us (27%)
  local copies, waits for them, and re-layouts  3.57 us (5%)
  other arithmetic  1.39 us (2%)
    ppermute x14, starting transfers between devices, per_device(): lax.ppermute(packs[m - 1], 'fix', [(i, i ^ m) for i in range(fix_count)])  11.9 us
    pallas_call x2, Pallas kernels, smooth(): pl.pallas_call(functools.partial(smooth_kernel, plan, sizes, tile_total /...  10.5 us
    ppermute x3, waiting for transfers between devices, per_device(): named = jnp.concatenate([named, lax.ppermute(named, 'fix', pairs)])  8.12 us
    ppermute x2, waiting for transfers between devices, per_device(): lax.ppermute(own[c], 'fix', [(i, (i + k * group) % fix_count) for i in ra...  6.19 us
    ppermute x14, waiting for transfers between devices, per_device(): lax.ppermute(packs[m - 1], 'fix', [(i, i ^ m) for i in range(fix_count)])  5.28 us
    pallas_call x2, Pallas kernels, pack(): pl.pallas_call(functools.partial(pack_kernel, piece_of, sizes), out_shape...  5 us
    ppermute x2, waiting for transfers between devices, per_device(): halves = [lax.ppermute(value, 'subj', pairs) for value in smoothed]  4.71 us
    ppermute x3, starting transfers between devices, per_device(): named = jnp.concatenate([named, lax.ppermute(named, 'fix', pairs)])  4.17 us
  transfers between devices with their start and end apart: 22, of which 9 were waited for; matrix products, arithmetic and copies ran while one was open for 2% of the time, Pallas kernels for 24%

profile of v2, /device:TPU:0, one launch (start us, length us, event | category | flops | bytes accessed | tf_op | source)
XLA Modules:
  0.0 73.1 jit_solution(3388097049066682718)
XLA Ops:
  0.0 0.8 %copy.10 = s32[8,4]{1,0:T(8,128)S(1)} copy(s32[8,4]{0,1:T(4,128)} %param.9) | data formatting | bytes 256 | tf_op args[2]
  1.3 1.0 %copy-done.1 = f32[1024,128]{1,0:T(8,128)S(1)} copy-done((f32[1024,128]{1,0:T(8,128)S(1)}, f32[1024,128]{1,0:T(8,128)}, u32[]{:S(2)}) %copy-start.1) | copy-done | bytes 524312
  2.5 3.7 %collective-permute-start.13 = (f32[8,64,128]{2,1,0:T(8,128)S(1)}, f32[8,64,128]{2,1,0:T(8,128)S(1)}, u32[]{:S(2)}, u32[]{:S(2)}) collective-permute-start(f32[8,64,128]{2,1,0:T(8,128)S(1)} %get-tuple-element.29.refs_0_), channel_id=1, source_target_pairs={{0,16},{2,18},{4,20},{6,22},{8,24},{10,26},{12,28},{14,30},{16,0},... | collective-permute-start | bytes 786440 | tf_op jit(solution)/shard_map/ppermute | solution.py:279
  6.3 1.8 %collective-permute-start.2 = (s32[2,32]{1,0:T(2,128)S(1)}, s32[2,32]{1,0:T(2,128)S(1)}, u32[]{:S(2)}, u32[]{:S(2)}) collective-permute-start(s32[2,32]{1,0:T(2,128)S(1)} %pad_add_fusion.2), channel_id=1, source_target_pairs={{0,4},{2,6},{4,0},{6,2},{8,12},{10,14},{12,8},{14,10},{16,20},{18,... | collective-permute-start | bytes 776 | tf_op jit(solution)/shard_map/ppermute | solution.py:293
  8.1 1.8 %collective-permute-done.2 = s32[2,32]{1,0:T(2,128)S(1)} collective-permute-done((s32[2,32]{1,0:T(2,128)S(1)}, s32[2,32]{1,0:T(2,128)S(1)}, u32[]{:S(2)}, u32[]{:S(2)}) %collective-permute-start.2) | collective-permute-done | bytes 288 | tf_op jit(solution)/shard_map/ppermute | solution.py:293
  9.9 1.9 %collective-permute-start.3 = (s32[4,32]{1,0:T(4,128)S(1)}, s32[4,32]{1,0:T(4,128)S(1)}, u32[]{:S(2)}, u32[]{:S(2)}) collective-permute-start(s32[4,32]{1,0:T(4,128)S(1)} %pad_add_fusion.1), channel_id=1, source_target_pairs={{0,8},{2,10},{4,12},{6,14},{8,0},{10,2},{12,4},{14,6},{16,24},{18,... | collective-permute-start | bytes 1544 | tf_op jit(solution)/shard_map/ppermute | solution.py:293
  11.8 6.3 %collective-permute-done.3 = s32[4,32]{1,0:T(4,128)S(1)} collective-permute-done((s32[4,32]{1,0:T(4,128)S(1)}, s32[4,32]{1,0:T(4,128)S(1)}, u32[]{:S(2)}, u32[]{:S(2)}) %collective-permute-start.3) | collective-permute-done | bytes 544 | tf_op jit(solution)/shard_map/ppermute | solution.py:293
  18.8 5.8 %collective-permute-done.13.refs_1_ = f32[8,64,128]{2,1,0:T(8,128)S(1)} collective-permute-done((f32[8,64,128]{2,1,0:T(8,128)S(1)}, f32[8,64,128]{2,1,0:T(8,128)S(1)}, u32[]{:S(2)}, u32[]{:S(2)}) %collective-permute-start.13) | collective-permute-done | bytes 262176 | tf_op jit(solution)/shard_map/ppermute | solution.py:279
  24.6 2.5 %shard_map.78 = (f32[4,64,128]{2,1,0:T(8,128)S(1)}, f32[4,64,128]{2,1,0:T(8,128)S(1)}, f32[4,64,128]{2,1,0:T(8,128)S(1)}, f32[4,64,128]{2,1,0:T(8,128)S(1)}, f32...) custom-call(s32[256]{0:T(256)S(1)} %sub.13.table_ref, s32[1]{0:T(128)} %bitcast.place_ref, ...), custom_call_target="tpu_custom_call" | custom-call | bytes 1835008 | tf_op jit(solution)/shard_map/pallas_call | solution.py:107
  27.2 1.8 %collective-permute-start.15 = (f32[4,64,128]{2,1,0:T(8,128)S(1)}, f32[4,64,128]{2,1,0:T(8,128)S(1)}, u32[]{:S(2)}, u32[]{:S(2)}) collective-permute-start(f32[4,64,128]{2,1,0:T(8,128)S(1)} %get-tuple-element.31), channel_id=1, source_target_pairs={{0,4},{2,6},{4,0},{6,2},{8,12},{10,14},{12,8},{14,10},{16,20},{18,... | collective-permute-start | bytes 393224 | tf_op jit(solution)/shard_map/ppermute | solution.py:330
  29.1 0.6 collective-permute-start.17
  30.0 0.7 collective-permute-start.18
  30.7 2.5 %shard_map.75 = (f32[4,64,128]{2,1,0:T(8,128)S(1)}, f32[4,64,128]{2,1,0:T(8,128)S(1)}, f32[4,64,128]{2,1,0:T(8,128)S(1)}, f32[4,64,128]{2,1,0:T(8,128)S(1)}, f32...) custom-call(s32[256]{0:T(256)S(1)} %sub.13.table_ref, s32[1]{0:T(128)} %bitcast.place_ref, ...), custom_call_target="tpu_custom_call" | custom-call | bytes 1835008 | tf_op jit(solution)/shard_map/pallas_call | solution.py:107
  33.3 1.7 %collective-permute-start.19 = (f32[4,64,128]{2,1,0:T(8,128)S(1)}, f32[4,64,128]{2,1,0:T(8,128)S(1)}, u32[]{:S(2)}, u32[]{:S(2)}) collective-permute-start(f32[4,64,128]{2,1,0:T(8,128)S(1)} %get-tuple-element.35), channel_id=1, source_target_pairs={{0,12},{2,14},{4,8},{6,10},{8,4},{10,6},{12,0},{14,2},{16,28},{18,... | collective-permute-start | bytes 393224 | tf_op jit(solution)/shard_map/ppermute | solution.py:330
  34.9 1.1 %collective-permute-start.20 = (f32[4,64,128]{2,1,0:T(8,128)S(1)}, f32[4,64,128]{2,1,0:T(8,128)S(1)}, u32[]{:S(2)}, u32[]{:S(2)}) collective-permute-start(f32[4,64,128]{2,1,0:T(8,128)S(1)} %get-tuple-element.36), channel_id=1, source_target_pairs={{0,14},{2,12},{4,10},{6,8},{8,6},{10,4},{12,2},{14,0},{16,30},{18,... | collective-permute-start | bytes 393224 | tf_op jit(solution)/shard_map/ppermute | solution.py:330
  36.0 1.9 %collective-permute-start.10 = (f32[4,64,128]{2,1,0:T(8,128)S(1)}, f32[4,64,128]{2,1,0:T(8,128)S(1)}, u32[]{:S(2)}, u32[]{:S(2)}) collective-permute-start(f32[4,64,128]{2,1,0:T(8,128)S(1)} %get-tuple-element.27), channel_id=1, source_target_pairs={{0,12},{2,14},{4,8},{6,10},{8,4},{10,6},{12,0},{14,2},{16,28},{18,... | collective-permute-start | bytes 393224 | tf_op jit(solution)/shard_map/ppermute | solution.py:330
  38.0 0.6 collective-permute-start.11
  39.1 0.8 %dynamic-slice_convert_fusion.1 = (f32[64,128]{1,0:T(8,128)S(1)}, f32[64,128]{1,0:T(8,128)S(1)}) fusion(s32[128,128]{1,0:T(8,128)} %param.13, s32[]{:T(128)S(6)} %select_n.48, s32[]{:T(128)S(6)} %select_n.50), kind=kLoop, calls=%fused_computation.6 | loop fusion | flops 16384 | bytes 131080 | tf_op jit(solution)/shard_map/convert_element_type | solution.py:311
  39.9 1.6 %copy-done = f32[8,4,128,128]{3,2,1,0:T(8,128)S(1)} copy-done((f32[8,4,128,128]{3,2,1,0:T(8,128)S(1)}, f32[8,4,128,128]{3,2,1,0:T(8,128)}, u32[]{:S(2)}) %copy-start) | copy-done | bytes 2097176
  42.2 1.5 %collective-permute-start.6 = (f32[4,64,128]{2,1,0:T(8,128)S(1)}, f32[4,64,128]{2,1,0:T(8,128)S(1)}, u32[]{:S(2)}, u32[]{:S(2)}) collective-permute-start(f32[4,64,128]{2,1,0:T(8,128)S(1)} %get-tuple-element.23), channel_id=1, source_target_pairs={{0,4},{2,6},{4,0},{6,2},{8,12},{10,14},{12,8},{14,10},{16,20},{18,... | collective-permute-start | bytes 393224 | tf_op jit(solution)/shard_map/ppermute | solution.py:330
  43.8 0.7 collective-permute-start.7
  44.5 3.4 %collective-permute-done.10.refs_7_ = f32[4,64,128]{2,1,0:T(8,128)S(1)} collective-permute-done((f32[4,64,128]{2,1,0:T(8,128)S(1)}, f32[4,64,128]{2,1,0:T(8,128)S(1)}, u32[]{:S(2)}, u32[]{:S(2)}) %collective-permute-start.10) | collective-permute-done | bytes 131104 | tf_op jit(solution)/shard_map/ppermute | solution.py:330
  48.2 1.4 %collective-permute-done.11.refs_8_ = f32[4,64,128]{2,1,0:T(8,128)S(1)} collective-permute-done((f32[4,64,128]{2,1,0:T(8,128)S(1)}, f32[4,64,128]{2,1,0:T(8,128)S(1)}, u32[]{:S(2)}, u32[]{:S(2)}) %collective-permute-start.11) | collective-permute-done | bytes 131104 | tf_op jit(solution)/shard_map/ppermute | solution.py:330
  50.0 1.6 %collective-permute-start = (f32[72,128]{1,0:T(8,128)S(1)}, f32[72,128]{1,0:T(8,128)S(1)}, u32[]{:S(2)}, u32[]{:S(2)}) collective-permute-start(f32[72,128]{1,0:T(8,128)S(1)} %pad_maximum_fusion.1), channel_id=1, source_target_pairs={{0,1},{1,0},{2,3},{3,2},{4,5},{5,4},{6,7},{7,6},{8,9},{9,8},{10,11... | collective-permute-start | bytes 110600 | tf_op jit(solution)/shard_map/ppermute | solution.py:318
  51.6 5.2 %shard_map.79.refs_1_ = f32[64,1024]{1,0:T(8,128)S(1)} custom-call(s32[256]{0:T(256)S(1)} %sub.13.table_ref, s32[1]{0:T(128)} %bitcast.place_ref, f32[8,64,128]{2,1,0:T(8,128)S(1)} %get-tuple-element.29.refs_0_, f32[8,64,128]{2,1,0:T(8,128)S(1)} %collective-permute-done.13.refs_1_, f32[4,64,128]{2,1,0:T(8,128)S(1)} %collective-permute-done.14.refs_2_, ...), custom_call_target="tpu_custom_call" | custom-call | flops 268435456 | bytes 3145728 | tf_op jit(solution)/shard_map/pallas_call | solution.py:161
  56.8 0.6 collective-permute-start.21
  57.4 5.2 %shard_map.77.refs_0_ = f32[64,1024]{1,0:T(8,128)S(1)} custom-call(s32[256]{0:T(256)S(1)} %sub.13.table_ref, s32[1]{0:T(128)} %bitcast.place_ref, f32[8,64,128]{2,1,0:T(8,128)S(1)} %get-tuple-element.21.refs_0_, f32[8,64,128]{2,1,0:T(8,128)S(1)} %collective-permute-done.4.refs_1_, f32[4,64,128]{2,1,0:T(8,128)S(1)} %collective-permute-done.5.refs_2_, ...), custom_call_target="tpu_custom_call" | custom-call | flops 268435456 | bytes 3145728 | tf_op jit(solution)/shard_map/pallas_call | solution.py:161
  62.7 1.6 %collective-permute-start.12 = (f32[64,1024]{1,0:T(8,128)S(1)}, f32[64,1024]{1,0:T(8,128)S(1)}, u32[]{:S(2)}, u32[]{:S(2)}) collective-permute-start(f32[64,1024]{1,0:T(8,128)S(1)} %shard_map.77.refs_0_), channel_id=1, source_target_pairs={{0,1},{1,0},{2,3},{3,2},{4,5},{5,4},{6,7},{7,6},{8,9},{9,8},{10,11... | collective-permute-start | bytes 786440 | tf_op jit(solution)/shard_map/ppermute | solution.py:344
  64.3 0.8 %shard_map.73.design_ref = bf16[4,256,256]{2,1,0:T(8,128)(2,1)S(1)} custom-call(f32[64,256]{1,0:T(8,128)S(1)} %slice.12.perm_ref, f32[4,256]{1,0:T(4,128)S(1)} %copy-done.2, f32[4,256]{1,0:T(4,128)S(1)} %get-tuple-element.38.nuisance_ref, f32[4,256]{1,0:T(4,128)S(1)} %get-tuple-element.37.pinv_ref), custom_call_target="tpu_custom_call" | custom-call | flops 2097152 | bytes 524288 | tf_op jit(solution)/shard_map/pallas_call | solution.py:210
  65.1 1.1 %shard_map.80.refs_2_ = f32[256,1024]{1,0:T(8,128)S(1)} custom-call(bf16[4,256,256]{2,1,0:T(8,128)(2,1)S(1)} %shard_map.73.design_ref, f32[64,1024]{1,0:T(8,128)S(1)} %shard_map.77.refs_0_, f32[64,1024]{1,0:T(8,128)S(1)} %shard_map.79.refs_1_), custom_call_target="tpu_custom_call" | custom-call | flops 268435456 | bytes 1572864 | tf_op jit(solution)/shard_map/pallas_call | solution.py:244
  66.2 4.7 %collective-permute-done.12.refs_0_ = f32[64,1024]{1,0:T(8,128)S(1)} collective-permute-done((f32[64,1024]{1,0:T(8,128)S(1)}, f32[64,1024]{1,0:T(8,128)S(1)}, u32[]{:S(2)}, u32[]{:S(2)}) %collective-permute-start.12) | collective-permute-done | bytes 262176 | tf_op jit(solution)/shard_map/ppermute | solution.py:344
  70.9 2.2 %shard_map.81 = f32[256,1024]{1,0:T(8,128)} custom-call(bf16[4,256,256]{2,1,0:T(8,128)(2,1)S(1)} %shard_map.73.design_ref, f32[64,1024]{1,0:T(8,128)S(1)} %collective-permute-done.12.refs_0_, f32[64,1024]{1,0:T(8,128)S(1)} %collective-permute-done.21.refs_1_, f32[256,1024]{1,0:T(8,128)S(1)} %shard_map.80.refs_2_), custom_call_target="tpu_custom_call" | custom-call | flops 268435456 | bytes 1572864 | tf_op jit(solution)/shard_map/pallas_call | solution.py:244
  (48 shorter events, 4.1 us)
Async XLA Ops:
  0.8 5.4 %collective-permute-start.1 = (s32[1,32]{1,0:T(1,128)S(1)}, s32[1,32]{1,0:T(1,128)S(1)}, u32[]{:S(2)}, u32[]{:S(2)}) collective-permute-start(s32[1,32]{1,0:T(1,128)S(1)} %concatenate.70), channel_id=1, source_target_pairs={{0,2},{2,0},{4,6},{6,4},{8,10},{10,8},{12,14},{14,12},{16,18},{18,... | collective-permute-start | bytes 392 | tf_op jit(solution)/shard_map/ppermute | solution.py:293
  1.3 1.0 %copy-start.1 = (f32[1024,128]{1,0:T(8,128)S(1)}, f32[1024,128]{1,0:T(8,128)}, u32[]{:S(2)}) copy-start(f32[1024,128]{1,0:T(8,128)} %fixels_ref.1) | copy-start | bytes 1572868
  2.5 22.1 %collective-permute-start.13 = (f32[8,64,128]{2,1,0:T(8,128)S(1)}, f32[8,64,128]{2,1,0:T(8,128)S(1)}, u32[]{:S(2)}, u32[]{:S(2)}) collective-permute-start(f32[8,64,128]{2,1,0:T(8,128)S(1)} %get-tuple-element.29.refs_0_), channel_id=1, source_target_pairs={{0,16},{2,18},{4,20},{6,22},{8,24},{10,26},{12,28},{14,30},{16,0},... | collective-permute-start | bytes 786440 | tf_op jit(solution)/shard_map/ppermute | solution.py:279
  6.2 23.8 %collective-permute-start.4 = (f32[8,64,128]{2,1,0:T(8,128)S(1)}, f32[8,64,128]{2,1,0:T(8,128)S(1)}, u32[]{:S(2)}, u32[]{:S(2)}) collective-permute-start(f32[8,64,128]{2,1,0:T(8,128)S(1)} %get-tuple-element.21.refs_0_), channel_id=1, source_target_pairs={{0,16},{2,18},{4,20},{6,22},{8,24},{10,26},{12,28},{14,30},{16,0},... | collective-permute-start | bytes 786440 | tf_op jit(solution)/shard_map/ppermute | solution.py:279
  6.3 3.6 %collective-permute-start.2 = (s32[2,32]{1,0:T(2,128)S(1)}, s32[2,32]{1,0:T(2,128)S(1)}, u32[]{:S(2)}, u32[]{:S(2)}) collective-permute-start(s32[2,32]{1,0:T(2,128)S(1)} %pad_add_fusion.2), channel_id=1, source_target_pairs={{0,4},{2,6},{4,0},{6,2},{8,12},{10,14},{12,8},{14,10},{16,20},{18,... | collective-permute-start | bytes 776 | tf_op jit(solution)/shard_map/ppermute | solution.py:293
  9.9 8.2 %collective-permute-start.3 = (s32[4,32]{1,0:T(4,128)S(1)}, s32[4,32]{1,0:T(4,128)S(1)}, u32[]{:S(2)}, u32[]{:S(2)}) collective-permute-start(s32[4,32]{1,0:T(4,128)S(1)} %pad_add_fusion.1), channel_id=1, source_target_pairs={{0,8},{2,10},{4,12},{6,14},{8,0},{10,2},{12,4},{14,6},{16,24},{18,... | collective-permute-start | bytes 1544 | tf_op jit(solution)/shard_map/ppermute | solution.py:293
  27.1 6.1 %collective-permute-start.14 = (f32[4,64,128]{2,1,0:T(8,128)S(1)}, f32[4,64,128]{2,1,0:T(8,128)S(1)}, u32[]{:S(2)}, u32[]{:S(2)}) collective-permute-start(f32[4,64,128]{2,1,0:T(8,128)S(1)} %get-tuple-element.30), channel_id=1, source_target_pairs={{0,2},{2,0},{4,6},{6,4},{8,10},{10,8},{12,14},{14,12},{16,18},{18,... | collective-permute-start | bytes 393224 | tf_op jit(solution)/shard_map/ppermute | solution.py:330
  27.2 7.7 %collective-permute-start.15 = (f32[4,64,128]{2,1,0:T(8,128)S(1)}, f32[4,64,128]{2,1,0:T(8,128)S(1)}, u32[]{:S(2)}, u32[]{:S(2)}) collective-permute-start(f32[4,64,128]{2,1,0:T(8,128)S(1)} %get-tuple-element.31), channel_id=1, source_target_pairs={{0,4},{2,6},{4,0},{6,2},{8,12},{10,14},{12,8},{14,10},{16,20},{18,... | collective-permute-start | bytes 393224 | tf_op jit(solution)/shard_map/ppermute | solution.py:330
  29.0 7.1 %collective-permute-start.16 = (f32[4,64,128]{2,1,0:T(8,128)S(1)}, f32[4,64,128]{2,1,0:T(8,128)S(1)}, u32[]{:S(2)}, u32[]{:S(2)}) collective-permute-start(f32[4,64,128]{2,1,0:T(8,128)S(1)} %get-tuple-element.32), channel_id=1, source_target_pairs={{0,6},{2,4},{4,2},{6,0},{8,14},{10,12},{12,10},{14,8},{16,22},{18,... | collective-permute-start | bytes 393224 | tf_op jit(solution)/shard_map/ppermute | solution.py:330
  29.1 8.9 %collective-permute-start.17 = (f32[4,64,128]{2,1,0:T(8,128)S(1)}, f32[4,64,128]{2,1,0:T(8,128)S(1)}, u32[]{:S(2)}, u32[]{:S(2)}) collective-permute-start(f32[4,64,128]{2,1,0:T(8,128)S(1)} %get-tuple-element.33), channel_id=1, source_target_pairs={{0,8},{2,10},{4,12},{6,14},{8,0},{10,2},{12,4},{14,6},{16,24},{18,... | collective-permute-start | bytes 393224 | tf_op jit(solution)/shard_map/ppermute | solution.py:330
  30.0 8.6 %collective-permute-start.18 = (f32[4,64,128]{2,1,0:T(8,128)S(1)}, f32[4,64,128]{2,1,0:T(8,128)S(1)}, u32[]{:S(2)}, u32[]{:S(2)}) collective-permute-start(f32[4,64,128]{2,1,0:T(8,128)S(1)} %get-tuple-element.34), channel_id=1, source_target_pairs={{0,10},{2,8},{4,14},{6,12},{8,2},{10,0},{12,6},{14,4},{16,26},{18,... | collective-permute-start | bytes 393224 | tf_op jit(solution)/shard_map/ppermute | solution.py:330
  33.3 8.9 %collective-permute-start.19 = (f32[4,64,128]{2,1,0:T(8,128)S(1)}, f32[4,64,128]{2,1,0:T(8,128)S(1)}, u32[]{:S(2)}, u32[]{:S(2)}) collective-permute-start(f32[4,64,128]{2,1,0:T(8,128)S(1)} %get-tuple-element.35), channel_id=1, source_target_pairs={{0,12},{2,14},{4,8},{6,10},{8,4},{10,6},{12,0},{14,2},{16,28},{18,... | collective-permute-start | bytes 393224 | tf_op jit(solution)/shard_map/ppermute | solution.py:330
  34.9 8.9 %collective-permute-start.20 = (f32[4,64,128]{2,1,0:T(8,128)S(1)}, f32[4,64,128]{2,1,0:T(8,128)S(1)}, u32[]{:S(2)}, u32[]{:S(2)}) collective-permute-start(f32[4,64,128]{2,1,0:T(8,128)S(1)} %get-tuple-element.36), channel_id=1, source_target_pairs={{0,14},{2,12},{4,10},{6,8},{8,6},{10,4},{12,2},{14,0},{16,30},{18,... | collective-permute-start | bytes 393224 | tf_op jit(solution)/shard_map/ppermute | solution.py:330
  36.0 11.8 %collective-permute-start.10 = (f32[4,64,128]{2,1,0:T(8,128)S(1)}, f32[4,64,128]{2,1,0:T(8,128)S(1)}, u32[]{:S(2)}, u32[]{:S(2)}) collective-permute-start(f32[4,64,128]{2,1,0:T(8,128)S(1)} %get-tuple-element.27), channel_id=1, source_target_pairs={{0,12},{2,14},{4,8},{6,10},{8,4},{10,6},{12,0},{14,2},{16,28},{18,... | collective-permute-start | bytes 393224 | tf_op jit(solution)/shard_map/ppermute | solution.py:330
  38.0 11.6 %collective-permute-start.11 = (f32[4,64,128]{2,1,0:T(8,128)S(1)}, f32[4,64,128]{2,1,0:T(8,128)S(1)}, u32[]{:S(2)}, u32[]{:S(2)}) collective-permute-start(f32[4,64,128]{2,1,0:T(8,128)S(1)} %get-tuple-element.28), channel_id=1, source_target_pairs={{0,14},{2,12},{4,10},{6,8},{8,6},{10,4},{12,2},{14,0},{16,30},{18,... | collective-permute-start | bytes 393224 | tf_op jit(solution)/shard_map/ppermute | solution.py:330
  38.6 11.3 %collective-permute-start.5 = (f32[4,64,128]{2,1,0:T(8,128)S(1)}, f32[4,64,128]{2,1,0:T(8,128)S(1)}, u32[]{:S(2)}, u32[]{:S(2)}) collective-permute-start(f32[4,64,128]{2,1,0:T(8,128)S(1)} %get-tuple-element.22), channel_id=1, source_target_pairs={{0,2},{2,0},{4,6},{6,4},{8,10},{10,8},{12,14},{14,12},{16,18},{18,... | collective-permute-start | bytes 393224 | tf_op jit(solution)/shard_map/ppermute | solution.py:330
  39.9 1.6 %copy-start = (f32[8,4,128,128]{3,2,1,0:T(8,128)S(1)}, f32[8,4,128,128]{3,2,1,0:T(8,128)}, u32[]{:S(2)}) copy-start(f32[8,4,128,128]{3,2,1,0:T(8,128)} %param.8) | copy-start | bytes 6291460
  41.5 8.5 %copy-start.3 = (f32[4,128]{1,0:T(4,128)S(1)}, f32[4,128]{1,0:T(4,128)}, u32[]{:S(2)}) copy-start(f32[4,128]{1,0:T(4,128)} %param.11) | copy-start | bytes 6148
  41.5 8.5 %copy-start.4 = (f32[4,128]{1,0:T(4,128)S(1)}, f32[4,128]{1,0:T(4,128)}, u32[]{:S(2)}) copy-start(f32[4,128]{1,0:T(4,128)} %param.10) | copy-start | bytes 6148
  42.2 14.7 %collective-permute-start.6 = (f32[4,64,128]{2,1,0:T(8,128)S(1)}, f32[4,64,128]{2,1,0:T(8,128)S(1)}, u32[]{:S(2)}, u32[]{:S(2)}) collective-permute-start(f32[4,64,128]{2,1,0:T(8,128)S(1)} %get-tuple-element.23), channel_id=1, source_target_pairs={{0,4},{2,6},{4,0},{6,2},{8,12},{10,14},{12,8},{14,10},{16,20},{18,... | collective-permute-start | bytes 393224 | tf_op jit(solution)/shard_map/ppermute | solution.py:330
  43.8 13.6 %collective-permute-start.7 = (f32[4,64,128]{2,1,0:T(8,128)S(1)}, f32[4,64,128]{2,1,0:T(8,128)S(1)}, u32[]{:S(2)}, u32[]{:S(2)}) collective-permute-start(f32[4,64,128]{2,1,0:T(8,128)S(1)} %get-tuple-element.24), channel_id=1, source_target_pairs={{0,6},{2,4},{4,2},{6,0},{8,14},{10,12},{12,10},{14,8},{16,22},{18,... | collective-permute-start | bytes 393224 | tf_op jit(solution)/shard_map/ppermute | solution.py:330
  47.9 9.5 %collective-permute-start.8 = (f32[4,64,128]{2,1,0:T(8,128)S(1)}, f32[4,64,128]{2,1,0:T(8,128)S(1)}, u32[]{:S(2)}, u32[]{:S(2)}) collective-permute-start(f32[4,64,128]{2,1,0:T(8,128)S(1)} %get-tuple-element.25), channel_id=1, source_target_pairs={{0,8},{2,10},{4,12},{6,14},{8,0},{10,2},{12,4},{14,6},{16,24},{18,... | collective-permute-start | bytes 393224 | tf_op jit(solution)/shard_map/ppermute | solution.py:330
  49.5 7.9 %collective-permute-start.9 = (f32[4,64,128]{2,1,0:T(8,128)S(1)}, f32[4,64,128]{2,1,0:T(8,128)S(1)}, u32[]{:S(2)}, u32[]{:S(2)}) collective-permute-start(f32[4,64,128]{2,1,0:T(8,128)S(1)} %get-tuple-element.26), channel_id=1, source_target_pairs={{0,10},{2,8},{4,14},{6,12},{8,2},{10,0},{12,6},{14,4},{16,26},{18,... | collective-permute-start | bytes 393224 | tf_op jit(solution)/shard_map/ppermute | solution.py:330
  50.0 14.3 %collective-permute-start = (f32[72,128]{1,0:T(8,128)S(1)}, f32[72,128]{1,0:T(8,128)S(1)}, u32[]{:S(2)}, u32[]{:S(2)}) collective-permute-start(f32[72,128]{1,0:T(8,128)S(1)} %pad_maximum_fusion.1), channel_id=1, source_target_pairs={{0,1},{1,0},{2,3},{3,2},{4,5},{5,4},{6,7},{7,6},{8,9},{9,8},{10,11... | collective-permute-start | bytes 110600 | tf_op jit(solution)/shard_map/ppermute | solution.py:318
  56.8 7.5 %copy-start.2 = (f32[4,256]{1,0:T(4,128)S(1)}, f32[4,256]{1,0:T(4,128)}, u32[]{:S(2)}) copy-start(f32[4,256]{1,0:T(4,128)} %contrast_ref.1) | copy-start | bytes 12292
  56.8 9.3 %collective-permute-start.21 = (f32[64,1024]{1,0:T(8,128)S(1)}, f32[64,1024]{1,0:T(8,128)S(1)}, u32[]{:S(2)}, u32[]{:S(2)}) collective-permute-start(f32[64,1024]{1,0:T(8,128)S(1)} %shard_map.79.refs_1_), channel_id=1, source_target_pairs={{0,1},{1,0},{2,3},{3,2},{4,5},{5,4},{6,7},{7,6},{8,9},{9,8},{10,11... | collective-permute-start | bytes 786440 | tf_op jit(solution)/shard_map/ppermute | solution.py:344
  62.7 8.2 %collective-permute-start.12 = (f32[64,1024]{1,0:T(8,128)S(1)}, f32[64,1024]{1,0:T(8,128)S(1)}, u32[]{:S(2)}, u32[]{:S(2)}) collective-permute-start(f32[64,1024]{1,0:T(8,128)S(1)} %shard_map.77.refs_0_), channel_id=1, source_target_pairs={{0,1},{1,0},{2,3},{3,2},{4,5},{5,4},{6,7},{7,6},{8,9},{9,8},{10,11... | collective-permute-start | bytes 786440 | tf_op jit(solution)/shard_map/ppermute | solution.py:344

commit v3 on v0

v3 whole, which is shorter than its diff:
```python
import functools

import jax
import jax.numpy as jnp
from jax import lax
from jax.experimental import pallas as pl
from jax.experimental.pallas import tpu as pltpu
from jax.sharding import PartitionSpec as P

GROUP = 8
SHARES = (1, 1)
GATE = 2
LANES = 128
ANY = pl.BlockSpec(memory_space=pl.ANY)
SMEM = pl.BlockSpec(memory_space=pltpu.SMEM)
VMEM = pl.BlockSpec(memory_space=pltpu.VMEM)
PARAMS = pltpu.CompilerParams(vmem_limit_bytes=16 * 1024 * 1024)


def cost(flops, bytes_accessed):
    return pl.CostEstimate(flops=flops, bytes_accessed=bytes_accessed, transcendentals=0)


def split(value):
    high = value.astype(jnp.bfloat16)
    return high, (value - high.astype(jnp.float32)).astype(jnp.bfloat16)


def turn_kernel(fixels_ref, out_ref):
    block_count, _, size = out_ref.shape
    for b in range(block_count):
        out_ref[b] = fixels_ref[b * size : (b + 1) * size, :].T


def turn(fixels, block_count):
    rows, width = fixels.shape
    return pl.pallas_call(
        turn_kernel,
        out_shape=jax.ShapeDtypeStruct((block_count, width, rows // block_count), jnp.float32),
        in_specs=[VMEM],
        out_specs=VMEM,
        compiler_params=PARAMS,
        cost_estimate=cost(0, 8 * rows * width),
    )(fixels)


def copy_kernel(value_ref, *refs):
    refs[-1][...] = value_ref[...]


def follow(value, after):
    return pl.pallas_call(
        copy_kernel,
        out_shape=jax.ShapeDtypeStruct(value.shape, value.dtype),
        in_specs=[VMEM] + [ANY] * len(after),
        out_specs=VMEM,
        compiler_params=PARAMS,
        cost_estimate=cost(0, 8 * value.size),
    )(value, *after)


def tiles_kernel(conn_ref, out_ref):
    size = conn_ref.shape[1]
    for t in range(conn_ref.shape[0]):
        high, low = split(conn_ref[t].T)
        out_ref[t, :, :size] = high
        out_ref[t, :, size:] = low


def split_tiles(conn):
    total, size, _ = conn.shape
    return pl.pallas_call(
        tiles_kernel,
        out_shape=jax.ShapeDtypeStruct((total, size, 2 * size), jnp.bfloat16),
        in_specs=[VMEM],
        out_specs=VMEM,
        compiler_params=PARAMS,
        cost_estimate=cost(4 * total * size * size, 8 * total * size * size),
    )(conn)


def pack_kernel(entries, cuts, table_ref, *refs):
    pieces = refs[: len(entries[0])]
    outs = refs[len(pieces) :]
    for partner, columns in enumerate(entries):
        at = 0
        for piece, places in zip(pieces, columns):
            for place in places:
                block = piece[table_ref[1, place]]
                for cut, (start, sub) in enumerate(cuts):
                    outs[partner * len(cuts) + cut][at] = block[start : start + sub, :]
                at += 1


def pack(entries, cuts, pieces, table):
    count = len(entries[0][0]) * len(pieces)
    size = pieces[0].shape[2]
    outs = [
        jax.ShapeDtypeStruct((count, sub, size), jnp.float32) for _ in entries for _, sub in cuts
    ]
    return pl.pallas_call(
        functools.partial(pack_kernel, entries, cuts),
        out_shape=outs,
        in_specs=[SMEM] + [VMEM] * len(pieces),
        out_specs=[VMEM] * len(outs),
        compiler_params=PARAMS,
        cost_estimate=cost(0, 8 * sum(out.size for out in outs)),
    )(table, *pieces)


def smooth_kernel(plan, per_row, source_count, table_ref, *refs):
    sources = refs[:source_count]
    tiles_ref, out_ref, highs, lows = refs[source_count:]
    sub, size = highs.shape[1:]
    block_count = out_ref.shape[1] // size
    for place, source, at, start in plan:
        block = sources[source][table_ref[1, place] if at is None else at]
        tile = table_ref[0, place]
        highs[tile], lows[tile] = split(block[start : start + sub, :])

    for row in range(block_count):
        span = range(row * per_row, (row + 1) * per_row)
        left = jnp.concatenate(
            [
                jnp.concatenate([highs[tile] for tile in span], axis=1),
                jnp.concatenate([lows[tile] for tile in span], axis=1),
            ],
            axis=0,
        )
        right = jnp.concatenate([tiles_ref[tile] for tile in span], axis=0)
        terms = jnp.dot(left, right, preferred_element_type=jnp.float32)
        value = (terms[:sub, :size] + terms[sub:, :size]) + (
            terms[:sub, size:] + terms[sub:, size:]
        )
        out_ref[:, row * size : (row + 1) * size] = value


def smooth(plan, table, sources, sub, tiles, block_count):
    tile_total, size, _ = tiles.shape
    return pl.pallas_call(
        functools.partial(smooth_kernel, plan, tile_total // block_count, len(sources)),
        out_shape=jax.ShapeDtypeStruct((sub, block_count * size), jnp.float32),
        in_specs=[SMEM] + [VMEM] * (len(sources) + 1),
        out_specs=VMEM,
        scratch_shapes=[pltpu.VMEM((tile_total + 1, sub, size), jnp.bfloat16)] * 2,
        compiler_params=PARAMS,
        cost_estimate=cost(
            8 * tile_total * size * size * sub, 4 * tile_total * size * (sub + size)
        ),
    )(table, *sources, tiles)


def design_kernel(cuts, perm_ref, contrast_ref, nuisance_ref, pinv_ref, *refs):
    outs, rows_ref = refs[:-1], refs[-1]
    perms, subjects = perm_ref.shape
    regressors = contrast_ref.shape[0]
    for start in range(0, subjects, LANES):
        want = perm_ref[:, start : start + LANES].astype(jnp.int32)
        lane, part = want % LANES, want // LANES
        for r in range(regressors):
            value = jnp.zeros((perms, LANES), jnp.float32)
            for base in range(0, subjects, LANES):
                table = jnp.broadcast_to(
                    contrast_ref[r : r + 1, base : base + LANES], (perms, LANES)
                )
                found = jnp.take_along_axis(table, lane, axis=1, mode="promise_in_bounds")
                value = jnp.where(part == base // LANES, found, value)
            rows_ref[start // LANES, pl.ds(r, perms, stride=regressors), :] = value
    design = jnp.concatenate([rows_ref[i] for i in range(rows_ref.shape[0])], axis=1)
    result = design
    for n in range(nuisance_ref.shape[0]):
        weight = jnp.sum(design * nuisance_ref[n : n + 1, :], axis=1, keepdims=True)
        result = result - weight * pinv_ref[n : n + 1, :]
    high, low = split(result)
    for (start, sub), out in zip(cuts, outs):
        columns = slice(start, start + sub)
        out[...] = jnp.concatenate(
            [high[:, columns], high[:, columns], low[:, columns], low[:, columns]], axis=1
        )


def reduced_design(perm, contrast, nuisance, pinv, cuts):
    rows = perm.shape[0] * contrast.shape[0]
    subjects = perm.shape[1]
    return pl.pallas_call(
        functools.partial(design_kernel, cuts),
        out_shape=[jax.ShapeDtypeStruct((rows, 4 * sub), jnp.bfloat16) for _, sub in cuts],
        in_specs=[VMEM] * 4,
        out_specs=[VMEM] * len(cuts),
        scratch_shapes=[pltpu.VMEM((subjects // LANES, rows, LANES), jnp.float32)],
        compiler_params=PARAMS,
        cost_estimate=cost(32 * rows * subjects, 8 * rows * subjects),
    )(perm, contrast, nuisance, pinv)


def project_kernel(count, step, last, *refs):
    designs, parts = refs[:count], refs[count : 2 * count]
    before = refs[2 * count : -3] if last else refs[2 * count : -1]
    out_ref = refs[-3] if last else refs[-1]
    fixels = out_ref.shape[1]
    copies = []
    for i, start in enumerate(range(0, fixels, step)):
        span = slice(start, start + step)
        total = before[0][:, span] if before else None
        for design, part in zip(designs, parts):
            high, low = split(part[:, span])
            term = jnp.dot(
                design[...],
                jnp.concatenate([high, low, high, low], axis=0),
                preferred_element_type=jnp.float32,
            )
            total = term if total is None else total + term
        if last:
            held, sems = refs[-2:]
            held[i] = total
            copy = pltpu.make_async_copy(held.at[i], out_ref.at[:, span], sems.at[i])
            copy.start()
            copies.append(copy)
        else:
            out_ref[:, span] = total
    for copy in copies:
        copy.wait()


def project(designs, parts, before, last):
    rows = designs[0].shape[0]
    fixels = parts[0].shape[1]
    step = 256
    steps = fixels // step
    scratch = [pltpu.VMEM((steps, rows, step), jnp.float32), pltpu.SemaphoreType.DMA((steps,))]
    return pl.pallas_call(
        functools.partial(project_kernel, len(parts), step, last),
        out_shape=jax.ShapeDtypeStruct((rows, fixels), jnp.float32),
        in_specs=[VMEM] * (2 * len(parts) + len(before)),
        out_specs=ANY if last else VMEM,
        scratch_shapes=scratch if last else [],
        compiler_params=PARAMS,
        cost_estimate=cost(
            8 * rows * fixels * sum(part.shape[0] for part in parts), 8 * fixels * rows
        ),
    )(*designs, *parts, *before)


def per_device(fixels, conn_tiles, columns, nuisance, nuisance_pinv, contrast, perm_table):
    fix_count = lax.axis_size("fix")
    subj_count = lax.axis_size("subj")
    group = GROUP if fix_count % GROUP == 0 else 1
    lines = fix_count // group
    block_count, per_row = columns.shape
    size = conn_tiles.shape[2]
    width = fixels.shape[1]
    subs = [width * share // sum(SHARES) for share in SHARES]
    starts = [sum(subs[:c]) for c in range(len(subs))]
    tile_total = block_count * per_row
    cap = (tile_total + fix_count - 1) // fix_count
    me = lax.axis_index("fix")
    part = lax.axis_index("subj")

    def swap(value, mask):
        return lax.ppermute(value, "fix", [(i, i ^ mask) for i in range(fix_count)])

    own = turn(fixels, block_count)
    beside = swap(own, 1)
    sent = follow(columns.T, [beside])
    partners = range(group - 2, 0, -2)
    named = jnp.stack([sent.reshape(-1)] + [swap(sent, m).reshape(-1) for m in partners])
    positions = jnp.arange(tile_total)
    earlier = positions[:, None] > positions[None, :]
    owners = named // block_count
    same = owners[:, :, None] == owners[:, None, :]
    ranks = jnp.sum(jnp.logical_and(same, earlier[None]).astype(jnp.int32), axis=2)
    order = jnp.arange(fix_count * cap)
    owner = (me // group + lines - order // (group * cap)) % lines * group + (
        (me % group) ^ (order // cap % group)
    )
    hits = (owners * cap + ranks)[:, None, :] == (owner * cap + order % cap)[:, None]
    tile = positions % block_count * per_row + positions // block_count
    codes = (tile - tile_total) * block_count + named % block_count
    codes = jnp.sum(jnp.where(hits, codes[:, None, :], 0), axis=2).reshape(-1)
    codes = codes + tile_total * block_count
    table = jnp.stack([codes // block_count, codes % block_count]).astype(jnp.int32)

    def places(row, k, other):
        base = ((row * lines + k) * group + other) * cap
        return tuple(range(base, base + cap))

    rows = perm_table.shape[0] // subj_count
    count = nuisance.shape[0]
    shares = []
    for shift in range(subj_count):
        to = (part + shift) % subj_count
        share = jnp.concatenate(
            [
                lax.dynamic_slice_in_dim(perm_table, to * rows, rows, 0).astype(jnp.float32),
                nuisance,
                nuisance_pinv,
            ]
        )
        if shift:
            pairs = [(i, (i + shift) % subj_count) for i in range(subj_count)]
            share = lax.ppermute(share, "subj", pairs)
        shares.append(share)
    shares = jnp.concatenate(shares, axis=1)
    cuts = [
        (shift * width + start, sub)
        for shift in range(subj_count)
        for start, sub in zip(starts, subs)
    ]
    design = reduced_design(
        shares[:rows], contrast, shares[rows : rows + count], shares[rows + count :], cuts
    )

    tiles = split_tiles(conn_tiles.reshape(tile_total, size, size))

    def exchange(pieces, k, cuts, base):
        entries = tuple(
            tuple(places(row, k, e) for e in range(2)) for row in range(1, len(partners) + 1)
        )
        packs = pack(entries, cuts, pieces, table)
        got = [
            [swap(packs[i * len(cuts) + c], m) for i, m in enumerate(partners)]
            for c in range(len(cuts))
        ]
        plan = []
        for e in range(2):
            plan.extend((place, base + e, None) for place in places(0, k, e))
            for source, m in enumerate(partners, base + 2):
                plan.extend(
                    (place, source, e * cap + rank)
                    for rank, place in enumerate(places(0, k, m ^ e))
                )
        return got, plan

    pieces = [own, beside]
    (got,), plan = exchange(pieces, 0, ((0, width),), 0)
    gate = got[GATE:] + [design[0], tiles]
    whole = pieces + got
    plans = [[(place, source, at, start) for place, source, at in plan] for start in starts]
    sources = [list(whole) for _ in subs]
    for k in range(1, lines):
        pairs = [(i, (i + k * group) % fix_count) for i in range(fix_count)]
        piece = follow(lax.ppermute(own, "fix", pairs), gate)
        pieces = [piece, swap(piece, 1)]
        got, plan = exchange(pieces, k, tuple(zip(starts, subs)), len(sources[0]))
        for c, start in enumerate(starts):
            plans[c].extend(
                (place, source, at, start if at is None else 0) for place, source, at in plan
            )
            sources[c].extend(pieces + got[c])
    smoothed = [
        smooth(tuple(plans[c]), table, sources[c], sub, tiles, block_count)
        for c, sub in enumerate(subs)
    ]

    parts = list(smoothed)
    for shift in range(1, subj_count):
        pairs = [(i, (i + shift) % subj_count) for i in range(subj_count)]
        parts.extend(lax.ppermute(value, "subj", pairs) for value in smoothed)
    total = project(design[:-1], parts[:-1], [], False)
    return project(design[-1:], parts[-1:], [total], True)


def solution(mesh):
    placed = (
        P("fix", "subj"),
        P("fix", None, None, None),
        P("fix", None),
        P(None, "subj"),
        P(None, "subj"),
        P(),
        P(None, "subj"),
    )
    return jax.shard_map(
        per_device, mesh=mesh, in_specs=placed, out_specs=P("subj", "fix"), check_vma=False
    )
```

time: 155 us -> 67.2 us (0.43)
  local copies, waits for them, and re-layouts: 69.4 us -> 2.36 us
  blocking collectives: 21.8 us -> 0 us
  starting transfers between devices: 4.61 us -> 24.2 us
  between operations: 13.6 us -> 0.18 us
  matrix products: 8.82 us -> 0 us
  Pallas kernels: 0 us -> 7.96 us
  waiting for transfers between devices: 32.3 us -> 30.1 us
  other arithmetic: 4.15 us -> 2.03 us
    gather x4 -> x0, local copies, waits for them, and re-layouts: 66.6 us -> none  [the longest x2 59.9 us: design_rows(): picked = jnp.take(contrast, perm_table, axis=1)]
    reduce_scatter x1 -> x0, waiting for transfers between devices: 32.3 us -> none  [per_device(): lax.psum_scatter(partial_value, 'subj', scatter_dimension=0, tiled=True)]
    ppermute x0 -> x18, waiting for transfers between devices: none -> 30.1 us  [the longest x14 16.9 us: swap(): return lax.ppermute(value, 'fix', [(i, i ^ mask) for i in range(fix_count)])]
    ppermute x0 -> x18, starting transfers between devices: none -> 24.2 us  [the longest x14 15.4 us: swap(): return lax.ppermute(value, 'fix', [(i, i ^ mask) for i in range(fix_count)])]
    all_to_all x1 -> x0, blocking collectives: 13.6 us -> none  [per_device(): lax.all_to_all(request.reshape(fix_count, capacity), 'fix', split_axis=0,...]
    dot_general x4 -> x0, matrix products: 8.82 us -> none  [the longest x1 4.12 us: per_device(): jnp.einsum('bkij,bkjs->bis', conn_tiles, needed, precision=lax.Precision....]
    psum x1 -> x0, blocking collectives: 8.19 us -> none  [per_device(): fitted = lax.psum(fitted_part, 'subj')]
    pallas_call x0 -> x11, Pallas kernels: none -> 7.96 us  [the longest x2 2.28 us: smooth(): pl.pallas_call(functools.partial(smooth_kernel, plan, tile_total // block...]
  transfers between devices with their start and end apart: 2 -> 18, of which waited for: 1 -> 10; matrix products, arithmetic and copies ran while one was open for 39% -> 4% of each run, Pallas kernels for 0% -> 8%
where the time goes in v3:
time: 67.2 us; the launch traced here: 66.9 us
  waiting for transfers between devices  30.1 us (45%)
  starting transfers between devices  24.2 us (36%)
  Pallas kernels  7.96 us (12%)
  local copies, waits for them, and re-layouts  2.36 us (4%)
  other arithmetic  2.03 us (3%)
    ppermute x14, waiting for transfers between devices, swap(): return lax.ppermute(value, 'fix', [(i, i ^ mask) for i in range(fix_count)])  16.9 us
    ppermute x14, starting transfers between devices, swap(): return lax.ppermute(value, 'fix', [(i, i ^ mask) for i in range(fix_count)])  15.4 us
    ppermute x1, waiting for transfers between devices, per_device(): piece = follow(lax.ppermute(own, 'fix', pairs), gate)  7.49 us
    ppermute x2, waiting for transfers between devices, per_device(): parts.extend((lax.ppermute(value, 'subj', pairs) for value in smoothed))  5.78 us
    ppermute x1, starting transfers between devices, per_device(): piece = follow(lax.ppermute(own, 'fix', pairs), gate)  4.1 us
    ppermute x2, starting transfers between devices, per_device(): parts.extend((lax.ppermute(value, 'subj', pairs) for value in smoothed))  3.17 us
    pallas_call x2, Pallas kernels, smooth(): pl.pallas_call(functools.partial(smooth_kernel, plan, tile_total // block...  2.28 us
    unnamed x12, local copies, waits for them, and re-layouts  1.94 us
  transfers between devices with their start and end apart: 18, of which 10 were waited for; matrix products, arithmetic and copies ran while one was open for 4% of the time, Pallas kernels for 8%

profile of v3, /device:TPU:0, one launch (start us, length us, event | category | flops | bytes accessed | tf_op | source)
XLA Modules:
  0.0 66.9 jit_solution(16596219574202223744)
XLA Ops:
  0.0 1.2 %copy-done.1 = f32[1024,128]{1,0:T(8,128)S(1)} copy-done((f32[1024,128]{1,0:T(8,128)S(1)}, f32[1024,128]{1,0:T(8,128)}, u32[]{:S(2)}) %copy-start.1) | copy-done | bytes 524312
  1.4 4.1 %collective-permute-start.8 = (f32[8,128,128]{2,1,0:T(8,128)S(1)}, f32[8,128,128]{2,1,0:T(8,128)}, u32[]{:S(2)}, u32[]{:S(2)}) collective-permute-start(f32[8,128,128]{2,1,0:T(8,128)S(1)} %shard_map.74.refs_0_), channel_id=1, source_target_pairs={{0,16},{2,18},{4,20},{6,22},{8,24},{10,26},{12,28},{14,30},{16,0},... | collective-permute-start | bytes 1572872 | tf_op jit(solution)/shard_map/ppermute | solution.py:342
  5.5 0.8 %dynamic-slice_convert_fusion.1 = (f32[64,128]{1,0:T(8,128)S(1)}, f32[64,128]{1,0:T(8,128)S(1)}) fusion(s32[128,128]{1,0:T(8,128)} %param.13, s32[]{:T(128)S(6)} %select_n.138, s32[]{:T(128)S(6)} %select_n.140), kind=kLoop, calls=%fused_computation.5 | loop fusion | flops 16384 | bytes 131080 | tf_op jit(solution)/shard_map/convert_element_type | solution.py:294
  6.3 0.7 %pad_maximum_fusion.1 = f32[72,128]{1,0:T(8,128)S(1)} fusion(f32[4,128]{1,0:T(4,128)} %param.11, f32[4,128]{1,0:T(4,128)} %param.10, f32[64,128]{1,0:T(8,128)S(1)} %get-tuple-element.34), kind=kLoop, calls=%fused_computation.3 | loop fusion | flops 18432 | bytes 73728 | tf_op jit(solution)/shard_map/concatenate | solution.py:292
  7.0 1.5 %collective-permute-start = (f32[72,128]{1,0:T(8,128)S(1)}, f32[72,128]{1,0:T(8,128)S(1)}, u32[]{:S(2)}, u32[]{:S(2)}) collective-permute-start(f32[72,128]{1,0:T(8,128)S(1)} %pad_maximum_fusion.1), channel_id=1, source_target_pairs={{0,1},{1,0},{2,3},{3,2},{4,5},{5,4},{6,7},{7,6},{8,9},{9,8},{10,11... | collective-permute-start | bytes 110600 | tf_op jit(solution)/shard_map/ppermute | solution.py:301
  8.6 0.7 %copy-done.3 = s32[8,4]{0,1:T(4,128)S(1)} copy-done((s32[8,4]{0,1:T(4,128)S(1)}, s32[8,4]{0,1:T(4,128)}, u32[]{:S(2)}) %copy-start.3) | copy-done | bytes 152
  9.3 1.5 %collective-permute-start.4 = (s32[4,8]{1,0:T(4,128)S(1)}, s32[4,8]{1,0:T(4,128)S(1)}, u32[]{:S(2)}, u32[]{:S(2)}) collective-permute-start(s32[4,8]{1,0:T(4,128)S(1)} %shard_map.75), channel_id=1, source_target_pairs={{0,4},{2,6},{4,0},{6,2},{8,12},{10,14},{12,8},{14,10},{16,20},{18,... | collective-permute-start | bytes 392 | tf_op jit(solution)/shard_map/ppermute | solution.py:260
  10.8 1.6 %collective-permute-start.3 = (s32[4,8]{1,0:T(4,128)S(1)}, s32[4,8]{1,0:T(4,128)S(1)}, u32[]{:S(2)}, u32[]{:S(2)}) collective-permute-start(s32[4,8]{1,0:T(4,128)S(1)} %shard_map.75), channel_id=1, source_target_pairs={{0,8},{2,10},{4,12},{6,14},{8,0},{10,2},{12,4},{14,6},{16,24},{18,... | collective-permute-start | bytes 392 | tf_op jit(solution)/shard_map/ppermute | solution.py:260
  13.0 3.8 %collective-permute-done.3 = s32[4,8]{1,0:T(4,128)S(1)} collective-permute-done((s32[4,8]{1,0:T(4,128)S(1)}, s32[4,8]{1,0:T(4,128)S(1)}, u32[]{:S(2)}, u32[]{:S(2)}) %collective-permute-start.3) | collective-permute-done | bytes 160 | tf_op jit(solution)/shard_map/ppermute | solution.py:260
  18.2 1.6 %collective-permute-start.7 = (f32[4,128,128]{2,1,0:T(8,128)S(1)}, f32[4,128,128]{2,1,0:T(8,128)S(1)}, u32[]{:S(2)}, u32[]{:S(2)}) collective-permute-start(f32[4,128,128]{2,1,0:T(8,128)S(1)} %get-tuple-element.21), channel_id=1, source_target_pairs={{0,4},{2,6},{4,0},{6,2},{8,12},{10,14},{12,8},{14,10},{16,20},{18,... | collective-permute-start | bytes 786440 | tf_op jit(solution)/shard_map/ppermute | solution.py:260
  19.7 0.6 shard_map.77.refs_2_.refs_10_
  20.5 0.8 %shard_map.73 = (bf16[256,256]{1,0:T(8,128)(2,1)S(1)}, bf16[256,256]{1,0:T(8,128)(2,1)S(1)}, bf16[256,256]{1,0:T(8,128)(2,1)S(1)}, bf16[256,256]{1,0:T(8,128)(2,1)S(1)}) custom-call(f32[64,256]{1,0:T(8,128)S(1)} %slice.12.perm_ref, f32[4,256]{1,0:T(4,128)S(1)} %copy-done.2, f32[4,256]{1,0:T(4,128)S(1)} %get-tuple-element.32.nuisance_ref, ...), custom_call_target="tpu_custom_call" | custom-call | flops 2097152 | bytes 524288 | tf_op jit(solution)/shard_map/pallas_call | solution.py:185
  21.3 7.5 %collective-permute-done.8.value_ref = f32[8,128,128]{2,1,0:T(8,128)} collective-permute-done((f32[8,128,128]{2,1,0:T(8,128)S(1)}, f32[8,128,128]{2,1,0:T(8,128)}, u32[]{:S(2)}, u32[]{:S(2)}) %collective-permute-start.8) | collective-permute-done | bytes 524320 | tf_op jit(solution)/shard_map/ppermute | solution.py:342
  28.8 1.1 %shard_map.78.refs_0_.refs_5_ = f32[8,128,128]{2,1,0:T(8,128)S(1)} custom-call(f32[8,128,128]{2,1,0:T(8,128)} %collective-permute-done.8.value_ref, f32[4,128,128]{2,1,0:T(8,128)S(1)} %collective-permute-done.7.refs_0_.refs_4_, bf16[256,256]{1,0:T(8,128)(2,1)S(1)} %get-tuple-element.22.refs_1_.refs_0_, bf16[32,128,256]{2,1,0:T(8,128)(2,1)S(1)} %shard_map.77.refs_2_.refs_10_), custom_call_target="tpu_custom_call" | custom-call | bytes 1048576 | tf_op jit(solution)/shard_map/pallas_call | solution.py:52
  29.9 1.6 %collective-permute-start.5 = (f32[4,128,128]{2,1,0:T(8,128)S(1)}, f32[4,128,128]{2,1,0:T(8,128)S(1)}, u32[]{:S(2)}, u32[]{:S(2)}) collective-permute-start(f32[4,128,128]{2,1,0:T(8,128)S(1)} %get-tuple-element.19), channel_id=1, source_target_pairs={{0,12},{2,14},{4,8},{6,10},{8,4},{10,6},{12,0},{14,2},{16,28},{18,... | collective-permute-start | bytes 786440 | tf_op jit(solution)/shard_map/ppermute | solution.py:260
  31.5 1.5 %collective-permute-start.6 = (f32[4,128,128]{2,1,0:T(8,128)S(1)}, f32[4,128,128]{2,1,0:T(8,128)S(1)}, u32[]{:S(2)}, u32[]{:S(2)}) collective-permute-start(f32[4,128,128]{2,1,0:T(8,128)S(1)} %get-tuple-element.20), channel_id=1, source_target_pairs={{0,8},{2,10},{4,12},{6,14},{8,0},{10,2},{12,4},{14,6},{16,24},{18,... | collective-permute-start | bytes 786440 | tf_op jit(solution)/shard_map/ppermute | solution.py:260
  34.2 1.4 %collective-permute-start.15 = (f32[4,64,128]{2,1,0:T(8,128)S(1)}, f32[4,64,128]{2,1,0:T(8,128)S(1)}, u32[]{:S(2)}, u32[]{:S(2)}) collective-permute-start(f32[4,64,128]{2,1,0:T(8,128)S(1)} %get-tuple-element.29), channel_id=1, source_target_pairs={{0,8},{2,10},{4,12},{6,14},{8,0},{10,2},{12,4},{14,6},{16,24},{18,... | collective-permute-start | bytes 393224 | tf_op jit(solution)/shard_map/ppermute | solution.py:260
  35.6 1.5 %collective-permute-start.16 = (f32[4,64,128]{2,1,0:T(8,128)S(1)}, f32[4,64,128]{2,1,0:T(8,128)S(1)}, u32[]{:S(2)}, u32[]{:S(2)}) collective-permute-start(f32[4,64,128]{2,1,0:T(8,128)S(1)} %get-tuple-element.30), channel_id=1, source_target_pairs={{0,4},{2,6},{4,0},{6,2},{8,12},{10,14},{12,8},{14,10},{16,20},{18,... | collective-permute-start | bytes 393224 | tf_op jit(solution)/shard_map/ppermute | solution.py:260
  37.2 2.8 %collective-permute-done.5.refs_2_ = f32[4,128,128]{2,1,0:T(8,128)S(1)} collective-permute-done((f32[4,128,128]{2,1,0:T(8,128)S(1)}, f32[4,128,128]{2,1,0:T(8,128)S(1)}, u32[]{:S(2)}, u32[]{:S(2)}) %collective-permute-start.5) | collective-permute-done | bytes 262176 | tf_op jit(solution)/shard_map/ppermute | solution.py:260
  40.0 1.5 %collective-permute-start.10 = (f32[4,64,128]{2,1,0:T(8,128)S(1)}, f32[4,64,128]{2,1,0:T(8,128)S(1)}, u32[]{:S(2)}, u32[]{:S(2)}) collective-permute-start(f32[4,64,128]{2,1,0:T(8,128)S(1)} %get-tuple-element.23), channel_id=1, source_target_pairs={{0,12},{2,14},{4,8},{6,10},{8,4},{10,6},{12,0},{14,2},{16,28},{18,... | collective-permute-start | bytes 393224 | tf_op jit(solution)/shard_map/ppermute | solution.py:260
  41.5 4.2 %collective-permute-done.6.refs_3_ = f32[4,128,128]{2,1,0:T(8,128)S(1)} collective-permute-done((f32[4,128,128]{2,1,0:T(8,128)S(1)}, f32[4,128,128]{2,1,0:T(8,128)S(1)}, u32[]{:S(2)}, u32[]{:S(2)}) %collective-permute-start.6) | collective-permute-done | bytes 262176 | tf_op jit(solution)/shard_map/ppermute | solution.py:260
  46.3 2.2 %collective-permute-done.14.refs_7_ = f32[4,64,128]{2,1,0:T(8,128)S(1)} collective-permute-done((f32[4,64,128]{2,1,0:T(8,128)S(1)}, f32[4,64,128]{2,1,0:T(8,128)S(1)}, u32[]{:S(2)}, u32[]{:S(2)}) %collective-permute-start.14) | collective-permute-done | bytes 131104 | tf_op jit(solution)/shard_map/ppermute | solution.py:260
  48.4 1.5 %collective-permute-start.12 = (f32[4,64,128]{2,1,0:T(8,128)S(1)}, f32[4,64,128]{2,1,0:T(8,128)S(1)}, u32[]{:S(2)}, u32[]{:S(2)}) collective-permute-start(f32[4,64,128]{2,1,0:T(8,128)S(1)} %get-tuple-element.25), channel_id=1, source_target_pairs={{0,4},{2,6},{4,0},{6,2},{8,12},{10,14},{12,8},{14,10},{16,20},{18,... | collective-permute-start | bytes 393224 | tf_op jit(solution)/shard_map/ppermute | solution.py:260
  50.0 1.3 %collective-permute-done.15.refs_8_ = f32[4,64,128]{2,1,0:T(8,128)S(1)} collective-permute-done((f32[4,64,128]{2,1,0:T(8,128)S(1)}, f32[4,64,128]{2,1,0:T(8,128)S(1)}, u32[]{:S(2)}, u32[]{:S(2)}) %collective-permute-start.15) | collective-permute-done | bytes 131104 | tf_op jit(solution)/shard_map/ppermute | solution.py:260
  51.3 1.1 %shard_map.81.refs_3_ = f32[64,1024]{1,0:T(8,128)S(1)} custom-call(s32[2,128]{1,0:T(2,128)S(1)} %pad_add_fusion.1.table_ref, f32[8,128,128]{2,1,0:T(8,128)S(1)} %shard_map.74.refs_0_, f32[8,128,128]{2,1,0:T(8,128)S(1)} %collective-permute-done.1.refs_0_.refs_1_, f32[4,128,128]{2,1,0:T(8,128)S(1)} %collective-permute-done.5.refs_2_, ...), custom_call_target="tpu_custom_call" | custom-call | flops 268435456 | bytes 3145728 | tf_op jit(solution)/shard_map/pallas_call | solution.py:140
  52.5 1.6 %collective-permute-start.17 = (f32[64,1024]{1,0:T(8,128)S(1)}, f32[64,1024]{1,0:T(8,128)S(1)}, u32[]{:S(2)}, u32[]{:S(2)}) collective-permute-start(f32[64,1024]{1,0:T(8,128)S(1)} %shard_map.81.refs_3_), channel_id=1, source_target_pairs={{0,1},{1,0},{2,3},{3,2},{4,5},{5,4},{6,7},{7,6},{8,9},{9,8},{10,11... | collective-permute-start | bytes 786440 | tf_op jit(solution)/shard_map/ppermute | solution.py:358
  54.1 2.4 %collective-permute-done.11.refs_8_ = f32[4,64,128]{2,1,0:T(8,128)S(1)} collective-permute-done((f32[4,64,128]{2,1,0:T(8,128)S(1)}, f32[4,64,128]{2,1,0:T(8,128)S(1)}, u32[]{:S(2)}, u32[]{:S(2)}) %collective-permute-start.11) | collective-permute-done | bytes 131104 | tf_op jit(solution)/shard_map/ppermute | solution.py:260
  56.5 1.1 %shard_map.80.refs_4_ = f32[64,1024]{1,0:T(8,128)S(1)} custom-call(s32[2,128]{1,0:T(2,128)S(1)} %pad_add_fusion.1.table_ref, f32[8,128,128]{2,1,0:T(8,128)S(1)} %shard_map.74.refs_0_, f32[8,128,128]{2,1,0:T(8,128)S(1)} %collective-permute-done.1.refs_0_.refs_1_, f32[4,128,128]{2,1,0:T(8,128)S(1)} %collective-permute-done.5.refs_2_, ...), custom_call_target="tpu_custom_call" | custom-call | flops 268435456 | bytes 3145728 | tf_op jit(solution)/shard_map/pallas_call | solution.py:140
  57.7 1.6 %collective-permute-start.13 = (f32[64,1024]{1,0:T(8,128)S(1)}, f32[64,1024]{1,0:T(8,128)S(1)}, u32[]{:S(2)}, u32[]{:S(2)}) collective-permute-start(f32[64,1024]{1,0:T(8,128)S(1)} %shard_map.80.refs_4_), channel_id=1, source_target_pairs={{0,1},{1,0},{2,3},{3,2},{4,5},{5,4},{6,7},{7,6},{8,9},{9,8},{10,11... | collective-permute-start | bytes 786440 | tf_op jit(solution)/shard_map/ppermute | solution.py:358
  59.3 0.7 %collective-permute-done.17.refs_5_ = f32[64,1024]{1,0:T(8,128)S(1)} collective-permute-done((f32[64,1024]{1,0:T(8,128)S(1)}, f32[64,1024]{1,0:T(8,128)S(1)}, u32[]{:S(2)}, u32[]{:S(2)}) %collective-permute-start.17) | collective-permute-done | bytes 262176 | tf_op jit(solution)/shard_map/ppermute | solution.py:358
  60.5 5.1 %collective-permute-done.13.refs_1_ = f32[64,1024]{1,0:T(8,128)S(1)} collective-permute-done((f32[64,1024]{1,0:T(8,128)S(1)}, f32[64,1024]{1,0:T(8,128)S(1)}, u32[]{:S(2)}, u32[]{:S(2)}) %collective-permute-start.13) | collective-permute-done | bytes 262176 | tf_op jit(solution)/shard_map/ppermute | solution.py:358
  65.6 1.2 %shard_map.83 = f32[256,1024]{1,0:T(8,128)} custom-call(bf16[256,256]{1,0:T(8,128)(2,1)S(1)} %get-tuple-element.18.refs_0_, f32[64,1024]{1,0:T(8,128)S(1)} %collective-permute-done.13.refs_1_, f32[256,1024]{1,0:T(8,128)S(1)} %shard_map.82.refs_2_), custom_call_target="tpu_custom_call" | custom-call | flops 134217728 | bytes 2097152 | tf_op jit(solution)/shard_map/pallas_call | solution.py:231
  (47 shorter events, 4.8 us)
Async XLA Ops:
  0.0 19.7 %copy-start = (f32[8,4,128,128]{3,2,1,0:T(8,128)S(1)}, f32[8,4,128,128]{3,2,1,0:T(8,128)}, u32[]{:S(2)}) copy-start(f32[8,4,128,128]{3,2,1,0:T(8,128)} %param.8) | copy-start | bytes 6291460
  0.0 1.2 %copy-start.1 = (f32[1024,128]{1,0:T(8,128)S(1)}, f32[1024,128]{1,0:T(8,128)}, u32[]{:S(2)}) copy-start(f32[1024,128]{1,0:T(8,128)} %fixels_ref.1) | copy-start | bytes 1572868
  1.4 27.4 %collective-permute-start.8 = (f32[8,128,128]{2,1,0:T(8,128)S(1)}, f32[8,128,128]{2,1,0:T(8,128)}, u32[]{:S(2)}, u32[]{:S(2)}) collective-permute-start(f32[8,128,128]{2,1,0:T(8,128)S(1)} %shard_map.74.refs_0_), channel_id=1, source_target_pairs={{0,16},{2,18},{4,20},{6,22},{8,24},{10,26},{12,28},{14,30},{16,0},... | collective-permute-start | bytes 1572872 | tf_op jit(solution)/shard_map/ppermute | solution.py:342
  5.5 3.0 %collective-permute-start.1 = (f32[8,128,128]{2,1,0:T(8,128)S(1)}, f32[8,128,128]{2,1,0:T(8,128)S(1)}, u32[]{:S(2)}, u32[]{:S(2)}) collective-permute-start(f32[8,128,128]{2,1,0:T(8,128)S(1)} %shard_map.74.refs_0_), channel_id=1, source_target_pairs={{0,2},{2,0},{4,6},{6,4},{8,10},{10,8},{12,14},{14,12},{16,18},{18,... | collective-permute-start | bytes 1572872 | tf_op jit(solution)/shard_map/ppermute | solution.py:260
  7.0 13.4 %collective-permute-start = (f32[72,128]{1,0:T(8,128)S(1)}, f32[72,128]{1,0:T(8,128)S(1)}, u32[]{:S(2)}, u32[]{:S(2)}) collective-permute-start(f32[72,128]{1,0:T(8,128)S(1)} %pad_maximum_fusion.1), channel_id=1, source_target_pairs={{0,1},{1,0},{2,3},{3,2},{4,5},{5,4},{6,7},{7,6},{8,9},{9,8},{10,11... | collective-permute-start | bytes 110600 | tf_op jit(solution)/shard_map/ppermute | solution.py:301
  8.6 0.7 %copy-start.3 = (s32[8,4]{0,1:T(4,128)S(1)}, s32[8,4]{0,1:T(4,128)}, u32[]{:S(2)}) copy-start(s32[8,4]{0,1:T(4,128)} %param.9) | copy-start | bytes 388
  9.3 3.6 %collective-permute-start.4 = (s32[4,8]{1,0:T(4,128)S(1)}, s32[4,8]{1,0:T(4,128)S(1)}, u32[]{:S(2)}, u32[]{:S(2)}) collective-permute-start(s32[4,8]{1,0:T(4,128)S(1)} %shard_map.75), channel_id=1, source_target_pairs={{0,4},{2,6},{4,0},{6,2},{8,12},{10,14},{12,8},{14,10},{16,20},{18,... | collective-permute-start | bytes 392 | tf_op jit(solution)/shard_map/ppermute | solution.py:260
  10.8 6.0 %collective-permute-start.3 = (s32[4,8]{1,0:T(4,128)S(1)}, s32[4,8]{1,0:T(4,128)S(1)}, u32[]{:S(2)}, u32[]{:S(2)}) collective-permute-start(s32[4,8]{1,0:T(4,128)S(1)} %shard_map.75), channel_id=1, source_target_pairs={{0,8},{2,10},{4,12},{6,14},{8,0},{10,2},{12,4},{14,6},{16,24},{18,... | collective-permute-start | bytes 392 | tf_op jit(solution)/shard_map/ppermute | solution.py:260
  12.4 4.5 %collective-permute-start.2 = (s32[4,8]{1,0:T(4,128)S(1)}, s32[4,8]{1,0:T(4,128)S(1)}, u32[]{:S(2)}, u32[]{:S(2)}) collective-permute-start(s32[4,8]{1,0:T(4,128)S(1)} %shard_map.75), channel_id=1, source_target_pairs={{0,12},{2,14},{4,8},{6,10},{8,4},{10,6},{12,0},{14,2},{16,28},{18,... | collective-permute-start | bytes 392 | tf_op jit(solution)/shard_map/ppermute | solution.py:260
  18.2 10.6 %collective-permute-start.7 = (f32[4,128,128]{2,1,0:T(8,128)S(1)}, f32[4,128,128]{2,1,0:T(8,128)S(1)}, u32[]{:S(2)}, u32[]{:S(2)}) collective-permute-start(f32[4,128,128]{2,1,0:T(8,128)S(1)} %get-tuple-element.21), channel_id=1, source_target_pairs={{0,4},{2,6},{4,0},{6,2},{8,12},{10,14},{12,8},{14,10},{16,20},{18,... | collective-permute-start | bytes 786440 | tf_op jit(solution)/shard_map/ppermute | solution.py:260
  19.7 0.7 %copy-start.4 = (f32[4,128]{1,0:T(4,128)S(1)}, f32[4,128]{1,0:T(4,128)}, u32[]{:S(2)}) copy-start(f32[4,128]{1,0:T(4,128)} %param.11) | copy-start | bytes 6148
  19.7 0.7 %copy-start.5 = (f32[4,128]{1,0:T(4,128)S(1)}, f32[4,128]{1,0:T(4,128)}, u32[]{:S(2)}) copy-start(f32[4,128]{1,0:T(4,128)} %param.10) | copy-start | bytes 6148
  19.7 0.7 %copy-start.2 = (f32[4,256]{1,0:T(4,128)S(1)}, f32[4,256]{1,0:T(4,128)}, u32[]{:S(2)}) copy-start(f32[4,256]{1,0:T(4,128)} %contrast_ref.1) | copy-start | bytes 12292
  29.8 3.1 %collective-permute-start.9 = (f32[8,128,128]{2,1,0:T(8,128)S(1)}, f32[8,128,128]{2,1,0:T(8,128)S(1)}, u32[]{:S(2)}, u32[]{:S(2)}) collective-permute-start(f32[8,128,128]{2,1,0:T(8,128)S(1)} %shard_map.78.refs_0_.refs_5_), channel_id=1, source_target_pairs={{0,2},{2,0},{4,6},{6,4},{8,10},{10,8},{12,14},{14,12},{16,18},{18,... | collective-permute-start | bytes 1572872 | tf_op jit(solution)/shard_map/ppermute | solution.py:260
  29.9 10.1 %collective-permute-start.5 = (f32[4,128,128]{2,1,0:T(8,128)S(1)}, f32[4,128,128]{2,1,0:T(8,128)S(1)}, u32[]{:S(2)}, u32[]{:S(2)}) collective-permute-start(f32[4,128,128]{2,1,0:T(8,128)S(1)} %get-tuple-element.19), channel_id=1, source_target_pairs={{0,12},{2,14},{4,8},{6,10},{8,4},{10,6},{12,0},{14,2},{16,28},{18,... | collective-permute-start | bytes 786440 | tf_op jit(solution)/shard_map/ppermute | solution.py:260
  31.5 14.2 %collective-permute-start.6 = (f32[4,128,128]{2,1,0:T(8,128)S(1)}, f32[4,128,128]{2,1,0:T(8,128)S(1)}, u32[]{:S(2)}, u32[]{:S(2)}) collective-permute-start(f32[4,128,128]{2,1,0:T(8,128)S(1)} %get-tuple-element.20), channel_id=1, source_target_pairs={{0,8},{2,10},{4,12},{6,14},{8,0},{10,2},{12,4},{14,6},{16,24},{18,... | collective-permute-start | bytes 786440 | tf_op jit(solution)/shard_map/ppermute | solution.py:260
  33.6 14.8 %collective-permute-start.14 = (f32[4,64,128]{2,1,0:T(8,128)S(1)}, f32[4,64,128]{2,1,0:T(8,128)S(1)}, u32[]{:S(2)}, u32[]{:S(2)}) collective-permute-start(f32[4,64,128]{2,1,0:T(8,128)S(1)} %get-tuple-element.28), channel_id=1, source_target_pairs={{0,12},{2,14},{4,8},{6,10},{8,4},{10,6},{12,0},{14,2},{16,28},{18,... | collective-permute-start | bytes 393224 | tf_op jit(solution)/shard_map/ppermute | solution.py:260
  34.2 17.1 %collective-permute-start.15 = (f32[4,64,128]{2,1,0:T(8,128)S(1)}, f32[4,64,128]{2,1,0:T(8,128)S(1)}, u32[]{:S(2)}, u32[]{:S(2)}) collective-permute-start(f32[4,64,128]{2,1,0:T(8,128)S(1)} %get-tuple-element.29), channel_id=1, source_target_pairs={{0,8},{2,10},{4,12},{6,14},{8,0},{10,2},{12,4},{14,6},{16,24},{18,... | collective-permute-start | bytes 393224 | tf_op jit(solution)/shard_map/ppermute | solution.py:260
  35.6 15.7 %collective-permute-start.16 = (f32[4,64,128]{2,1,0:T(8,128)S(1)}, f32[4,64,128]{2,1,0:T(8,128)S(1)}, u32[]{:S(2)}, u32[]{:S(2)}) collective-permute-start(f32[4,64,128]{2,1,0:T(8,128)S(1)} %get-tuple-element.30), channel_id=1, source_target_pairs={{0,4},{2,6},{4,0},{6,2},{8,12},{10,14},{12,8},{14,10},{16,20},{18,... | collective-permute-start | bytes 393224 | tf_op jit(solution)/shard_map/ppermute | solution.py:260
  40.0 14.1 %collective-permute-start.10 = (f32[4,64,128]{2,1,0:T(8,128)S(1)}, f32[4,64,128]{2,1,0:T(8,128)S(1)}, u32[]{:S(2)}, u32[]{:S(2)}) collective-permute-start(f32[4,64,128]{2,1,0:T(8,128)S(1)} %get-tuple-element.23), channel_id=1, source_target_pairs={{0,12},{2,14},{4,8},{6,10},{8,4},{10,6},{12,0},{14,2},{16,28},{18,... | collective-permute-start | bytes 393224 | tf_op jit(solution)/shard_map/ppermute | solution.py:260
  45.7 10.8 %collective-permute-start.11 = (f32[4,64,128]{2,1,0:T(8,128)S(1)}, f32[4,64,128]{2,1,0:T(8,128)S(1)}, u32[]{:S(2)}, u32[]{:S(2)}) collective-permute-start(f32[4,64,128]{2,1,0:T(8,128)S(1)} %get-tuple-element.24), channel_id=1, source_target_pairs={{0,8},{2,10},{4,12},{6,14},{8,0},{10,2},{12,4},{14,6},{16,24},{18,... | collective-permute-start | bytes 393224 | tf_op jit(solution)/shard_map/ppermute | solution.py:260
  48.4 8.1 %collective-permute-start.12 = (f32[4,64,128]{2,1,0:T(8,128)S(1)}, f32[4,64,128]{2,1,0:T(8,128)S(1)}, u32[]{:S(2)}, u32[]{:S(2)}) collective-permute-start(f32[4,64,128]{2,1,0:T(8,128)S(1)} %get-tuple-element.25), channel_id=1, source_target_pairs={{0,4},{2,6},{4,0},{6,2},{8,12},{10,14},{12,8},{14,10},{16,20},{18,... | collective-permute-start | bytes 393224 | tf_op jit(solution)/shard_map/ppermute | solution.py:260
  52.5 7.5 %collective-permute-start.17 = (f32[64,1024]{1,0:T(8,128)S(1)}, f32[64,1024]{1,0:T(8,128)S(1)}, u32[]{:S(2)}, u32[]{:S(2)}) collective-permute-start(f32[64,1024]{1,0:T(8,128)S(1)} %shard_map.81.refs_3_), channel_id=1, source_target_pairs={{0,1},{1,0},{2,3},{3,2},{4,5},{5,4},{6,7},{7,6},{8,9},{9,8},{10,11... | collective-permute-start | bytes 786440 | tf_op jit(solution)/shard_map/ppermute | solution.py:358
  57.7 7.9 %collective-permute-start.13 = (f32[64,1024]{1,0:T(8,128)S(1)}, f32[64,1024]{1,0:T(8,128)S(1)}, u32[]{:S(2)}, u32[]{:S(2)}) collective-permute-start(f32[64,1024]{1,0:T(8,128)S(1)} %shard_map.80.refs_4_), channel_id=1, source_target_pairs={{0,1},{1,0},{2,3},{3,2},{4,5},{5,4},{6,7},{7,6},{8,9},{9,8},{10,11... | collective-permute-start | bytes 786440 | tf_op jit(solution)/shard_map/ppermute | solution.py:358

commit v4 on v3

--- a/solution.py
+++ b/solution.py
@@ -2,14 +2,14 @@
 
 import jax
 import jax.numpy as jnp
+import numpy as np
 from jax import lax
 from jax.experimental import pallas as pl
 from jax.experimental.pallas import tpu as pltpu
 from jax.sharding import PartitionSpec as P
 
 GROUP = 8
-SHARES = (1, 1)
-GATE = 2
+SHARES = (5, 3)
 LANES = 128
 ANY = pl.BlockSpec(memory_space=pl.ANY)
 SMEM = pl.BlockSpec(memory_space=pltpu.SMEM)
@@ -26,29 +26,27 @@
     return high, (value - high.astype(jnp.float32)).astype(jnp.bfloat16)
 
 
-def turn_kernel(fixels_ref, out_ref):
-    block_count, _, size = out_ref.shape
-    for b in range(block_count):
-        out_ref[b] = fixels_ref[b * size : (b + 1) * size, :].T
-
-
-def turn(fixels, block_count):
-    rows, width = fixels.shape
-    return pl.pallas_call(
-        turn_kernel,
-        out_shape=jax.ShapeDtypeStruct((block_count, width, rows // block_count), jnp.float32),
-        in_specs=[VMEM],
-        out_specs=VMEM,
-        compiler_params=PARAMS,
-        cost_estimate=cost(0, 8 * rows * width),
-    )(fixels)
+def follow_kernel(*refs):
+    pass
+
+
+def follow(value, after):
+    return pl.pallas_call(
+        follow_kernel,
+        out_shape=jax.ShapeDtypeStruct(value.shape, value.dtype),
+        in_specs=[ANY] * (1 + len(after)),
+        out_specs=ANY,
+        input_output_aliases={0: 0},
+        compiler_params=PARAMS,
+        cost_estimate=cost(0, 0),
+    )(value, *after)
 
 
 def copy_kernel(value_ref, *refs):
     refs[-1][...] = value_ref[...]
 
 
-def follow(value, after):
+def follow_copy(value, after):
     return pl.pallas_call(
         copy_kernel,
         out_shape=jax.ShapeDtypeStruct(value.shape, value.dtype),
@@ -79,33 +77,35 @@
     )(conn)
 
 
-def pack_kernel(entries, cuts, table_ref, *refs):
-    pieces = refs[: len(entries[0])]
-    outs = refs[len(pieces) :]
-    for partner, columns in enumerate(entries):
+def pack_kernel(lists, cap, counts, base_ref, *refs):
+    table_count, piece_count = counts
+    tables, pieces = refs[:table_count], refs[table_count : table_count + piece_count]
+    outs = refs[-len(lists) :]
+    for entries, out in zip(lists, outs):
         at = 0
-        for piece, places in zip(pieces, columns):
-            for place in places:
-                block = piece[table_ref[1, place]]
-                for cut, (start, sub) in enumerate(cuts):
-                    outs[partner * len(cuts) + cut][at] = block[start : start + sub, :]
-                at += 1
-
-
-def pack(entries, cuts, pieces, table):
-    count = len(entries[0][0]) * len(pieces)
-    size = pieces[0].shape[2]
+        for piece, table, row, owner, start, sub in entries:
+            for rank in range(cap):
+                block = pieces[piece][tables[table][row, base_ref[owner] + rank]]
+                out[at : at + sub, :] = block.T[start : start + sub, :]
+                at += sub
+
+
+def pack(lists, cap, bases, tables, pieces, after):
+    size = pieces[0].shape[1]
     outs = [
-        jax.ShapeDtypeStruct((count, sub, size), jnp.float32) for _ in entries for _, sub in cuts
+        jax.ShapeDtypeStruct(
+            (sum(cap * sub for _, _, _, _, _, sub in entries), size), jnp.float32
+        )
+        for entries in lists
     ]
     return pl.pallas_call(
-        functools.partial(pack_kernel, entries, cuts),
+        functools.partial(pack_kernel, lists, cap, (len(tables), len(pieces))),
         out_shape=outs,
-        in_specs=[SMEM] + [VMEM] * len(pieces),
+        in_specs=[SMEM] * (1 + len(tables)) + [VMEM] * len(pieces) + [ANY] * len(after),
         out_specs=[VMEM] * len(outs),
         compiler_params=PARAMS,
         cost_estimate=cost(0, 8 * sum(out.size for out in outs)),
-    )(table, *pieces)
+    )(bases, *tables, *pieces, *after)
 
 
 def smooth_kernel(plan, per_row, source_count, table_ref, *refs):
@@ -113,10 +113,9 @@
     tiles_ref, out_ref, highs, lows = refs[source_count:]
     sub, size = highs.shape[1:]
     block_count = out_ref.shape[1] // size
-    for place, source, at, start in plan:
-        block = sources[source][table_ref[1, place] if at is None else at]
-        tile = table_ref[0, place]
-        highs[tile], lows[tile] = split(block[start : start + sub, :])
+    for place, source, at in plan:
+        tile = table_ref[place]
+        highs[tile], lows[tile] = split(sources[source][at : at + sub, :])
 
     for row in range(block_count):
         span = range(row * per_row, (row + 1) * per_row)
@@ -259,31 +258,43 @@
     def swap(value, mask):
         return lax.ppermute(value, "fix", [(i, i ^ mask) for i in range(fix_count)])
 
-    own = turn(fixels, block_count)
-    beside = swap(own, 1)
-    sent = follow(columns.T, [beside])
-    partners = range(group - 2, 0, -2)
-    named = jnp.stack([sent.reshape(-1)] + [swap(sent, m).reshape(-1) for m in partners])
+    named = columns.T.reshape(-1)
     positions = jnp.arange(tile_total)
-    earlier = positions[:, None] > positions[None, :]
-    owners = named // block_count
-    same = owners[:, :, None] == owners[:, None, :]
-    ranks = jnp.sum(jnp.logical_and(same, earlier[None]).astype(jnp.int32), axis=2)
+    owners, blocks = named // block_count, named % block_count
+    earlier = jnp.logical_and(
+        owners[:, None] == owners[None, :], positions[:, None] > positions[None, :]
+    )
+    slots = owners * cap + jnp.sum(earlier.astype(jnp.int32), axis=1)
     order = jnp.arange(fix_count * cap)
-    owner = (me // group + lines - order // (group * cap)) % lines * group + (
-        (me % group) ^ (order // cap % group)
-    )
-    hits = (owners * cap + ranks)[:, None, :] == (owner * cap + order % cap)[:, None]
+    hits = slots == order[:, None]
+    request = jnp.sum(jnp.where(hits, blocks, 0), axis=1).reshape(1, -1).astype(jnp.int32)
+    line, member = me // group, me % group
+    near_first = (line + lines - np.arange(lines)) % lines * group
+    bases = ((near_first[:, None] + (member ^ np.arange(group))) * cap).reshape(-1)
+    bases = bases.astype(jnp.int32)
+    owner = jnp.repeat(bases, cap) + order % cap
     tile = positions % block_count * per_row + positions // block_count
-    codes = (tile - tile_total) * block_count + named % block_count
-    codes = jnp.sum(jnp.where(hits, codes[:, None, :], 0), axis=2).reshape(-1)
-    codes = codes + tile_total * block_count
-    table = jnp.stack([codes // block_count, codes % block_count]).astype(jnp.int32)
-
-    def places(row, k, other):
-        base = ((row * lines + k) * group + other) * cap
+    table = jnp.sum(jnp.where(slots == owner[:, None], tile - tile_total, 0), axis=1)
+    table = (table + tile_total).astype(jnp.int32)
+
+    def places(k, other):
+        base = (k * group + other) * cap
         return tuple(range(base, base + cap))
 
+    raw = fixels.reshape(block_count, size, width)
+    far_raw = {}
+    for k in range(1, lines):
+        pairs = [(i, (i + k * group) % fix_count) for i in range(fix_count)]
+        far_raw[k] = lax.ppermute(raw, "fix", pairs)
+    across_raw = {m: swap(raw, m) for m in range(4, group, 4)}
+    beside = swap(raw, 1)
+    asked = {2: (swap(request, 2), 0)}
+    both_requests = jnp.concatenate([request, asked[2][0]])
+    for m in range(4, group, 4):
+        pair = swap(both_requests, m)
+        asked[m], asked[m + 2] = (pair, 0), (pair, 1)
+
+    perm_table = follow_copy(perm_table, [asked[2][0]])
     rows = perm_table.shape[0] // subj_count
     count = nuisance.shape[0]
     shares = []
@@ -312,46 +323,52 @@
 
     tiles = split_tiles(conn_tiles.reshape(tile_total, size, size))
 
-    def exchange(pieces, k, cuts, base):
-        entries = tuple(
-            tuple(places(row, k, e) for e in range(2)) for row in range(1, len(partners) + 1)
-        )
-        packs = pack(entries, cuts, pieces, table)
-        got = [
-            [swap(packs[i * len(cuts) + c], m) for i, m in enumerate(partners)]
-            for c in range(len(cuts))
-        ]
-        plan = []
-        for e in range(2):
-            plan.extend((place, base + e, None) for place in places(0, k, e))
-            for source, m in enumerate(partners, base + 2):
-                plan.extend(
-                    (place, source, e * cap + rank)
-                    for rank, place in enumerate(places(0, k, m ^ e))
+    plans, sources = [[] for _ in subs], [[] for _ in subs]
+
+    def pick(chosen, after):
+        pieces, tables, lists = [], [], []
+        for index, (m, items, start, count) in enumerate(chosen):
+            row = asked[m][1] if m else 0
+            lists.append(
+                tuple(
+                    (len(pieces) + i, index, row, key[0] * group + key[1], start, count)
+                    for i, key in enumerate(items)
                 )
-        return got, plan
-
-    pieces = [own, beside]
-    (got,), plan = exchange(pieces, 0, ((0, width),), 0)
-    gate = got[GATE:] + [design[0], tiles]
-    whole = pieces + got
-    plans = [[(place, source, at, start) for place, source, at in plan] for start in starts]
-    sources = [list(whole) for _ in subs]
-    for k in range(1, lines):
-        pairs = [(i, (i + k * group) % fix_count) for i in range(fix_count)]
-        piece = follow(lax.ppermute(own, "fix", pairs), gate)
-        pieces = [piece, swap(piece, 1)]
-        got, plan = exchange(pieces, k, tuple(zip(starts, subs)), len(sources[0]))
-        for c, start in enumerate(starts):
-            plans[c].extend(
-                (place, source, at, start if at is None else 0) for place, source, at in plan
             )
-            sources[c].extend(pieces + got[c])
+            pieces.extend(items.values())
+            tables.append(asked[m][0] if m else request)
+        packs = pack(tuple(lists), cap, bases, tables, pieces, after)
+        got = [swap(value, m) if m else value for value, (m, *_) in zip(packs, chosen)]
+        for value, (m, items, start, count) in zip(got, chosen):
+            for c, sub in enumerate(subs):
+                if start <= starts[c] and starts[c] + sub <= start + count:
+                    for i, (k, other) in enumerate(items):
+                        for rank, place in enumerate(places(k, other ^ m)):
+                            at = (i * cap + rank) * count + starts[c] - start
+                            plans[c].append((place, len(sources[c]), at))
+                    sources[c].append(value)
+        return got
+
+    near = {(0, 0): raw, (0, 1): beside}
+    after = pick([(2, near, 0, width)], [])
+    after = after + [design[0], tiles] + [asked[m][0] for m in range(4, group, 4)]
+    arrived = {(k, 0): value for k, value in far_raw.items()}
+    arrived.update({(0, m): value for m, value in across_raw.items()})
+    arrived = {key: follow(value, after) for key, value in arrived.items()}
+    second = {(k, m ^ 1): swap(value, 1) for (k, m), value in arrived.items()}
+    everything = {**arrived, **second}
+    far = {key: value for key, value in everything.items() if key[0]}
+    others = [(m, far) for m in range(4, group, 2)]
+    sooner = pick([(2, arrived, 0, subs[0])], [])
+    later = pick([(m, items, 0, subs[0]) for m, items in [(2, second)] + others], [])
+    after = (sooner[:1] + later[:0])
+    for start, sub in list(zip(starts, subs))[1:]:
+        pick([(m, items, start, sub) for m, items in [(2, everything)] + others], after)
+    pick([(0, {**near, **arrived, **second}, 0, width)], [])
     smoothed = [
         smooth(tuple(plans[c]), table, sources[c], sub, tiles, block_count)
         for c, sub in enumerate(subs)
     ]
-
     parts = list(smoothed)
     for shift in range(1, subj_count):
         pairs = [(i, (i + shift) % subj_count) for i in range(subj_count)]

time: 67.2 us -> 61.6 us (0.917)
  waiting for transfers between devices: 30.1 us -> 23.6 us
  Pallas kernels: 7.96 us -> 10.9 us
  starting transfers between devices: 24.2 us -> 22.3 us
  other arithmetic: 2.03 us -> 0.52 us
  local copies, waits for them, and re-layouts: 2.36 us -> 3.85 us
    ppermute x1, waiting for transfers between devices: 7.49 us -> 2.42 us  [per_device(): far_raw[k] = lax.ppermute(raw, 'fix', pairs)]
    pallas_call x5 -> x8, Pallas kernels: 2.48 us -> 4.93 us  [the longest x5 4.92 us: pack(): pl.pallas_call(functools.partial(pack_kernel, lists, cap, (len(tables), l...]
    ppermute x1, starting transfers between devices: 4.1 us -> 2.59 us  [per_device(): far_raw[k] = lax.ppermute(raw, 'fix', pairs)]
    ppermute x2, waiting for transfers between devices: 5.78 us -> 4.31 us  [per_device(): parts.extend((lax.ppermute(value, 'subj', pairs) for value in smoothed))]
    ppermute x2, starting transfers between devices: 3.17 us -> 2.15 us  [per_device(): parts.extend((lax.ppermute(value, 'subj', pairs) for value in smoothed))]
    unnamed x12 -> x14, local copies, waits for them, and re-layouts: 1.94 us -> 2.84 us
    reshape x0 -> x2, local copies, waits for them, and re-layouts: none -> 0.85 us  [the longest x1 0.76 us: per_device(): named = columns.T.reshape(-1)]
    convert_element_type x1, other arithmetic: 0.78 us -> 0.01 us  [per_device(): lax.dynamic_slice_in_dim(perm_table, to * rows, rows, 0).astype(jnp.float32)]
  transfers between devices with their start and end apart: 18 -> 18, of which waited for: 10 -> 7; matrix products, arithmetic and copies ran while one was open for 4% -> 2% of each run, Pallas kernels for 8% -> 16%
where the time goes in v4:
time: 61.6 us; the launch traced here: 61.3 us
  waiting for transfers between devices  23.6 us (38%)
  starting transfers between devices  22.3 us (36%)
  Pallas kernels  10.9 us (18%)
  local copies, waits for them, and re-layouts  3.85 us (6%)
    ppermute x14, waiting for transfers between devices, swap(): return lax.ppermute(value, 'fix', [(i, i ^ mask) for i in range(fix_count)])  16.8 us
    ppermute x14, starting transfers between devices, swap(): return lax.ppermute(value, 'fix', [(i, i ^ mask) for i in range(fix_count)])  15.9 us
    pallas_call x5, Pallas kernels, pack(): pl.pallas_call(functools.partial(pack_kernel, lists, cap, (len(tables), l...  4.92 us
    ppermute x2, waiting for transfers between devices, per_device(): parts.extend((lax.ppermute(value, 'subj', pairs) for value in smoothed))  4.31 us
    unnamed x14, local copies, waits for them, and re-layouts  2.84 us
    ppermute x1, starting transfers between devices, per_device(): far_raw[k] = lax.ppermute(raw, 'fix', pairs)  2.59 us
    ppermute x1, waiting for transfers between devices, per_device(): far_raw[k] = lax.ppermute(raw, 'fix', pairs)  2.42 us
    pallas_call x2, Pallas kernels, smooth(): pl.pallas_call(functools.partial(smooth_kernel, plan, tile_total // block...  2.3 us
  transfers between devices with their start and end apart: 18, of which 7 were waited for; matrix products, arithmetic and copies ran while one was open for 2% of the time, Pallas kernels for 16%

profile of v4, /device:TPU:0, one launch (start us, length us, event | category | flops | bytes accessed | tf_op | source)
XLA Modules:
  0.0 61.3 jit_solution(5527676910390710197)
XLA Ops:
  0.0 3.0 %collective-permute-start.6 = (f32[8,128,128]{2,1,0:T(8,128)}, f32[8,128,128]{2,1,0:T(8,128)S(1)}, u32[]{:S(2)}, u32[]{:S(2)}) collective-permute-start(f32[8,128,128]{2,1,0:T(8,128)} %bitcast.4), channel_id=1, source_target_pairs={{0,8},{2,10},{4,12},{6,14},{8,0},{10,2},{12,4},{14,6},{16,24},{18,... | collective-permute-start | bytes 1572872 | tf_op jit(solution)/shard_map/ppermute | solution.py:259
  3.0 2.6 %collective-permute-start.5 = (f32[8,128,128]{2,1,0:T(8,128)}, f32[8,128,128]{2,1,0:T(8,128)S(1)}, u32[]{:S(2)}, u32[]{:S(2)}) collective-permute-start(f32[8,128,128]{2,1,0:T(8,128)} %bitcast.5), channel_id=1, source_target_pairs={{0,16},{2,18},{4,20},{6,22},{8,24},{10,26},{12,28},{14,30},{16,0},... | collective-permute-start | bytes 1572872 | tf_op jit(solution)/shard_map/ppermute | solution.py:288
  5.8 0.8 %reshape.106 = s32[32]{0:T(128)S(1)} reshape(s32[4,8]{1,0:T(4,128)} %bitcast.13) | data formatting | bytes 256 | tf_op jit(solution)/shard_map/reshape | solution.py:261
  7.1 1.6 %collective-permute-start = (s32[1,32]{1,0:T(1,128)S(1)}, s32[1,32]{1,0:T(1,128)S(1)}, u32[]{:S(2)}, u32[]{:S(2)}) collective-permute-start(s32[1,32]{1,0:T(1,128)S(1)} %bitcast.10), channel_id=1, source_target_pairs={{0,4},{2,6},{4,0},{6,2},{8,12},{10,14},{12,8},{14,10},{16,20},{18,... | collective-permute-start | bytes 392 | tf_op jit(solution)/shard_map/ppermute | solution.py:259
  8.7 1.6 %copy-done.2 = f32[8,4,128,128]{3,2,1,0:T(8,128)S(1)} copy-done((f32[8,4,128,128]{3,2,1,0:T(8,128)S(1)}, f32[8,4,128,128]{3,2,1,0:T(8,128)}, u32[]{:S(2)}) %copy-start.2) | copy-done | bytes 2097176
  10.3 0.6 shard_map.94.refs_3_.refs_5_.refs_6_
  11.2 1.6 %collective-permute-start.1 = (f32[72,128]{1,0:T(8,128)S(1)}, f32[72,128]{1,0:T(8,128)S(1)}, u32[]{:S(2)}, u32[]{:S(2)}) collective-permute-start(f32[72,128]{1,0:T(8,128)S(1)} %pad_maximum_fusion.1), channel_id=1, source_target_pairs={{0,1},{1,0},{2,3},{3,2},{4,5},{5,4},{6,7},{7,6},{8,9},{9,8},{10,11... | collective-permute-start | bytes 110600 | tf_op jit(solution)/shard_map/ppermute | solution.py:312
  12.8 1.0 %copy-done = f32[1024,128]{1,0:T(8,128)S(1)} copy-done((f32[1024,128]{1,0:T(8,128)S(1)}, f32[1024,128]{1,0:T(8,128)}, u32[]{:S(2)}) %copy-start) | copy-done | bytes 524312
  13.8 1.2 %shard_map.93 = f32[512,128]{1,0:T(8,128)S(1)} custom-call(s32[16]{0:T(128)S(1)} %mul.38.base_ref, s32[1,32]{1,0:T(1,128)S(1)} %collective-permute-done.refs_0_, f32[8,128,128]{2,1,0:T(8,128)S(1)} %bitcast.7, f32[8,128,128]{2,1,0:T(8,128)} %collective-permute-done.2.refs_2_), custom_call_target="tpu_custom_call" | custom-call | bytes 524288 | tf_op jit(solution)/shard_map/pallas_call | solution.py:101
  15.0 1.2 %collective-permute-start.3 = (f32[512,128]{1,0:T(8,128)S(1)}, f32[512,128]{1,0:T(8,128)S(1)}, u32[]{:S(2)}, u32[]{:S(2)}) collective-permute-start(f32[512,128]{1,0:T(8,128)S(1)} %shard_map.93), channel_id=1, source_target_pairs={{0,4},{2,6},{4,0},{6,2},{8,12},{10,14},{12,8},{14,10},{16,20},{18,... | collective-permute-start | bytes 786440 | tf_op jit(solution)/shard_map/ppermute | solution.py:259
  16.7 0.9 %shard_map.92 = (bf16[256,320]{1,0:T(8,128)(2,1)S(1)}, bf16[256,192]{1,0:T(8,128)(2,1)S(1)}, bf16[256,320]{1,0:T(8,128)(2,1)S(1)}, bf16[256,192]{1,0:T(8,128)(2,1)S(1)}) custom-call(f32[64,256]{1,0:T(8,128)S(1)} %slice.12.perm_ref, f32[4,256]{1,0:T(4,128)S(1)} %copy-done.4, f32[4,256]{1,0:T(4,128)S(1)} %get-tuple-element.28.nuisance_ref, ...), custom_call_target="tpu_custom_call" | custom-call | flops 2097152 | bytes 524288 | tf_op jit(solution)/shard_map/pallas_call | solution.py:184
  17.6 8.7 %collective-permute-done.4.refs_4_.refs_1_.refs_2_ = s32[2,32]{1,0:T(2,128)S(1)} collective-permute-done((s32[2,32]{1,0:T(2,128)S(1)}, s32[2,32]{1,0:T(2,128)S(1)}, u32[]{:S(2)}, u32[]{:S(2)}) %collective-permute-start.4) | collective-permute-done | bytes 288 | tf_op jit(solution)/shard_map/ppermute | solution.py:259
  26.4 2.4 %collective-permute-done.5.refs_0_ = f32[8,128,128]{2,1,0:T(8,128)S(1)} collective-permute-done((f32[8,128,128]{2,1,0:T(8,128)}, f32[8,128,128]{2,1,0:T(8,128)S(1)}, u32[]{:S(2)}, u32[]{:S(2)}) %collective-permute-start.5) | collective-permute-done | bytes 524320 | tf_op jit(solution)/shard_map/ppermute | solution.py:288
  28.8 0.7 %shard_map.97 = f32[320,128]{1,0:T(8,128)S(1)} custom-call(s32[16]{0:T(128)S(1)} %mul.38.base_ref, s32[1,32]{1,0:T(1,128)S(1)} %collective-permute-done.refs_0_, f32[8,128,128]{2,1,0:T(8,128)S(1)} %shard_map.95.refs_1_.refs_3_.refs_7_.refs_9_.refs_5_, f32[8,128,128]{2,1,0:T(8,128)S(1)} %shard_map.96.refs_2_.refs_4_), custom_call_target="tpu_custom_call" | custom-call | bytes 327680 | tf_op jit(solution)/shard_map/pallas_call | solution.py:101
  29.5 1.6 %collective-permute-start.9 = (f32[320,128]{1,0:T(8,128)S(1)}, f32[320,128]{1,0:T(8,128)S(1)}, u32[]{:S(2)}, u32[]{:S(2)}) collective-permute-start(f32[320,128]{1,0:T(8,128)S(1)} %shard_map.97), channel_id=1, source_target_pairs={{0,4},{2,6},{4,0},{6,2},{8,12},{10,14},{12,8},{14,10},{16,20},{18,... | collective-permute-start | bytes 491528 | tf_op jit(solution)/shard_map/ppermute | solution.py:259
  31.1 0.8 %shard_map.101 = (f32[320,128]{1,0:T(8,128)S(1)}, f32[320,128]{1,0:T(8,128)S(1)}, f32[320,128]{1,0:T(8,128)S(1)}) custom-call(s32[16]{0:T(128)S(1)} %mul.38.base_ref, s32[1,32]{1,0:T(1,128)S(1)} %collective-permute-done.refs_0_, s32[2,32]{1,0:T(2,128)S(1)} %collective-permute-done.4.refs_4_.refs_1_.refs_2_, ...), custom_call_target="tpu_custom_call" | custom-call | bytes 983040 | tf_op jit(solution)/shard_map/pallas_call | solution.py:101
  31.9 1.2 %collective-permute-start.14 = (f32[320,128]{1,0:T(8,128)S(1)}, f32[320,128]{1,0:T(8,128)S(1)}, u32[]{:S(2)}, u32[]{:S(2)}) collective-permute-start(f32[320,128]{1,0:T(8,128)S(1)} %get-tuple-element.22), channel_id=1, source_target_pairs={{0,4},{2,6},{4,0},{6,2},{8,12},{10,14},{12,8},{14,10},{16,20},{18,... | collective-permute-start | bytes 491528 | tf_op jit(solution)/shard_map/ppermute | solution.py:259
  33.6 1.9 %collective-permute-start.16 = (f32[320,128]{1,0:T(8,128)S(1)}, f32[320,128]{1,0:T(8,128)S(1)}, u32[]{:S(2)}, u32[]{:S(2)}) collective-permute-start(f32[320,128]{1,0:T(8,128)S(1)} %get-tuple-element.24), channel_id=1, source_target_pairs={{0,12},{2,14},{4,8},{6,10},{8,4},{10,6},{12,0},{14,2},{16,28},{18,... | collective-permute-start | bytes 491528 | tf_op jit(solution)/shard_map/ppermute | solution.py:259
  35.5 1.1 %collective-permute-done.9.refs_11_.refs_1_ = f32[320,128]{1,0:T(8,128)S(1)} collective-permute-done((f32[320,128]{1,0:T(8,128)S(1)}, f32[320,128]{1,0:T(8,128)S(1)}, u32[]{:S(2)}, u32[]{:S(2)}) %collective-permute-start.9) | collective-permute-done | bytes 163872 | tf_op jit(solution)/shard_map/ppermute | solution.py:259
  36.6 0.9 %shard_map.98 = (f32[384,128]{1,0:T(8,128)S(1)}, f32[192,128]{1,0:T(8,128)S(1)}, f32[192,128]{1,0:T(8,128)S(1)}) custom-call(s32[16]{0:T(128)S(1)} %mul.38.base_ref, s32[1,32]{1,0:T(1,128)S(1)} %collective-permute-done.refs_0_, s32[2,32]{1,0:T(2,128)S(1)} %collective-permute-done.4.refs_4_.refs_1_.refs_2_, ...), custom_call_target="tpu_custom_call" | custom-call | bytes 786432 | tf_op jit(solution)/shard_map/pallas_call | solution.py:101
  37.5 1.6 %collective-permute-start.10 = (f32[384,128]{1,0:T(8,128)S(1)}, f32[384,128]{1,0:T(8,128)S(1)}, u32[]{:S(2)}, u32[]{:S(2)}) collective-permute-start(f32[384,128]{1,0:T(8,128)S(1)} %get-tuple-element.17), channel_id=1, source_target_pairs={{0,4},{2,6},{4,0},{6,2},{8,12},{10,14},{12,8},{14,10},{16,20},{18,... | collective-permute-start | bytes 589832 | tf_op jit(solution)/shard_map/ppermute | solution.py:259
  39.0 1.3 %shard_map.99.refs_4_.refs_5_ = f32[1536,128]{1,0:T(8,128)S(1)} custom-call(s32[16]{0:T(128)S(1)} %mul.38.base_ref, s32[1,32]{1,0:T(1,128)S(1)} %bitcast.12, f32[8,128,128]{2,1,0:T(8,128)S(1)} %bitcast.8, f32[8,128,128]{2,1,0:T(8,128)} %collective-permute-done.2.refs_2_, f32[8,128,128]{2,1,0:T(8,128)S(1)} %shard_map.95.refs_1_.refs_3_.refs_7_.refs_9_.refs_5_, ...), custom_call_target="tpu_custom_call" | custom-call | bytes 1572864 | tf_op jit(solution)/shard_map/pallas_call | solution.py:101
  40.4 3.2 %collective-permute-done.14.refs_2_ = f32[320,128]{1,0:T(8,128)S(1)} collective-permute-done((f32[320,128]{1,0:T(8,128)S(1)}, f32[320,128]{1,0:T(8,128)S(1)}, u32[]{:S(2)}, u32[]{:S(2)}) %collective-permute-start.14) | collective-permute-done | bytes 163872 | tf_op jit(solution)/shard_map/ppermute | solution.py:259
  43.6 1.2 %shard_map.102.refs_3_ = f32[80,1024]{1,0:T(8,128)S(1)} custom-call(s32[32]{0:T(128)S(1)} %broadcast_add_fusion.table_ref, f32[512,128]{1,0:T(8,128)S(1)} %collective-permute-done.3.refs_1_.refs_0_, f32[320,128]{1,0:T(8,128)S(1)} %collective-permute-done.9.refs_11_.refs_1_, f32[320,128]{1,0:T(8,128)S(1)} %collective-permute-done.14.refs_2_, ...), custom_call_target="tpu_custom_call" | custom-call | flops 335544320 | bytes 3407872 | tf_op jit(solution)/shard_map/pallas_call | solution.py:139
  44.8 1.6 %collective-permute-start.17 = (f32[80,1024]{1,0:T(8,128)S(1)}, f32[80,1024]{1,0:T(8,128)S(1)}, u32[]{:S(2)}, u32[]{:S(2)}) collective-permute-start(f32[80,1024]{1,0:T(8,128)S(1)} %shard_map.102.refs_3_), channel_id=1, source_target_pairs={{0,1},{1,0},{2,3},{3,2},{4,5},{5,4},{6,7},{7,6},{8,9},{9,8},{10,11... | collective-permute-start | bytes 983048 | tf_op jit(solution)/shard_map/ppermute | solution.py:375
  46.8 2.5 %collective-permute-start.12 = (f32[192,128]{1,0:T(8,128)S(1)}, f32[192,128]{1,0:T(8,128)S(1)}, u32[]{:S(2)}, u32[]{:S(2)}) collective-permute-start(f32[192,128]{1,0:T(8,128)S(1)} %get-tuple-element.19), channel_id=1, source_target_pairs={{0,12},{2,14},{4,8},{6,10},{8,4},{10,6},{12,0},{14,2},{16,28},{18,... | collective-permute-start | bytes 294920 | tf_op jit(solution)/shard_map/ppermute | solution.py:259
  49.4 1.9 %collective-permute-done.11.refs_2_ = f32[192,128]{1,0:T(8,128)S(1)} collective-permute-done((f32[192,128]{1,0:T(8,128)S(1)}, f32[192,128]{1,0:T(8,128)S(1)}, u32[]{:S(2)}, u32[]{:S(2)}) %collective-permute-start.11) | collective-permute-done | bytes 98336 | tf_op jit(solution)/shard_map/ppermute | solution.py:259
  51.2 2.0 %collective-permute-done.12.refs_3_ = f32[192,128]{1,0:T(8,128)S(1)} collective-permute-done((f32[192,128]{1,0:T(8,128)S(1)}, f32[192,128]{1,0:T(8,128)S(1)}, u32[]{:S(2)}, u32[]{:S(2)}) %collective-permute-start.12) | collective-permute-done | bytes 98336 | tf_op jit(solution)/shard_map/ppermute | solution.py:259
  53.2 1.1 %shard_map.100.refs_4_ = f32[48,1024]{1,0:T(8,128)S(1)} custom-call(s32[32]{0:T(128)S(1)} %broadcast_add_fusion.table_ref, f32[512,128]{1,0:T(8,128)S(1)} %collective-permute-done.3.refs_1_.refs_0_, f32[384,128]{1,0:T(8,128)S(1)} %collective-permute-done.10.refs_1_, f32[192,128]{1,0:T(8,128)S(1)} %collective-permute-done.11.refs_2_, ...), custom_call_target="tpu_custom_call" | custom-call | flops 201326592 | bytes 2883584 | tf_op jit(solution)/shard_map/pallas_call | solution.py:139
  54.9 0.8 %shard_map.103.refs_2_ = f32[256,1024]{1,0:T(8,128)S(1)} custom-call(bf16[256,320]{1,0:T(8,128)(2,1)S(1)} %get-tuple-element.16.refs_2_.refs_0_, bf16[256,192]{1,0:T(8,128)(2,1)S(1)} %get-tuple-element.20.refs_1_, bf16[256,320]{1,0:T(8,128)(2,1)S(1)} %get-tuple-element.21.refs_2_, f32[80,1024]{1,0:T(8,128)S(1)} %shard_map.102.refs_3_, ...), custom_call_target="tpu_custom_call" | custom-call | flops 436207616 | bytes 2097152 | tf_op jit(solution)/shard_map/pallas_call | solution.py:230
  55.7 4.3 %collective-permute-done.13.refs_1_ = f32[48,1024]{1,0:T(8,128)S(1)} collective-permute-done((f32[48,1024]{1,0:T(8,128)S(1)}, f32[48,1024]{1,0:T(8,128)S(1)}, u32[]{:S(2)}, u32[]{:S(2)}) %collective-permute-start.13) | collective-permute-done | bytes 196640 | tf_op jit(solution)/shard_map/ppermute | solution.py:375
  60.0 1.2 %shard_map.104 = f32[256,1024]{1,0:T(8,128)} custom-call(bf16[256,192]{1,0:T(8,128)(2,1)S(1)} %get-tuple-element.15.refs_0_, f32[48,1024]{1,0:T(8,128)S(1)} %collective-permute-done.13.refs_1_, f32[256,1024]{1,0:T(8,128)S(1)} %shard_map.103.refs_2_), custom_call_target="tpu_custom_call" | custom-call | flops 100663296 | bytes 2097152 | tf_op jit(solution)/shard_map/pallas_call | solution.py:230
  (51 shorter events, 3.0 us)
Async XLA Ops:
  0.0 26.3 %collective-permute-start.6 = (f32[8,128,128]{2,1,0:T(8,128)}, f32[8,128,128]{2,1,0:T(8,128)S(1)}, u32[]{:S(2)}, u32[]{:S(2)}) collective-permute-start(f32[8,128,128]{2,1,0:T(8,128)} %bitcast.4), channel_id=1, source_target_pairs={{0,8},{2,10},{4,12},{6,14},{8,0},{10,2},{12,4},{14,6},{16,24},{18,... | collective-permute-start | bytes 1572872 | tf_op jit(solution)/shard_map/ppermute | solution.py:259
  3.0 25.8 %collective-permute-start.5 = (f32[8,128,128]{2,1,0:T(8,128)}, f32[8,128,128]{2,1,0:T(8,128)S(1)}, u32[]{:S(2)}, u32[]{:S(2)}) collective-permute-start(f32[8,128,128]{2,1,0:T(8,128)} %bitcast.5), channel_id=1, source_target_pairs={{0,16},{2,18},{4,20},{6,22},{8,24},{10,26},{12,28},{14,30},{16,0},... | collective-permute-start | bytes 1572872 | tf_op jit(solution)/shard_map/ppermute | solution.py:288
  5.6 7.1 %collective-permute-start.2 = (f32[8,128,128]{2,1,0:T(8,128)}, f32[8,128,128]{2,1,0:T(8,128)}, u32[]{:S(2)}, u32[]{:S(2)}) collective-permute-start(f32[8,128,128]{2,1,0:T(8,128)} %bitcast.6), channel_id=1, source_target_pairs={{0,2},{2,0},{4,6},{6,4},{8,10},{10,8},{12,14},{14,12},{16,18},{18,... | collective-permute-start | bytes 1572872 | tf_op jit(solution)/shard_map/ppermute | solution.py:259
  7.1 3.8 %collective-permute-start = (s32[1,32]{1,0:T(1,128)S(1)}, s32[1,32]{1,0:T(1,128)S(1)}, u32[]{:S(2)}, u32[]{:S(2)}) collective-permute-start(s32[1,32]{1,0:T(1,128)S(1)} %bitcast.10), channel_id=1, source_target_pairs={{0,4},{2,6},{4,0},{6,2},{8,12},{10,14},{12,8},{14,10},{16,20},{18,... | collective-permute-start | bytes 392 | tf_op jit(solution)/shard_map/ppermute | solution.py:259
  8.7 1.6 %copy-start.2 = (f32[8,4,128,128]{3,2,1,0:T(8,128)S(1)}, f32[8,4,128,128]{3,2,1,0:T(8,128)}, u32[]{:S(2)}) copy-start(f32[8,4,128,128]{3,2,1,0:T(8,128)} %param.10) | copy-start | bytes 6291460
  10.3 0.8 %copy-start.3 = (s32[128,128]{1,0:T(8,128)S(1)}, s32[128,128]{1,0:T(8,128)}, u32[]{:S(2)}) copy-start(s32[128,128]{1,0:T(8,128)} %value_ref.1) | copy-start | bytes 196612
  10.3 0.9 %copy-start.5 = (f32[4,128]{1,0:T(4,128)S(1)}, f32[4,128]{1,0:T(4,128)}, u32[]{:S(2)}) copy-start(f32[4,128]{1,0:T(4,128)} %param.13) | copy-start | bytes 6148
  10.3 0.9 %copy-start.6 = (f32[4,128]{1,0:T(4,128)S(1)}, f32[4,128]{1,0:T(4,128)}, u32[]{:S(2)}) copy-start(f32[4,128]{1,0:T(4,128)} %param.12) | copy-start | bytes 6148
  10.3 6.4 %copy-start.4 = (f32[4,256]{1,0:T(4,128)S(1)}, f32[4,256]{1,0:T(4,128)}, u32[]{:S(2)}) copy-start(f32[4,256]{1,0:T(4,128)} %contrast_ref.1) | copy-start | bytes 12292
  11.2 5.5 %collective-permute-start.1 = (f32[72,128]{1,0:T(8,128)S(1)}, f32[72,128]{1,0:T(8,128)S(1)}, u32[]{:S(2)}, u32[]{:S(2)}) collective-permute-start(f32[72,128]{1,0:T(8,128)S(1)} %pad_maximum_fusion.1), channel_id=1, source_target_pairs={{0,1},{1,0},{2,3},{3,2},{4,5},{5,4},{6,7},{7,6},{8,9},{9,8},{10,11... | collective-permute-start | bytes 110600 | tf_op jit(solution)/shard_map/ppermute | solution.py:312
  12.8 1.0 %copy-start = (f32[1024,128]{1,0:T(8,128)S(1)}, f32[1024,128]{1,0:T(8,128)}, u32[]{:S(2)}) copy-start(f32[1024,128]{1,0:T(8,128)} %param.9) | copy-start | bytes 1572868
  15.0 11.3 %collective-permute-start.3 = (f32[512,128]{1,0:T(8,128)S(1)}, f32[512,128]{1,0:T(8,128)S(1)}, u32[]{:S(2)}, u32[]{:S(2)}) collective-permute-start(f32[512,128]{1,0:T(8,128)S(1)} %shard_map.93), channel_id=1, source_target_pairs={{0,4},{2,6},{4,0},{6,2},{8,12},{10,14},{12,8},{14,10},{16,20},{18,... | collective-permute-start | bytes 786440 | tf_op jit(solution)/shard_map/ppermute | solution.py:259
  16.2 10.1 %collective-permute-start.4 = (s32[2,32]{1,0:T(2,128)S(1)}, s32[2,32]{1,0:T(2,128)S(1)}, u32[]{:S(2)}, u32[]{:S(2)}) collective-permute-start(s32[2,32]{1,0:T(2,128)S(1)} %pad_add_fusion), channel_id=1, source_target_pairs={{0,8},{2,10},{4,12},{6,14},{8,0},{10,2},{12,4},{14,6},{16,24},{18,... | collective-permute-start | bytes 776 | tf_op jit(solution)/shard_map/ppermute | solution.py:259
  26.3 4.7 %collective-permute-start.8 = (f32[8,128,128]{2,1,0:T(8,128)S(1)}, f32[8,128,128]{2,1,0:T(8,128)S(1)}, u32[]{:S(2)}, u32[]{:S(2)}) collective-permute-start(f32[8,128,128]{2,1,0:T(8,128)S(1)} %shard_map.96.refs_2_.refs_4_), channel_id=1, source_target_pairs={{0,2},{2,0},{4,6},{6,4},{8,10},{10,8},{12,14},{14,12},{16,18},{18,... | collective-permute-start | bytes 1572872 | tf_op jit(solution)/shard_map/ppermute | solution.py:259
  28.8 2.2 %collective-permute-start.7 = (f32[8,128,128]{2,1,0:T(8,128)S(1)}, f32[8,128,128]{2,1,0:T(8,128)S(1)}, u32[]{:S(2)}, u32[]{:S(2)}) collective-permute-start(f32[8,128,128]{2,1,0:T(8,128)S(1)} %shard_map.95.refs_1_.refs_3_.refs_7_.refs_9_.refs_5_), channel_id=1, source_target_pairs={{0,2},{2,0},{4,6},{6,4},{8,10},{10,8},{12,14},{14,12},{16,18},{18,... | collective-permute-start | bytes 1572872 | tf_op jit(solution)/shard_map/ppermute | solution.py:259
  29.5 7.1 %collective-permute-start.9 = (f32[320,128]{1,0:T(8,128)S(1)}, f32[320,128]{1,0:T(8,128)S(1)}, u32[]{:S(2)}, u32[]{:S(2)}) collective-permute-start(f32[320,128]{1,0:T(8,128)S(1)} %shard_map.97), channel_id=1, source_target_pairs={{0,4},{2,6},{4,0},{6,2},{8,12},{10,14},{12,8},{14,10},{16,20},{18,... | collective-permute-start | bytes 491528 | tf_op jit(solution)/shard_map/ppermute | solution.py:259
  31.9 11.7 %collective-permute-start.14 = (f32[320,128]{1,0:T(8,128)S(1)}, f32[320,128]{1,0:T(8,128)S(1)}, u32[]{:S(2)}, u32[]{:S(2)}) collective-permute-start(f32[320,128]{1,0:T(8,128)S(1)} %get-tuple-element.22), channel_id=1, source_target_pairs={{0,4},{2,6},{4,0},{6,2},{8,12},{10,14},{12,8},{14,10},{16,20},{18,... | collective-permute-start | bytes 491528 | tf_op jit(solution)/shard_map/ppermute | solution.py:259
  33.1 10.4 %collective-permute-start.15 = (f32[320,128]{1,0:T(8,128)S(1)}, f32[320,128]{1,0:T(8,128)S(1)}, u32[]{:S(2)}, u32[]{:S(2)}) collective-permute-start(f32[320,128]{1,0:T(8,128)S(1)} %get-tuple-element.23), channel_id=1, source_target_pairs={{0,8},{2,10},{4,12},{6,14},{8,0},{10,2},{12,4},{14,6},{16,24},{18,... | collective-permute-start | bytes 491528 | tf_op jit(solution)/shard_map/ppermute | solution.py:259
  33.6 5.5 %copy-start.1 = (f32[1024,128]{1,0:T(8,128)S(1)}, f32[1024,128]{1,0:T(8,128)}, u32[]{:S(2)}) copy-start(f32[1024,128]{1,0:T(8,128)} %param.9) | copy-start | bytes 1572868
  33.6 10.0 %collective-permute-start.16 = (f32[320,128]{1,0:T(8,128)S(1)}, f32[320,128]{1,0:T(8,128)S(1)}, u32[]{:S(2)}, u32[]{:S(2)}) collective-permute-start(f32[320,128]{1,0:T(8,128)S(1)} %get-tuple-element.24), channel_id=1, source_target_pairs={{0,12},{2,14},{4,8},{6,10},{8,4},{10,6},{12,0},{14,2},{16,28},{18,... | collective-permute-start | bytes 491528 | tf_op jit(solution)/shard_map/ppermute | solution.py:259
  37.5 15.7 %collective-permute-start.10 = (f32[384,128]{1,0:T(8,128)S(1)}, f32[384,128]{1,0:T(8,128)S(1)}, u32[]{:S(2)}, u32[]{:S(2)}) collective-permute-start(f32[384,128]{1,0:T(8,128)S(1)} %get-tuple-element.17), channel_id=1, source_target_pairs={{0,4},{2,6},{4,0},{6,2},{8,12},{10,14},{12,8},{14,10},{16,20},{18,... | collective-permute-start | bytes 589832 | tf_op jit(solution)/shard_map/ppermute | solution.py:259
  44.8 10.1 %collective-permute-start.17 = (f32[80,1024]{1,0:T(8,128)S(1)}, f32[80,1024]{1,0:T(8,128)S(1)}, u32[]{:S(2)}, u32[]{:S(2)}) collective-permute-start(f32[80,1024]{1,0:T(8,128)S(1)} %shard_map.102.refs_3_), channel_id=1, source_target_pairs={{0,1},{1,0},{2,3},{3,2},{4,5},{5,4},{6,7},{7,6},{8,9},{9,8},{10,11... | collective-permute-start | bytes 983048 | tf_op jit(solution)/shard_map/ppermute | solution.py:375
  46.4 4.9 %collective-permute-start.11 = (f32[192,128]{1,0:T(8,128)S(1)}, f32[192,128]{1,0:T(8,128)S(1)}, u32[]{:S(2)}, u32[]{:S(2)}) collective-permute-start(f32[192,128]{1,0:T(8,128)S(1)} %get-tuple-element.18), channel_id=1, source_target_pairs={{0,8},{2,10},{4,12},{6,14},{8,0},{10,2},{12,4},{14,6},{16,24},{18,... | collective-permute-start | bytes 294920 | tf_op jit(solution)/shard_map/ppermute | solution.py:259
  46.8 6.4 %collective-permute-start.12 = (f32[192,128]{1,0:T(8,128)S(1)}, f32[192,128]{1,0:T(8,128)S(1)}, u32[]{:S(2)}, u32[]{:S(2)}) collective-permute-start(f32[192,128]{1,0:T(8,128)S(1)} %get-tuple-element.19), channel_id=1, source_target_pairs={{0,12},{2,14},{4,8},{6,10},{8,4},{10,6},{12,0},{14,2},{16,28},{18,... | collective-permute-start | bytes 294920 | tf_op jit(solution)/shard_map/ppermute | solution.py:259
  54.3 5.7 %collective-permute-start.13 = (f32[48,1024]{1,0:T(8,128)S(1)}, f32[48,1024]{1,0:T(8,128)S(1)}, u32[]{:S(2)}, u32[]{:S(2)}) collective-permute-start(f32[48,1024]{1,0:T(8,128)S(1)} %shard_map.100.refs_4_), channel_id=1, source_target_pairs={{0,1},{1,0},{2,3},{3,2},{4,5},{5,4},{6,7},{7,6},{8,9},{9,8},{10,11... | collective-permute-start | bytes 589832 | tf_op jit(solution)/shard_map/ppermute | solution.py:375

commit v5 on v4

--- a/solution.py
+++ b/solution.py
@@ -282,11 +282,11 @@
         return tuple(range(base, base + cap))
 
     raw = fixels.reshape(block_count, size, width)
+    across_raw = {m: swap(raw, m) for m in range(4, group, 4)}
     far_raw = {}
     for k in range(1, lines):
         pairs = [(i, (i + k * group) % fix_count) for i in range(fix_count)]
         far_raw[k] = lax.ppermute(raw, "fix", pairs)
-    across_raw = {m: swap(raw, m) for m in range(4, group, 4)}
     beside = swap(raw, 1)
     asked = {2: (swap(request, 2), 0)}
     both_requests = jnp.concatenate([request, asked[2][0]])
@@ -352,18 +352,18 @@
     near = {(0, 0): raw, (0, 1): beside}
     after = pick([(2, near, 0, width)], [])
     after = after + [design[0], tiles] + [asked[m][0] for m in range(4, group, 4)]
-    arrived = {(k, 0): value for k, value in far_raw.items()}
-    arrived.update({(0, m): value for m, value in across_raw.items()})
+    arrived = {(0, m): value for m, value in across_raw.items()}
+    arrived.update({(k, 0): value for k, value in far_raw.items()})
     arrived = {key: follow(value, after) for key, value in arrived.items()}
     second = {(k, m ^ 1): swap(value, 1) for (k, m), value in arrived.items()}
     everything = {**arrived, **second}
     far = {key: value for key, value in everything.items() if key[0]}
     others = [(m, far) for m in range(4, group, 2)]
+    pick([(m, far, 0, subs[0]) for m in (6, 4)], [])
     sooner = pick([(2, arrived, 0, subs[0])], [])
-    later = pick([(m, items, 0, subs[0]) for m, items in [(2, second)] + others], [])
-    after = (sooner[:1] + later[:0])
+    pick([(2, second, 0, subs[0])], [])
     for start, sub in list(zip(starts, subs))[1:]:
-        pick([(m, items, start, sub) for m, items in [(2, everything)] + others], after)
+        pick([(m, items, start, sub) for m, items in [(2, everything)] + others], [])
     pick([(0, {**near, **arrived, **second}, 0, width)], [])
     smoothed = [
         smooth(tuple(plans[c]), table, sources[c], sub, tiles, block_count)

time: 61.6 us -> 61.4 us (level)
  waiting for transfers between devices: 23.6 us -> 22.2 us
    ppermute x1, waiting for transfers between devices: 2.42 us -> 0.01 us  [per_device(): far_raw[k] = lax.ppermute(raw, 'fix', pairs)]
    ppermute x1, starting transfers between devices: 2.59 us -> 4.04 us  [per_device(): far_raw[k] = lax.ppermute(raw, 'fix', pairs)]
    ppermute x14, waiting for transfers between devices: 16.8 us -> 17.9 us  [swap(): return lax.ppermute(value, 'fix', [(i, i ^ mask) for i in range(fix_count)])]
    ppermute x14, starting transfers between devices: 15.9 us -> 15 us  [swap(): return lax.ppermute(value, 'fix', [(i, i ^ mask) for i in range(fix_count)])]
    pallas_call x5 -> x6, Pallas kernels: 4.92 us -> 5.51 us  [pack(): pl.pallas_call(functools.partial(pack_kernel, lists, cap, (len(tables), l...]
  transfers between devices with their start and end apart: 18 -> 18, of which waited for: 7 -> 5; matrix products, arithmetic and copies ran while one was open for 2% -> 3% of each run, Pallas kernels for 16% -> 17%
where the time goes in v5:
time: 61.4 us; the launch traced here: 61 us
  starting transfers between devices  22.8 us (37%)
  waiting for transfers between devices  22.2 us (36%)
  Pallas kernels  11.4 us (19%)
  local copies, waits for them, and re-layouts  3.85 us (6%)
    ppermute x14, waiting for transfers between devices, swap(): return lax.ppermute(value, 'fix', [(i, i ^ mask) for i in range(fix_count)])  17.9 us
    ppermute x14, starting transfers between devices, swap(): return lax.ppermute(value, 'fix', [(i, i ^ mask) for i in range(fix_count)])  15 us
    pallas_call x6, Pallas kernels, pack(): pl.pallas_call(functools.partial(pack_kernel, lists, cap, (len(tables), l...  5.51 us
    ppermute x2, waiting for transfers between devices, per_device(): parts.extend((lax.ppermute(value, 'subj', pairs) for value in smoothed))  4.33 us
    ppermute x1, starting transfers between devices, per_device(): far_raw[k] = lax.ppermute(raw, 'fix', pairs)  4.04 us
    unnamed x14, local copies, waits for them, and re-layouts  2.84 us
    pallas_call x2, Pallas kernels, smooth(): pl.pallas_call(functools.partial(smooth_kernel, plan, tile_total // block...  2.29 us
    ppermute x2, starting transfers between devices, per_device(): parts.extend((lax.ppermute(value, 'subj', pairs) for value in smoothed))  2.21 us
  transfers between devices with their start and end apart: 18, of which 5 were waited for; matrix products, arithmetic and copies ran while one was open for 3% of the time, Pallas kernels for 17%

profile of v5, /device:TPU:0, one launch (start us, length us, event | category | flops | bytes accessed | tf_op | source)
XLA Modules:
  0.0 61.0 jit_solution(555644344454544574)
XLA Ops:
  0.0 4.0 %collective-permute-start.6 = (f32[8,128,128]{2,1,0:T(8,128)}, f32[8,128,128]{2,1,0:T(8,128)S(1)}, u32[]{:S(2)}, u32[]{:S(2)}) collective-permute-start(f32[8,128,128]{2,1,0:T(8,128)} %bitcast.4), channel_id=1, source_target_pairs={{0,16},{2,18},{4,20},{6,22},{8,24},{10,26},{12,28},{14,30},{16,0},... | collective-permute-start | bytes 1572872 | tf_op jit(solution)/shard_map/ppermute | solution.py:289
  4.0 1.6 %collective-permute-start.5 = (f32[8,128,128]{2,1,0:T(8,128)}, f32[8,128,128]{2,1,0:T(8,128)S(1)}, u32[]{:S(2)}, u32[]{:S(2)}) collective-permute-start(f32[8,128,128]{2,1,0:T(8,128)} %bitcast.5), channel_id=1, source_target_pairs={{0,8},{2,10},{4,12},{6,14},{8,0},{10,2},{12,4},{14,6},{16,24},{18,... | collective-permute-start | bytes 1572872 | tf_op jit(solution)/shard_map/ppermute | solution.py:259
  5.8 0.8 %reshape.106 = s32[32]{0:T(128)S(1)} reshape(s32[4,8]{1,0:T(4,128)} %bitcast.13) | data formatting | bytes 256 | tf_op jit(solution)/shard_map/reshape | solution.py:261
  7.1 1.6 %collective-permute-start = (s32[1,32]{1,0:T(1,128)S(1)}, s32[1,32]{1,0:T(1,128)S(1)}, u32[]{:S(2)}, u32[]{:S(2)}) collective-permute-start(s32[1,32]{1,0:T(1,128)S(1)} %bitcast.10), channel_id=1, source_target_pairs={{0,4},{2,6},{4,0},{6,2},{8,12},{10,14},{12,8},{14,10},{16,20},{18,... | collective-permute-start | bytes 392 | tf_op jit(solution)/shard_map/ppermute | solution.py:259
  8.7 1.6 %copy-done.2 = f32[8,4,128,128]{3,2,1,0:T(8,128)S(1)} copy-done((f32[8,4,128,128]{3,2,1,0:T(8,128)S(1)}, f32[8,4,128,128]{3,2,1,0:T(8,128)}, u32[]{:S(2)}) %copy-start.2) | copy-done | bytes 2097176
  10.3 0.6 shard_map.94.refs_3_.refs_5_.refs_6_
  11.2 1.6 %collective-permute-start.1 = (f32[72,128]{1,0:T(8,128)S(1)}, f32[72,128]{1,0:T(8,128)S(1)}, u32[]{:S(2)}, u32[]{:S(2)}) collective-permute-start(f32[72,128]{1,0:T(8,128)S(1)} %pad_maximum_fusion.1), channel_id=1, source_target_pairs={{0,1},{1,0},{2,3},{3,2},{4,5},{5,4},{6,7},{7,6},{8,9},{9,8},{10,11... | collective-permute-start | bytes 110600 | tf_op jit(solution)/shard_map/ppermute | solution.py:312
  12.8 1.0 %copy-done = f32[1024,128]{1,0:T(8,128)S(1)} copy-done((f32[1024,128]{1,0:T(8,128)S(1)}, f32[1024,128]{1,0:T(8,128)}, u32[]{:S(2)}) %copy-start) | copy-done | bytes 524312
  13.8 1.2 %shard_map.93 = f32[512,128]{1,0:T(8,128)S(1)} custom-call(s32[16]{0:T(128)S(1)} %mul.38.base_ref, s32[1,32]{1,0:T(1,128)S(1)} %collective-permute-done.refs_0_, f32[8,128,128]{2,1,0:T(8,128)S(1)} %bitcast.7, f32[8,128,128]{2,1,0:T(8,128)} %collective-permute-done.2.refs_2_), custom_call_target="tpu_custom_call" | custom-call | bytes 524288 | tf_op jit(solution)/shard_map/pallas_call | solution.py:101
  15.0 1.2 %collective-permute-start.3 = (f32[512,128]{1,0:T(8,128)S(1)}, f32[512,128]{1,0:T(8,128)S(1)}, u32[]{:S(2)}, u32[]{:S(2)}) collective-permute-start(f32[512,128]{1,0:T(8,128)S(1)} %shard_map.93), channel_id=1, source_target_pairs={{0,4},{2,6},{4,0},{6,2},{8,12},{10,14},{12,8},{14,10},{16,20},{18,... | collective-permute-start | bytes 786440 | tf_op jit(solution)/shard_map/ppermute | solution.py:259
  16.7 0.9 %shard_map.92 = (bf16[256,320]{1,0:T(8,128)(2,1)S(1)}, bf16[256,192]{1,0:T(8,128)(2,1)S(1)}, bf16[256,320]{1,0:T(8,128)(2,1)S(1)}, bf16[256,192]{1,0:T(8,128)(2,1)S(1)}) custom-call(f32[64,256]{1,0:T(8,128)S(1)} %slice.12.perm_ref, f32[4,256]{1,0:T(4,128)S(1)} %copy-done.4, f32[4,256]{1,0:T(4,128)S(1)} %get-tuple-element.26.nuisance_ref, ...), custom_call_target="tpu_custom_call" | custom-call | flops 2097152 | bytes 524288 | tf_op jit(solution)/shard_map/pallas_call | solution.py:184
  17.6 10.1 %collective-permute-done.4.refs_4_.refs_1_.refs_2_.refs_0_ = s32[2,32]{1,0:T(2,128)S(1)} collective-permute-done((s32[2,32]{1,0:T(2,128)S(1)}, s32[2,32]{1,0:T(2,128)S(1)}, u32[]{:S(2)}, u32[]{:S(2)}) %collective-permute-start.4) | collective-permute-done | bytes 288 | tf_op jit(solution)/shard_map/ppermute | solution.py:259
  28.3 0.7 %shard_map.101 = f32[320,128]{1,0:T(8,128)S(1)} custom-call(s32[16]{0:T(128)S(1)} %mul.38.base_ref, s32[1,32]{1,0:T(1,128)S(1)} %collective-permute-done.refs_0_, f32[8,128,128]{2,1,0:T(8,128)S(1)} %shard_map.95.refs_3_.refs_1_, f32[8,128,128]{2,1,0:T(8,128)S(1)} %shard_map.96.refs_4_.refs_7_.refs_9_.refs_2_), custom_call_target="tpu_custom_call" | custom-call | bytes 327680 | tf_op jit(solution)/shard_map/pallas_call | solution.py:101
  29.0 1.6 %collective-permute-start.15 = (f32[320,128]{1,0:T(8,128)S(1)}, f32[320,128]{1,0:T(8,128)S(1)}, u32[]{:S(2)}, u32[]{:S(2)}) collective-permute-start(f32[320,128]{1,0:T(8,128)S(1)} %shard_map.101), channel_id=1, source_target_pairs={{0,4},{2,6},{4,0},{6,2},{8,12},{10,14},{12,8},{14,10},{16,20},{18,... | collective-permute-start | bytes 491528 | tf_op jit(solution)/shard_map/ppermute | solution.py:259
  30.6 0.7 %shard_map.102 = f32[320,128]{1,0:T(8,128)S(1)} custom-call(s32[16]{0:T(128)S(1)} %mul.38.base_ref, s32[1,32]{1,0:T(1,128)S(1)} %collective-permute-done.refs_0_, f32[8,128,128]{2,1,0:T(8,128)S(1)} %collective-permute-done.7.refs_5_.refs_1_, f32[8,128,128]{2,1,0:T(8,128)S(1)} %collective-permute-done.8.refs_6_.refs_8_.refs_10_.refs_3_.refs_5_.refs_2_), custom_call_target="tpu_custom_call" | custom-call | bytes 327680 | tf_op jit(solution)/shard_map/pallas_call | solution.py:101
  31.3 1.5 %collective-permute-start.16 = (f32[320,128]{1,0:T(8,128)S(1)}, f32[320,128]{1,0:T(8,128)S(1)}, u32[]{:S(2)}, u32[]{:S(2)}) collective-permute-start(f32[320,128]{1,0:T(8,128)S(1)} %shard_map.102), channel_id=1, source_target_pairs={{0,4},{2,6},{4,0},{6,2},{8,12},{10,14},{12,8},{14,10},{16,20},{18,... | collective-permute-start | bytes 491528 | tf_op jit(solution)/shard_map/ppermute | solution.py:259
  32.8 0.8 %shard_map.100 = (f32[320,128]{1,0:T(8,128)S(1)}, f32[320,128]{1,0:T(8,128)S(1)}) custom-call(s32[16]{0:T(128)S(1)} %mul.38.base_ref, s32[2,32]{1,0:T(2,128)S(1)} %collective-permute-done.4.refs_4_.refs_1_.refs_2_.refs_0_, s32[2,32]{1,0:T(2,128)S(1)} %collective-permute-done.4.refs_4_.refs_1_.refs_2_.refs_0_, ...), custom_call_target="tpu_custom_call" | custom-call | bytes 655360 | tf_op jit(solution)/shard_map/pallas_call | solution.py:101
  33.5 1.6 %collective-permute-start.13 = (f32[320,128]{1,0:T(8,128)S(1)}, f32[320,128]{1,0:T(8,128)S(1)}, u32[]{:S(2)}, u32[]{:S(2)}) collective-permute-start(f32[320,128]{1,0:T(8,128)S(1)} %get-tuple-element.21), channel_id=1, source_target_pairs={{0,12},{2,14},{4,8},{6,10},{8,4},{10,6},{12,0},{14,2},{16,28},{18,... | collective-permute-start | bytes 491528 | tf_op jit(solution)/shard_map/ppermute | solution.py:259
  35.7 0.9 %shard_map.97 = (f32[384,128]{1,0:T(8,128)S(1)}, f32[192,128]{1,0:T(8,128)S(1)}, f32[192,128]{1,0:T(8,128)S(1)}) custom-call(s32[16]{0:T(128)S(1)} %mul.38.base_ref, s32[1,32]{1,0:T(1,128)S(1)} %collective-permute-done.refs_0_, s32[2,32]{1,0:T(2,128)S(1)} %collective-permute-done.4.refs_4_.refs_1_.refs_2_.refs_0_, ...), custom_call_target="tpu_custom_call" | custom-call | bytes 786432 | tf_op jit(solution)/shard_map/pallas_call | solution.py:101
  36.6 1.5 %collective-permute-start.9 = (f32[384,128]{1,0:T(8,128)S(1)}, f32[384,128]{1,0:T(8,128)S(1)}, u32[]{:S(2)}, u32[]{:S(2)}) collective-permute-start(f32[384,128]{1,0:T(8,128)S(1)} %get-tuple-element.16), channel_id=1, source_target_pairs={{0,4},{2,6},{4,0},{6,2},{8,12},{10,14},{12,8},{14,10},{16,20},{18,... | collective-permute-start | bytes 589832 | tf_op jit(solution)/shard_map/ppermute | solution.py:259
  38.1 1.3 %shard_map.98.refs_4_.refs_5_ = f32[1536,128]{1,0:T(8,128)S(1)} custom-call(s32[16]{0:T(128)S(1)} %mul.38.base_ref, s32[1,32]{1,0:T(1,128)S(1)} %bitcast.12, f32[8,128,128]{2,1,0:T(8,128)S(1)} %bitcast.8, f32[8,128,128]{2,1,0:T(8,128)} %collective-permute-done.2.refs_2_, f32[8,128,128]{2,1,0:T(8,128)S(1)} %shard_map.95.refs_3_.refs_1_, ...), custom_call_target="tpu_custom_call" | custom-call | bytes 1572864 | tf_op jit(solution)/shard_map/pallas_call | solution.py:101
  39.4 3.7 %collective-permute-done.16.refs_4_ = f32[320,128]{1,0:T(8,128)S(1)} collective-permute-done((f32[320,128]{1,0:T(8,128)S(1)}, f32[320,128]{1,0:T(8,128)S(1)}, u32[]{:S(2)}, u32[]{:S(2)}) %collective-permute-start.16) | collective-permute-done | bytes 163872 | tf_op jit(solution)/shard_map/ppermute | solution.py:259
  43.2 1.2 %shard_map.103.refs_3_ = f32[80,1024]{1,0:T(8,128)S(1)} custom-call(s32[32]{0:T(128)S(1)} %broadcast_add_fusion.table_ref, f32[512,128]{1,0:T(8,128)S(1)} %collective-permute-done.3.refs_1_.refs_0_, f32[320,128]{1,0:T(8,128)S(1)} %collective-permute-done.13.refs_1_, f32[320,128]{1,0:T(8,128)S(1)} %collective-permute-done.14.refs_2_, ...), custom_call_target="tpu_custom_call" | custom-call | flops 335544320 | bytes 3407872 | tf_op jit(solution)/shard_map/pallas_call | solution.py:139
  44.4 1.6 %collective-permute-start.17 = (f32[80,1024]{1,0:T(8,128)S(1)}, f32[80,1024]{1,0:T(8,128)S(1)}, u32[]{:S(2)}, u32[]{:S(2)}) collective-permute-start(f32[80,1024]{1,0:T(8,128)S(1)} %shard_map.103.refs_3_), channel_id=1, source_target_pairs={{0,1},{1,0},{2,3},{3,2},{4,5},{5,4},{6,7},{7,6},{8,9},{9,8},{10,11... | collective-permute-start | bytes 983048 | tf_op jit(solution)/shard_map/ppermute | solution.py:375
  46.0 1.4 %collective-permute-start.10 = (f32[192,128]{1,0:T(8,128)S(1)}, f32[192,128]{1,0:T(8,128)S(1)}, u32[]{:S(2)}, u32[]{:S(2)}) collective-permute-start(f32[192,128]{1,0:T(8,128)S(1)} %get-tuple-element.17), channel_id=1, source_target_pairs={{0,8},{2,10},{4,12},{6,14},{8,0},{10,2},{12,4},{14,6},{16,24},{18,... | collective-permute-start | bytes 294920 | tf_op jit(solution)/shard_map/ppermute | solution.py:259
  47.5 1.5 %collective-permute-start.11 = (f32[192,128]{1,0:T(8,128)S(1)}, f32[192,128]{1,0:T(8,128)S(1)}, u32[]{:S(2)}, u32[]{:S(2)}) collective-permute-start(f32[192,128]{1,0:T(8,128)S(1)} %get-tuple-element.18), channel_id=1, source_target_pairs={{0,12},{2,14},{4,8},{6,10},{8,4},{10,6},{12,0},{14,2},{16,28},{18,... | collective-permute-start | bytes 294920 | tf_op jit(solution)/shard_map/ppermute | solution.py:259
  49.0 2.5 %collective-permute-done.10.refs_2_ = f32[192,128]{1,0:T(8,128)S(1)} collective-permute-done((f32[192,128]{1,0:T(8,128)S(1)}, f32[192,128]{1,0:T(8,128)S(1)}, u32[]{:S(2)}, u32[]{:S(2)}) %collective-permute-start.10) | collective-permute-done | bytes 98336 | tf_op jit(solution)/shard_map/ppermute | solution.py:259
  51.4 1.5 %collective-permute-done.11.refs_3_ = f32[192,128]{1,0:T(8,128)S(1)} collective-permute-done((f32[192,128]{1,0:T(8,128)S(1)}, f32[192,128]{1,0:T(8,128)S(1)}, u32[]{:S(2)}, u32[]{:S(2)}) %collective-permute-start.11) | collective-permute-done | bytes 98336 | tf_op jit(solution)/shard_map/ppermute | solution.py:259
  53.0 1.1 %shard_map.99.refs_4_ = f32[48,1024]{1,0:T(8,128)S(1)} custom-call(s32[32]{0:T(128)S(1)} %broadcast_add_fusion.table_ref, f32[512,128]{1,0:T(8,128)S(1)} %collective-permute-done.3.refs_1_.refs_0_, f32[384,128]{1,0:T(8,128)S(1)} %collective-permute-done.9.refs_1_, f32[192,128]{1,0:T(8,128)S(1)} %collective-permute-done.10.refs_2_, ...), custom_call_target="tpu_custom_call" | custom-call | flops 201326592 | bytes 2883584 | tf_op jit(solution)/shard_map/pallas_call | solution.py:139
  54.6 0.8 %shard_map.104.refs_2_ = f32[256,1024]{1,0:T(8,128)S(1)} custom-call(bf16[256,320]{1,0:T(8,128)(2,1)S(1)} %get-tuple-element.15.refs_2_.refs_0_, bf16[256,192]{1,0:T(8,128)(2,1)S(1)} %get-tuple-element.19.refs_1_, bf16[256,320]{1,0:T(8,128)(2,1)S(1)} %get-tuple-element.20.refs_2_, f32[80,1024]{1,0:T(8,128)S(1)} %shard_map.103.refs_3_, ...), custom_call_target="tpu_custom_call" | custom-call | flops 436207616 | bytes 2097152 | tf_op jit(solution)/shard_map/pallas_call | solution.py:230
  55.5 4.3 %collective-permute-done.12.refs_1_ = f32[48,1024]{1,0:T(8,128)S(1)} collective-permute-done((f32[48,1024]{1,0:T(8,128)S(1)}, f32[48,1024]{1,0:T(8,128)S(1)}, u32[]{:S(2)}, u32[]{:S(2)}) %collective-permute-start.12) | collective-permute-done | bytes 196640 | tf_op jit(solution)/shard_map/ppermute | solution.py:375
  59.8 1.2 %shard_map.105 = f32[256,1024]{1,0:T(8,128)} custom-call(bf16[256,192]{1,0:T(8,128)(2,1)S(1)} %get-tuple-element.14.refs_0_, f32[48,1024]{1,0:T(8,128)S(1)} %collective-permute-done.12.refs_1_, f32[256,1024]{1,0:T(8,128)S(1)} %shard_map.104.refs_2_), custom_call_target="tpu_custom_call" | custom-call | flops 100663296 | bytes 2097152 | tf_op jit(solution)/shard_map/pallas_call | solution.py:230
  (52 shorter events, 3.2 us)
Async XLA Ops:
  0.0 27.8 %collective-permute-start.6 = (f32[8,128,128]{2,1,0:T(8,128)}, f32[8,128,128]{2,1,0:T(8,128)S(1)}, u32[]{:S(2)}, u32[]{:S(2)}) collective-permute-start(f32[8,128,128]{2,1,0:T(8,128)} %bitcast.4), channel_id=1, source_target_pairs={{0,16},{2,18},{4,20},{6,22},{8,24},{10,26},{12,28},{14,30},{16,0},... | collective-permute-start | bytes 1572872 | tf_op jit(solution)/shard_map/ppermute | solution.py:289
  4.0 23.7 %collective-permute-start.5 = (f32[8,128,128]{2,1,0:T(8,128)}, f32[8,128,128]{2,1,0:T(8,128)S(1)}, u32[]{:S(2)}, u32[]{:S(2)}) collective-permute-start(f32[8,128,128]{2,1,0:T(8,128)} %bitcast.5), channel_id=1, source_target_pairs={{0,8},{2,10},{4,12},{6,14},{8,0},{10,2},{12,4},{14,6},{16,24},{18,... | collective-permute-start | bytes 1572872 | tf_op jit(solution)/shard_map/ppermute | solution.py:259
  5.6 7.1 %collective-permute-start.2 = (f32[8,128,128]{2,1,0:T(8,128)}, f32[8,128,128]{2,1,0:T(8,128)}, u32[]{:S(2)}, u32[]{:S(2)}) collective-permute-start(f32[8,128,128]{2,1,0:T(8,128)} %bitcast.6), channel_id=1, source_target_pairs={{0,2},{2,0},{4,6},{6,4},{8,10},{10,8},{12,14},{14,12},{16,18},{18,... | collective-permute-start | bytes 1572872 | tf_op jit(solution)/shard_map/ppermute | solution.py:259
  7.1 3.8 %collective-permute-start = (s32[1,32]{1,0:T(1,128)S(1)}, s32[1,32]{1,0:T(1,128)S(1)}, u32[]{:S(2)}, u32[]{:S(2)}) collective-permute-start(s32[1,32]{1,0:T(1,128)S(1)} %bitcast.10), channel_id=1, source_target_pairs={{0,4},{2,6},{4,0},{6,2},{8,12},{10,14},{12,8},{14,10},{16,20},{18,... | collective-permute-start | bytes 392 | tf_op jit(solution)/shard_map/ppermute | solution.py:259
  8.7 1.6 %copy-start.2 = (f32[8,4,128,128]{3,2,1,0:T(8,128)S(1)}, f32[8,4,128,128]{3,2,1,0:T(8,128)}, u32[]{:S(2)}) copy-start(f32[8,4,128,128]{3,2,1,0:T(8,128)} %param.10) | copy-start | bytes 6291460
  10.3 0.8 %copy-start.3 = (s32[128,128]{1,0:T(8,128)S(1)}, s32[128,128]{1,0:T(8,128)}, u32[]{:S(2)}) copy-start(s32[128,128]{1,0:T(8,128)} %value_ref.1) | copy-start | bytes 196612
  10.3 0.9 %copy-start.5 = (f32[4,128]{1,0:T(4,128)S(1)}, f32[4,128]{1,0:T(4,128)}, u32[]{:S(2)}) copy-start(f32[4,128]{1,0:T(4,128)} %param.13) | copy-start | bytes 6148
  10.3 0.9 %copy-start.6 = (f32[4,128]{1,0:T(4,128)S(1)}, f32[4,128]{1,0:T(4,128)}, u32[]{:S(2)}) copy-start(f32[4,128]{1,0:T(4,128)} %param.12) | copy-start | bytes 6148
  10.3 6.4 %copy-start.4 = (f32[4,256]{1,0:T(4,128)S(1)}, f32[4,256]{1,0:T(4,128)}, u32[]{:S(2)}) copy-start(f32[4,256]{1,0:T(4,128)} %contrast_ref.1) | copy-start | bytes 12292
  11.2 5.5 %collective-permute-start.1 = (f32[72,128]{1,0:T(8,128)S(1)}, f32[72,128]{1,0:T(8,128)S(1)}, u32[]{:S(2)}, u32[]{:S(2)}) collective-permute-start(f32[72,128]{1,0:T(8,128)S(1)} %pad_maximum_fusion.1), channel_id=1, source_target_pairs={{0,1},{1,0},{2,3},{3,2},{4,5},{5,4},{6,7},{7,6},{8,9},{9,8},{10,11... | collective-permute-start | bytes 110600 | tf_op jit(solution)/shard_map/ppermute | solution.py:312
  12.8 1.0 %copy-start = (f32[1024,128]{1,0:T(8,128)S(1)}, f32[1024,128]{1,0:T(8,128)}, u32[]{:S(2)}) copy-start(f32[1024,128]{1,0:T(8,128)} %param.9) | copy-start | bytes 1572868
  15.0 12.8 %collective-permute-start.3 = (f32[512,128]{1,0:T(8,128)S(1)}, f32[512,128]{1,0:T(8,128)S(1)}, u32[]{:S(2)}, u32[]{:S(2)}) collective-permute-start(f32[512,128]{1,0:T(8,128)S(1)} %shard_map.93), channel_id=1, source_target_pairs={{0,4},{2,6},{4,0},{6,2},{8,12},{10,14},{12,8},{14,10},{16,20},{18,... | collective-permute-start | bytes 786440 | tf_op jit(solution)/shard_map/ppermute | solution.py:259
  16.2 11.6 %collective-permute-start.4 = (s32[2,32]{1,0:T(2,128)S(1)}, s32[2,32]{1,0:T(2,128)S(1)}, u32[]{:S(2)}, u32[]{:S(2)}) collective-permute-start(s32[2,32]{1,0:T(2,128)S(1)} %pad_add_fusion), channel_id=1, source_target_pairs={{0,8},{2,10},{4,12},{6,14},{8,0},{10,2},{12,4},{14,6},{16,24},{18,... | collective-permute-start | bytes 776 | tf_op jit(solution)/shard_map/ppermute | solution.py:259
  27.8 2.9 %collective-permute-start.7 = (f32[8,128,128]{2,1,0:T(8,128)S(1)}, f32[8,128,128]{2,1,0:T(8,128)S(1)}, u32[]{:S(2)}, u32[]{:S(2)}) collective-permute-start(f32[8,128,128]{2,1,0:T(8,128)S(1)} %shard_map.95.refs_3_.refs_1_), channel_id=1, source_target_pairs={{0,2},{2,0},{4,6},{6,4},{8,10},{10,8},{12,14},{14,12},{16,18},{18,... | collective-permute-start | bytes 1572872 | tf_op jit(solution)/shard_map/ppermute | solution.py:259
  27.9 2.8 %collective-permute-start.8 = (f32[8,128,128]{2,1,0:T(8,128)S(1)}, f32[8,128,128]{2,1,0:T(8,128)S(1)}, u32[]{:S(2)}, u32[]{:S(2)}) collective-permute-start(f32[8,128,128]{2,1,0:T(8,128)S(1)} %shard_map.96.refs_4_.refs_7_.refs_9_.refs_2_), channel_id=1, source_target_pairs={{0,2},{2,0},{4,6},{6,4},{8,10},{10,8},{12,14},{14,12},{16,18},{18,... | collective-permute-start | bytes 1572872 | tf_op jit(solution)/shard_map/ppermute | solution.py:259
  29.0 10.4 %collective-permute-start.15 = (f32[320,128]{1,0:T(8,128)S(1)}, f32[320,128]{1,0:T(8,128)S(1)}, u32[]{:S(2)}, u32[]{:S(2)}) collective-permute-start(f32[320,128]{1,0:T(8,128)S(1)} %shard_map.101), channel_id=1, source_target_pairs={{0,4},{2,6},{4,0},{6,2},{8,12},{10,14},{12,8},{14,10},{16,20},{18,... | collective-permute-start | bytes 491528 | tf_op jit(solution)/shard_map/ppermute | solution.py:259
  31.3 11.8 %collective-permute-start.16 = (f32[320,128]{1,0:T(8,128)S(1)}, f32[320,128]{1,0:T(8,128)S(1)}, u32[]{:S(2)}, u32[]{:S(2)}) collective-permute-start(f32[320,128]{1,0:T(8,128)S(1)} %shard_map.102), channel_id=1, source_target_pairs={{0,4},{2,6},{4,0},{6,2},{8,12},{10,14},{12,8},{14,10},{16,20},{18,... | collective-permute-start | bytes 491528 | tf_op jit(solution)/shard_map/ppermute | solution.py:259
  33.5 9.6 %collective-permute-start.13 = (f32[320,128]{1,0:T(8,128)S(1)}, f32[320,128]{1,0:T(8,128)S(1)}, u32[]{:S(2)}, u32[]{:S(2)}) collective-permute-start(f32[320,128]{1,0:T(8,128)S(1)} %get-tuple-element.21), channel_id=1, source_target_pairs={{0,12},{2,14},{4,8},{6,10},{8,4},{10,6},{12,0},{14,2},{16,28},{18,... | collective-permute-start | bytes 491528 | tf_op jit(solution)/shard_map/ppermute | solution.py:259
  35.1 3.0 %copy-start.1 = (f32[1024,128]{1,0:T(8,128)S(1)}, f32[1024,128]{1,0:T(8,128)}, u32[]{:S(2)}) copy-start(f32[1024,128]{1,0:T(8,128)} %param.9) | copy-start | bytes 1572868
  35.1 8.1 %collective-permute-start.14 = (f32[320,128]{1,0:T(8,128)S(1)}, f32[320,128]{1,0:T(8,128)S(1)}, u32[]{:S(2)}, u32[]{:S(2)}) collective-permute-start(f32[320,128]{1,0:T(8,128)S(1)} %get-tuple-element.22), channel_id=1, source_target_pairs={{0,8},{2,10},{4,12},{6,14},{8,0},{10,2},{12,4},{14,6},{16,24},{18,... | collective-permute-start | bytes 491528 | tf_op jit(solution)/shard_map/ppermute | solution.py:259
  36.6 16.4 %collective-permute-start.9 = (f32[384,128]{1,0:T(8,128)S(1)}, f32[384,128]{1,0:T(8,128)S(1)}, u32[]{:S(2)}, u32[]{:S(2)}) collective-permute-start(f32[384,128]{1,0:T(8,128)S(1)} %get-tuple-element.16), channel_id=1, source_target_pairs={{0,4},{2,6},{4,0},{6,2},{8,12},{10,14},{12,8},{14,10},{16,20},{18,... | collective-permute-start | bytes 589832 | tf_op jit(solution)/shard_map/ppermute | solution.py:259
  44.4 10.3 %collective-permute-start.17 = (f32[80,1024]{1,0:T(8,128)S(1)}, f32[80,1024]{1,0:T(8,128)S(1)}, u32[]{:S(2)}, u32[]{:S(2)}) collective-permute-start(f32[80,1024]{1,0:T(8,128)S(1)} %shard_map.103.refs_3_), channel_id=1, source_target_pairs={{0,1},{1,0},{2,3},{3,2},{4,5},{5,4},{6,7},{7,6},{8,9},{9,8},{10,11... | collective-permute-start | bytes 983048 | tf_op jit(solution)/shard_map/ppermute | solution.py:375
  46.0 5.4 %collective-permute-start.10 = (f32[192,128]{1,0:T(8,128)S(1)}, f32[192,128]{1,0:T(8,128)S(1)}, u32[]{:S(2)}, u32[]{:S(2)}) collective-permute-start(f32[192,128]{1,0:T(8,128)S(1)} %get-tuple-element.17), channel_id=1, source_target_pairs={{0,8},{2,10},{4,12},{6,14},{8,0},{10,2},{12,4},{14,6},{16,24},{18,... | collective-permute-start | bytes 294920 | tf_op jit(solution)/shard_map/ppermute | solution.py:259
  47.5 5.5 %collective-permute-start.11 = (f32[192,128]{1,0:T(8,128)S(1)}, f32[192,128]{1,0:T(8,128)S(1)}, u32[]{:S(2)}, u32[]{:S(2)}) collective-permute-start(f32[192,128]{1,0:T(8,128)S(1)} %get-tuple-element.18), channel_id=1, source_target_pairs={{0,12},{2,14},{4,8},{6,10},{8,4},{10,6},{12,0},{14,2},{16,28},{18,... | collective-permute-start | bytes 294920 | tf_op jit(solution)/shard_map/ppermute | solution.py:259
  54.1 5.7 %collective-permute-start.12 = (f32[48,1024]{1,0:T(8,128)S(1)}, f32[48,1024]{1,0:T(8,128)S(1)}, u32[]{:S(2)}, u32[]{:S(2)}) collective-permute-start(f32[48,1024]{1,0:T(8,128)S(1)} %shard_map.99.refs_4_), channel_id=1, source_target_pairs={{0,1},{1,0},{2,3},{3,2},{4,5},{5,4},{6,7},{7,6},{8,9},{9,8},{10,11... | collective-permute-start | bytes 589832 | tf_op jit(solution)/shard_map/ppermute | solution.py:375

commit v6 on v5

--- a/solution.py
+++ b/solution.py
@@ -9,7 +9,7 @@
 from jax.sharding import PartitionSpec as P
 
 GROUP = 8
-SHARES = (5, 3)
+SHARES = (1, 1)
 LANES = 128
 ANY = pl.BlockSpec(memory_space=pl.ANY)
 SMEM = pl.BlockSpec(memory_space=pltpu.SMEM)
@@ -358,12 +358,11 @@
     second = {(k, m ^ 1): swap(value, 1) for (k, m), value in arrived.items()}
     everything = {**arrived, **second}
     far = {key: value for key, value in everything.items() if key[0]}
-    others = [(m, far) for m in range(4, group, 2)]
-    pick([(m, far, 0, subs[0]) for m in (6, 4)], [])
+    pick([(6, far, 0, width), (4, far, 0, subs[0])], [])
     sooner = pick([(2, arrived, 0, subs[0])], [])
     pick([(2, second, 0, subs[0])], [])
     for start, sub in list(zip(starts, subs))[1:]:
-        pick([(m, items, start, sub) for m, items in [(2, everything)] + others], [])
+        pick([(2, everything, start, sub), (4, far, start, sub)], sooner)
     pick([(0, {**near, **arrived, **second}, 0, width)], [])
     smoothed = [
         smooth(tuple(plans[c]), table, sources[c], sub, tiles, block_count)

time: 61.4 us -> 60.8 us (level)
    ppermute x14 -> x13, waiting for transfers between devices: 17.9 us -> 13.6 us  [swap(): return lax.ppermute(value, 'fix', [(i, i ^ mask) for i in range(fix_count)])]
    ppermute x1, waiting for transfers between devices: 0.01 us -> 2.5 us  [per_device(): far_raw[k] = lax.ppermute(raw, 'fix', pairs)]
    ppermute x2, waiting for transfers between devices: 4.33 us -> 6.08 us  [per_device(): parts.extend((lax.ppermute(value, 'subj', pairs) for value in smoothed))]
    ppermute x1, starting transfers between devices: 4.04 us -> 2.59 us  [per_device(): far_raw[k] = lax.ppermute(raw, 'fix', pairs)]
    ppermute x2, starting transfers between devices: 2.21 us -> 3.16 us  [per_device(): parts.extend((lax.ppermute(value, 'subj', pairs) for value in smoothed))]
    ppermute x14 -> x13, starting transfers between devices: 15 us -> 15.4 us  [swap(): return lax.ppermute(value, 'fix', [(i, i ^ mask) for i in range(fix_count)])]
  transfers between devices with their start and end apart: 18 -> 17, of which waited for: 5 -> 6; matrix products, arithmetic and copies ran while one was open for 3% -> 3% of each run, Pallas kernels for 17% -> 16%
where the time goes in v6:
time: 60.8 us; the launch traced here: 60.4 us
  starting transfers between devices  22.7 us (37%)
  waiting for transfers between devices  22.2 us (37%)
  Pallas kernels  10.9 us (18%)
  local copies, waits for them, and re-layouts  3.85 us (6%)
    ppermute x13, starting transfers between devices, swap(): return lax.ppermute(value, 'fix', [(i, i ^ mask) for i in range(fix_count)])  15.4 us
    ppermute x13, waiting for transfers between devices, swap(): return lax.ppermute(value, 'fix', [(i, i ^ mask) for i in range(fix_count)])  13.6 us
    ppermute x2, waiting for transfers between devices, per_device(): parts.extend((lax.ppermute(value, 'subj', pairs) for value in smoothed))  6.08 us
    pallas_call x6, Pallas kernels, pack(): pl.pallas_call(functools.partial(pack_kernel, lists, cap, (len(tables), l...  5.41 us
    ppermute x2, starting transfers between devices, per_device(): parts.extend((lax.ppermute(value, 'subj', pairs) for value in smoothed))  3.16 us
    unnamed x14, local copies, waits for them, and re-layouts  2.84 us
    ppermute x1, starting transfers between devices, per_device(): far_raw[k] = lax.ppermute(raw, 'fix', pairs)  2.59 us
    ppermute x1, waiting for transfers between devices, per_device(): far_raw[k] = lax.ppermute(raw, 'fix', pairs)  2.5 us
  transfers between devices with their start and end apart: 17, of which 6 were waited for; matrix products, arithmetic and copies ran while one was open for 3% of the time, Pallas kernels for 16%

profile of v6, /device:TPU:0, one launch (start us, length us, event | category | flops | bytes accessed | tf_op | source)
XLA Modules:
  0.0 60.4 jit_solution(2300518689940548517)
XLA Ops:
  0.0 3.0 %collective-permute-start.8 = (f32[8,128,128]{2,1,0:T(8,128)}, f32[8,128,128]{2,1,0:T(8,128)S(1)}, u32[]{:S(2)}, u32[]{:S(2)}) collective-permute-start(f32[8,128,128]{2,1,0:T(8,128)} %bitcast.4), channel_id=1, source_target_pairs={{0,8},{2,10},{4,12},{6,14},{8,0},{10,2},{12,4},{14,6},{16,24},{18,... | collective-permute-start | bytes 1572872 | tf_op jit(solution)/shard_map/ppermute | solution.py:259
  3.0 2.6 %collective-permute-start.5 = (f32[8,128,128]{2,1,0:T(8,128)}, f32[8,128,128]{2,1,0:T(8,128)S(1)}, u32[]{:S(2)}, u32[]{:S(2)}) collective-permute-start(f32[8,128,128]{2,1,0:T(8,128)} %bitcast.5), channel_id=1, source_target_pairs={{0,16},{2,18},{4,20},{6,22},{8,24},{10,26},{12,28},{14,30},{16,0},... | collective-permute-start | bytes 1572872 | tf_op jit(solution)/shard_map/ppermute | solution.py:289
  5.8 0.8 %reshape.106 = s32[32]{0:T(128)S(1)} reshape(s32[4,8]{1,0:T(4,128)} %bitcast.13) | data formatting | bytes 256 | tf_op jit(solution)/shard_map/reshape | solution.py:261
  7.1 1.6 %collective-permute-start = (s32[1,32]{1,0:T(1,128)S(1)}, s32[1,32]{1,0:T(1,128)S(1)}, u32[]{:S(2)}, u32[]{:S(2)}) collective-permute-start(s32[1,32]{1,0:T(1,128)S(1)} %bitcast.10), channel_id=1, source_target_pairs={{0,4},{2,6},{4,0},{6,2},{8,12},{10,14},{12,8},{14,10},{16,20},{18,... | collective-permute-start | bytes 392 | tf_op jit(solution)/shard_map/ppermute | solution.py:259
  8.7 1.6 %copy-done.2 = f32[8,4,128,128]{3,2,1,0:T(8,128)S(1)} copy-done((f32[8,4,128,128]{3,2,1,0:T(8,128)S(1)}, f32[8,4,128,128]{3,2,1,0:T(8,128)}, u32[]{:S(2)}) %copy-start.2) | copy-done | bytes 2097176
  10.3 0.6 %shard_map.94.refs_3_.refs_5_.refs_6_ = bf16[32,128,256]{2,1,0:T(8,128)(2,1)S(1)} custom-call(f32[32,128,128]{2,1,0:T(8,128)S(1)} %bitcast.9), custom_call_target="tpu_custom_call" | custom-call | flops 2097152 | bytes 4194304 | tf_op jit(solution)/shard_map/pallas_call | solution.py:70
  11.2 1.6 %collective-permute-start.1 = (f32[72,128]{1,0:T(8,128)S(1)}, f32[72,128]{1,0:T(8,128)S(1)}, u32[]{:S(2)}, u32[]{:S(2)}) collective-permute-start(f32[72,128]{1,0:T(8,128)S(1)} %pad_maximum_fusion.1), channel_id=1, source_target_pairs={{0,1},{1,0},{2,3},{3,2},{4,5},{5,4},{6,7},{7,6},{8,9},{9,8},{10,11... | collective-permute-start | bytes 110600 | tf_op jit(solution)/shard_map/ppermute | solution.py:312
  12.8 1.0 %copy-done = f32[1024,128]{1,0:T(8,128)S(1)} copy-done((f32[1024,128]{1,0:T(8,128)S(1)}, f32[1024,128]{1,0:T(8,128)}, u32[]{:S(2)}) %copy-start) | copy-done | bytes 524312
  13.8 1.2 %shard_map.93 = f32[512,128]{1,0:T(8,128)S(1)} custom-call(s32[16]{0:T(128)S(1)} %mul.38.base_ref, s32[1,32]{1,0:T(1,128)S(1)} %collective-permute-done.refs_0_, f32[8,128,128]{2,1,0:T(8,128)S(1)} %bitcast.7, f32[8,128,128]{2,1,0:T(8,128)} %collective-permute-done.2.refs_2_), custom_call_target="tpu_custom_call" | custom-call | bytes 524288 | tf_op jit(solution)/shard_map/pallas_call | solution.py:101
  15.0 1.2 %collective-permute-start.3 = (f32[512,128]{1,0:T(8,128)S(1)}, f32[512,128]{1,0:T(8,128)S(1)}, u32[]{:S(2)}, u32[]{:S(2)}) collective-permute-start(f32[512,128]{1,0:T(8,128)S(1)} %shard_map.93), channel_id=1, source_target_pairs={{0,4},{2,6},{4,0},{6,2},{8,12},{10,14},{12,8},{14,10},{16,20},{18,... | collective-permute-start | bytes 786440 | tf_op jit(solution)/shard_map/ppermute | solution.py:259
  16.7 0.8 %shard_map.92 = (bf16[256,256]{1,0:T(8,128)(2,1)S(1)}, bf16[256,256]{1,0:T(8,128)(2,1)S(1)}, bf16[256,256]{1,0:T(8,128)(2,1)S(1)}, bf16[256,256]{1,0:T(8,128)(2,1)S(1)}) custom-call(f32[64,256]{1,0:T(8,128)S(1)} %slice.12.perm_ref, f32[4,256]{1,0:T(4,128)S(1)} %copy-done.4, f32[4,256]{1,0:T(4,128)S(1)} %get-tuple-element.24.nuisance_ref, ...), custom_call_target="tpu_custom_call" | custom-call | flops 2097152 | bytes 524288 | tf_op jit(solution)/shard_map/pallas_call | solution.py:184
  17.5 8.8 %collective-permute-done.4.refs_4_.refs_0_.refs_1_ = s32[2,32]{1,0:T(2,128)S(1)} collective-permute-done((s32[2,32]{1,0:T(2,128)S(1)}, s32[2,32]{1,0:T(2,128)S(1)}, u32[]{:S(2)}, u32[]{:S(2)}) %collective-permute-start.4) | collective-permute-done | bytes 288 | tf_op jit(solution)/shard_map/ppermute | solution.py:259
  26.3 2.5 %collective-permute-done.5.refs_0_ = f32[8,128,128]{2,1,0:T(8,128)S(1)} collective-permute-done((f32[8,128,128]{2,1,0:T(8,128)}, f32[8,128,128]{2,1,0:T(8,128)S(1)}, u32[]{:S(2)}, u32[]{:S(2)}) %collective-permute-start.5) | collective-permute-done | bytes 524320 | tf_op jit(solution)/shard_map/ppermute | solution.py:289
  29.3 0.7 %shard_map.98 = f32[256,128]{1,0:T(8,128)S(1)} custom-call(s32[16]{0:T(128)S(1)} %mul.38.base_ref, s32[1,32]{1,0:T(1,128)S(1)} %collective-permute-done.refs_0_, f32[8,128,128]{2,1,0:T(8,128)S(1)} %shard_map.97.refs_1_.refs_2_.refs_3_, f32[8,128,128]{2,1,0:T(8,128)S(1)} %shard_map.95.refs_2_.refs_4_.refs_3_.refs_6_), custom_call_target="tpu_custom_call" | custom-call | bytes 262144 | tf_op jit(solution)/shard_map/pallas_call | solution.py:101
  30.0 1.6 %collective-permute-start.10 = (f32[256,128]{1,0:T(8,128)S(1)}, f32[256,128]{1,0:T(8,128)S(1)}, u32[]{:S(2)}, u32[]{:S(2)}) collective-permute-start(f32[256,128]{1,0:T(8,128)S(1)} %shard_map.98), channel_id=1, source_target_pairs={{0,4},{2,6},{4,0},{6,2},{8,12},{10,14},{12,8},{14,10},{16,20},{18,... | collective-permute-start | bytes 393224 | tf_op jit(solution)/shard_map/ppermute | solution.py:259
  31.6 0.8 %shard_map.96 = (f32[512,128]{1,0:T(8,128)S(1)}, f32[256,128]{1,0:T(8,128)S(1)}) custom-call(s32[16]{0:T(128)S(1)} %mul.38.base_ref, s32[2,32]{1,0:T(2,128)S(1)} %collective-permute-done.4.refs_4_.refs_0_.refs_1_, s32[2,32]{1,0:T(2,128)S(1)} %collective-permute-done.4.refs_4_.refs_0_.refs_1_, f32[8,128,128]{2,1,0:T(8,128)S(1)} %shard_map.95.refs_2_.refs_4_.refs_3_.refs_6_, ...), custom_call_target="tpu_custom_call" | custom-call | bytes 786432 | tf_op jit(solution)/shard_map/pallas_call | solution.py:101
  32.3 0.6 collective-permute-start.7
  32.9 0.7 %shard_map.102 = f32[256,128]{1,0:T(8,128)S(1)} custom-call(s32[16]{0:T(128)S(1)} %mul.38.base_ref, s32[1,32]{1,0:T(1,128)S(1)} %collective-permute-done.refs_0_, f32[8,128,128]{2,1,0:T(8,128)S(1)} %collective-permute-done.9.refs_4_.refs_5_.refs_1_, f32[8,128,128]{2,1,0:T(8,128)S(1)} %collective-permute-done.6.refs_3_.refs_5_.refs_7_.refs_6_.refs_2_), custom_call_target="tpu_custom_call" | custom-call | bytes 262144 | tf_op jit(solution)/shard_map/pallas_call | solution.py:101
  33.6 1.4 %collective-permute-start.15 = (f32[256,128]{1,0:T(8,128)S(1)}, f32[256,128]{1,0:T(8,128)S(1)}, u32[]{:S(2)}, u32[]{:S(2)}) collective-permute-start(f32[256,128]{1,0:T(8,128)S(1)} %shard_map.102), channel_id=1, source_target_pairs={{0,4},{2,6},{4,0},{6,2},{8,12},{10,14},{12,8},{14,10},{16,20},{18,... | collective-permute-start | bytes 393224 | tf_op jit(solution)/shard_map/ppermute | solution.py:259
  35.0 4.5 %collective-permute-done.10.refs_8_.refs_3_ = f32[256,128]{1,0:T(8,128)S(1)} collective-permute-done((f32[256,128]{1,0:T(8,128)S(1)}, f32[256,128]{1,0:T(8,128)S(1)}, u32[]{:S(2)}, u32[]{:S(2)}) %collective-permute-start.10) | collective-permute-done | bytes 131104 | tf_op jit(solution)/shard_map/ppermute | solution.py:259
  39.5 0.8 %shard_map.99 = (f32[512,128]{1,0:T(8,128)S(1)}, f32[256,128]{1,0:T(8,128)S(1)}) custom-call(s32[16]{0:T(128)S(1)} %mul.38.base_ref, s32[1,32]{1,0:T(1,128)S(1)} %collective-permute-done.refs_0_, s32[2,32]{1,0:T(2,128)S(1)} %collective-permute-done.4.refs_4_.refs_0_.refs_1_, f32[8,128,128]{2,1,0:T(8,128)S(1)} %shard_map.97.refs_1_.refs_2_.refs_3_, ...), custom_call_target="tpu_custom_call" | custom-call | bytes 786432 | tf_op jit(solution)/shard_map/pallas_call | solution.py:101
  40.9 1.6 %collective-permute-start.14 = (f32[256,128]{1,0:T(8,128)S(1)}, f32[256,128]{1,0:T(8,128)S(1)}, u32[]{:S(2)}, u32[]{:S(2)}) collective-permute-start(f32[256,128]{1,0:T(8,128)S(1)} %get-tuple-element.20), channel_id=1, source_target_pairs={{0,8},{2,10},{4,12},{6,14},{8,0},{10,2},{12,4},{14,6},{16,24},{18,... | collective-permute-start | bytes 393224 | tf_op jit(solution)/shard_map/ppermute | solution.py:259
  42.5 3.0 %collective-permute-start.11 = (f32[512,128]{1,0:T(8,128)S(1)}, f32[512,128]{1,0:T(8,128)S(1)}, u32[]{:S(2)}, u32[]{:S(2)}) collective-permute-start(f32[512,128]{1,0:T(8,128)S(1)} %get-tuple-element.16), channel_id=1, source_target_pairs={{0,4},{2,6},{4,0},{6,2},{8,12},{10,14},{12,8},{14,10},{16,20},{18,... | collective-permute-start | bytes 786440 | tf_op jit(solution)/shard_map/ppermute | solution.py:259
  45.5 1.3 %shard_map.100.refs_4_.refs_5_ = f32[1536,128]{1,0:T(8,128)S(1)} custom-call(s32[16]{0:T(128)S(1)} %mul.38.base_ref, s32[1,32]{1,0:T(1,128)S(1)} %bitcast.12, f32[8,128,128]{2,1,0:T(8,128)S(1)} %bitcast.8, f32[8,128,128]{2,1,0:T(8,128)} %collective-permute-done.2.refs_2_, f32[8,128,128]{2,1,0:T(8,128)S(1)} %shard_map.97.refs_1_.refs_2_.refs_3_, ...), custom_call_target="tpu_custom_call" | custom-call | bytes 1572864 | tf_op jit(solution)/shard_map/pallas_call | solution.py:101
  46.8 1.1 %shard_map.103.refs_3_ = f32[64,1024]{1,0:T(8,128)S(1)} custom-call(s32[32]{0:T(128)S(1)} %broadcast_add_fusion.table_ref, f32[512,128]{1,0:T(8,128)S(1)} %collective-permute-done.3.refs_1_.refs_0_, f32[512,128]{1,0:T(8,128)S(1)} %collective-permute-done.7.refs_1_, f32[256,128]{1,0:T(8,128)S(1)} %collective-permute-done.14.refs_2_, ...), custom_call_target="tpu_custom_call" | custom-call | flops 268435456 | bytes 3145728 | tf_op jit(solution)/shard_map/pallas_call | solution.py:139
  47.9 1.6 %collective-permute-start.16 = (f32[64,1024]{1,0:T(8,128)S(1)}, f32[64,1024]{1,0:T(8,128)S(1)}, u32[]{:S(2)}, u32[]{:S(2)}) collective-permute-start(f32[64,1024]{1,0:T(8,128)S(1)} %shard_map.103.refs_3_), channel_id=1, source_target_pairs={{0,1},{1,0},{2,3},{3,2},{4,5},{5,4},{6,7},{7,6},{8,9},{9,8},{10,11... | collective-permute-start | bytes 786440 | tf_op jit(solution)/shard_map/ppermute | solution.py:374
  49.8 1.1 %shard_map.101.refs_4_ = f32[64,1024]{1,0:T(8,128)S(1)} custom-call(s32[32]{0:T(128)S(1)} %broadcast_add_fusion.table_ref, f32[512,128]{1,0:T(8,128)S(1)} %collective-permute-done.3.refs_1_.refs_0_, f32[512,128]{1,0:T(8,128)S(1)} %collective-permute-done.7.refs_1_, f32[512,128]{1,0:T(8,128)S(1)} %collective-permute-done.11.refs_2_, ...), custom_call_target="tpu_custom_call" | custom-call | flops 268435456 | bytes 3145728 | tf_op jit(solution)/shard_map/pallas_call | solution.py:139
  50.9 1.6 %collective-permute-start.13 = (f32[64,1024]{1,0:T(8,128)S(1)}, f32[64,1024]{1,0:T(8,128)S(1)}, u32[]{:S(2)}, u32[]{:S(2)}) collective-permute-start(f32[64,1024]{1,0:T(8,128)S(1)} %shard_map.101.refs_4_), channel_id=1, source_target_pairs={{0,1},{1,0},{2,3},{3,2},{4,5},{5,4},{6,7},{7,6},{8,9},{9,8},{10,11... | collective-permute-start | bytes 786440 | tf_op jit(solution)/shard_map/ppermute | solution.py:374
  52.5 3.9 %collective-permute-done.16.refs_5_ = f32[64,1024]{1,0:T(8,128)S(1)} collective-permute-done((f32[64,1024]{1,0:T(8,128)S(1)}, f32[64,1024]{1,0:T(8,128)S(1)}, u32[]{:S(2)}, u32[]{:S(2)}) %collective-permute-start.16) | collective-permute-done | bytes 262176 | tf_op jit(solution)/shard_map/ppermute | solution.py:374
  56.4 0.6 shard_map.104.refs_2_
  56.9 2.2 %collective-permute-done.13.refs_1_ = f32[64,1024]{1,0:T(8,128)S(1)} collective-permute-done((f32[64,1024]{1,0:T(8,128)S(1)}, f32[64,1024]{1,0:T(8,128)S(1)}, u32[]{:S(2)}, u32[]{:S(2)}) %collective-permute-start.13) | collective-permute-done | bytes 262176 | tf_op jit(solution)/shard_map/ppermute | solution.py:374
  59.2 1.2 %shard_map.105 = f32[256,1024]{1,0:T(8,128)} custom-call(bf16[256,256]{1,0:T(8,128)(2,1)S(1)} %get-tuple-element.13.refs_0_, f32[64,1024]{1,0:T(8,128)S(1)} %collective-permute-done.13.refs_1_, f32[256,1024]{1,0:T(8,128)S(1)} %shard_map.104.refs_2_), custom_call_target="tpu_custom_call" | custom-call | flops 134217728 | bytes 2097152 | tf_op jit(solution)/shard_map/pallas_call | solution.py:230
  (50 shorter events, 2.8 us)
Async XLA Ops:
  0.0 28.8 %collective-permute-start.8 = (f32[8,128,128]{2,1,0:T(8,128)}, f32[8,128,128]{2,1,0:T(8,128)S(1)}, u32[]{:S(2)}, u32[]{:S(2)}) collective-permute-start(f32[8,128,128]{2,1,0:T(8,128)} %bitcast.4), channel_id=1, source_target_pairs={{0,8},{2,10},{4,12},{6,14},{8,0},{10,2},{12,4},{14,6},{16,24},{18,... | collective-permute-start | bytes 1572872 | tf_op jit(solution)/shard_map/ppermute | solution.py:259
  3.0 25.8 %collective-permute-start.5 = (f32[8,128,128]{2,1,0:T(8,128)}, f32[8,128,128]{2,1,0:T(8,128)S(1)}, u32[]{:S(2)}, u32[]{:S(2)}) collective-permute-start(f32[8,128,128]{2,1,0:T(8,128)} %bitcast.5), channel_id=1, source_target_pairs={{0,16},{2,18},{4,20},{6,22},{8,24},{10,26},{12,28},{14,30},{16,0},... | collective-permute-start | bytes 1572872 | tf_op jit(solution)/shard_map/ppermute | solution.py:289
  5.6 7.1 %collective-permute-start.2 = (f32[8,128,128]{2,1,0:T(8,128)}, f32[8,128,128]{2,1,0:T(8,128)}, u32[]{:S(2)}, u32[]{:S(2)}) collective-permute-start(f32[8,128,128]{2,1,0:T(8,128)} %bitcast.6), channel_id=1, source_target_pairs={{0,2},{2,0},{4,6},{6,4},{8,10},{10,8},{12,14},{14,12},{16,18},{18,... | collective-permute-start | bytes 1572872 | tf_op jit(solution)/shard_map/ppermute | solution.py:259
  7.1 3.8 %collective-permute-start = (s32[1,32]{1,0:T(1,128)S(1)}, s32[1,32]{1,0:T(1,128)S(1)}, u32[]{:S(2)}, u32[]{:S(2)}) collective-permute-start(s32[1,32]{1,0:T(1,128)S(1)} %bitcast.10), channel_id=1, source_target_pairs={{0,4},{2,6},{4,0},{6,2},{8,12},{10,14},{12,8},{14,10},{16,20},{18,... | collective-permute-start | bytes 392 | tf_op jit(solution)/shard_map/ppermute | solution.py:259
  8.7 1.6 %copy-start.2 = (f32[8,4,128,128]{3,2,1,0:T(8,128)S(1)}, f32[8,4,128,128]{3,2,1,0:T(8,128)}, u32[]{:S(2)}) copy-start(f32[8,4,128,128]{3,2,1,0:T(8,128)} %param.10) | copy-start | bytes 6291460
  10.3 0.8 %copy-start.3 = (s32[128,128]{1,0:T(8,128)S(1)}, s32[128,128]{1,0:T(8,128)}, u32[]{:S(2)}) copy-start(s32[128,128]{1,0:T(8,128)} %value_ref.1) | copy-start | bytes 196612
  10.3 0.9 %copy-start.5 = (f32[4,128]{1,0:T(4,128)S(1)}, f32[4,128]{1,0:T(4,128)}, u32[]{:S(2)}) copy-start(f32[4,128]{1,0:T(4,128)} %param.13) | copy-start | bytes 6148
  10.3 0.9 %copy-start.6 = (f32[4,128]{1,0:T(4,128)S(1)}, f32[4,128]{1,0:T(4,128)}, u32[]{:S(2)}) copy-start(f32[4,128]{1,0:T(4,128)} %param.12) | copy-start | bytes 6148
  10.3 6.4 %copy-start.4 = (f32[4,256]{1,0:T(4,128)S(1)}, f32[4,256]{1,0:T(4,128)}, u32[]{:S(2)}) copy-start(f32[4,256]{1,0:T(4,128)} %contrast_ref.1) | copy-start | bytes 12292
  11.2 5.5 %collective-permute-start.1 = (f32[72,128]{1,0:T(8,128)S(1)}, f32[72,128]{1,0:T(8,128)S(1)}, u32[]{:S(2)}, u32[]{:S(2)}) collective-permute-start(f32[72,128]{1,0:T(8,128)S(1)} %pad_maximum_fusion.1), channel_id=1, source_target_pairs={{0,1},{1,0},{2,3},{3,2},{4,5},{5,4},{6,7},{7,6},{8,9},{9,8},{10,11... | collective-permute-start | bytes 110600 | tf_op jit(solution)/shard_map/ppermute | solution.py:312
  12.8 1.0 %copy-start = (f32[1024,128]{1,0:T(8,128)S(1)}, f32[1024,128]{1,0:T(8,128)}, u32[]{:S(2)}) copy-start(f32[1024,128]{1,0:T(8,128)} %param.9) | copy-start | bytes 1572868
  15.0 13.8 %collective-permute-start.3 = (f32[512,128]{1,0:T(8,128)S(1)}, f32[512,128]{1,0:T(8,128)S(1)}, u32[]{:S(2)}, u32[]{:S(2)}) collective-permute-start(f32[512,128]{1,0:T(8,128)S(1)} %shard_map.93), channel_id=1, source_target_pairs={{0,4},{2,6},{4,0},{6,2},{8,12},{10,14},{12,8},{14,10},{16,20},{18,... | collective-permute-start | bytes 786440 | tf_op jit(solution)/shard_map/ppermute | solution.py:259
  16.2 10.1 %collective-permute-start.4 = (s32[2,32]{1,0:T(2,128)S(1)}, s32[2,32]{1,0:T(2,128)S(1)}, u32[]{:S(2)}, u32[]{:S(2)}) collective-permute-start(s32[2,32]{1,0:T(2,128)S(1)} %pad_add_fusion), channel_id=1, source_target_pairs={{0,8},{2,10},{4,12},{6,14},{8,0},{10,2},{12,4},{14,6},{16,24},{18,... | collective-permute-start | bytes 776 | tf_op jit(solution)/shard_map/ppermute | solution.py:259
  28.8 2.7 %collective-permute-start.6 = (f32[8,128,128]{2,1,0:T(8,128)S(1)}, f32[8,128,128]{2,1,0:T(8,128)S(1)}, u32[]{:S(2)}, u32[]{:S(2)}) collective-permute-start(f32[8,128,128]{2,1,0:T(8,128)S(1)} %shard_map.95.refs_2_.refs_4_.refs_3_.refs_6_), channel_id=1, source_target_pairs={{0,2},{2,0},{4,6},{6,4},{8,10},{10,8},{12,14},{14,12},{16,18},{18,... | collective-permute-start | bytes 1572872 | tf_op jit(solution)/shard_map/ppermute | solution.py:259
  28.8 4.1 %collective-permute-start.9 = (f32[8,128,128]{2,1,0:T(8,128)S(1)}, f32[8,128,128]{2,1,0:T(8,128)S(1)}, u32[]{:S(2)}, u32[]{:S(2)}) collective-permute-start(f32[8,128,128]{2,1,0:T(8,128)S(1)} %shard_map.97.refs_1_.refs_2_.refs_3_), channel_id=1, source_target_pairs={{0,2},{2,0},{4,6},{6,4},{8,10},{10,8},{12,14},{14,12},{16,18},{18,... | collective-permute-start | bytes 1572872 | tf_op jit(solution)/shard_map/ppermute | solution.py:259
  30.0 9.5 %collective-permute-start.10 = (f32[256,128]{1,0:T(8,128)S(1)}, f32[256,128]{1,0:T(8,128)S(1)}, u32[]{:S(2)}, u32[]{:S(2)}) collective-permute-start(f32[256,128]{1,0:T(8,128)S(1)} %shard_map.98), channel_id=1, source_target_pairs={{0,4},{2,6},{4,0},{6,2},{8,12},{10,14},{12,8},{14,10},{16,20},{18,... | collective-permute-start | bytes 393224 | tf_op jit(solution)/shard_map/ppermute | solution.py:259
  32.3 13.1 %copy-start.1 = (f32[1024,128]{1,0:T(8,128)S(1)}, f32[1024,128]{1,0:T(8,128)}, u32[]{:S(2)}) copy-start(f32[1024,128]{1,0:T(8,128)} %param.9) | copy-start | bytes 1572868
  32.3 14.5 %collective-permute-start.7 = (f32[512,128]{1,0:T(8,128)S(1)}, f32[512,128]{1,0:T(8,128)S(1)}, u32[]{:S(2)}, u32[]{:S(2)}) collective-permute-start(f32[512,128]{1,0:T(8,128)S(1)} %get-tuple-element.15), channel_id=1, source_target_pairs={{0,12},{2,14},{4,8},{6,10},{8,4},{10,6},{12,0},{14,2},{16,28},{18,... | collective-permute-start | bytes 786440 | tf_op jit(solution)/shard_map/ppermute | solution.py:259
  33.6 13.2 %collective-permute-start.15 = (f32[256,128]{1,0:T(8,128)S(1)}, f32[256,128]{1,0:T(8,128)S(1)}, u32[]{:S(2)}, u32[]{:S(2)}) collective-permute-start(f32[256,128]{1,0:T(8,128)S(1)} %shard_map.102), channel_id=1, source_target_pairs={{0,4},{2,6},{4,0},{6,2},{8,12},{10,14},{12,8},{14,10},{16,20},{18,... | collective-permute-start | bytes 393224 | tf_op jit(solution)/shard_map/ppermute | solution.py:259
  40.4 9.1 %collective-permute-start.12 = (f32[256,128]{1,0:T(8,128)S(1)}, f32[256,128]{1,0:T(8,128)S(1)}, u32[]{:S(2)}, u32[]{:S(2)}) collective-permute-start(f32[256,128]{1,0:T(8,128)S(1)} %get-tuple-element.17), channel_id=1, source_target_pairs={{0,8},{2,10},{4,12},{6,14},{8,0},{10,2},{12,4},{14,6},{16,24},{18,... | collective-permute-start | bytes 393224 | tf_op jit(solution)/shard_map/ppermute | solution.py:259
  40.9 5.9 %collective-permute-start.14 = (f32[256,128]{1,0:T(8,128)S(1)}, f32[256,128]{1,0:T(8,128)S(1)}, u32[]{:S(2)}, u32[]{:S(2)}) collective-permute-start(f32[256,128]{1,0:T(8,128)S(1)} %get-tuple-element.20), channel_id=1, source_target_pairs={{0,8},{2,10},{4,12},{6,14},{8,0},{10,2},{12,4},{14,6},{16,24},{18,... | collective-permute-start | bytes 393224 | tf_op jit(solution)/shard_map/ppermute | solution.py:259
  42.5 7.3 %collective-permute-start.11 = (f32[512,128]{1,0:T(8,128)S(1)}, f32[512,128]{1,0:T(8,128)S(1)}, u32[]{:S(2)}, u32[]{:S(2)}) collective-permute-start(f32[512,128]{1,0:T(8,128)S(1)} %get-tuple-element.16), channel_id=1, source_target_pairs={{0,4},{2,6},{4,0},{6,2},{8,12},{10,14},{12,8},{14,10},{16,20},{18,... | collective-permute-start | bytes 786440 | tf_op jit(solution)/shard_map/ppermute | solution.py:259
  47.9 8.4 %collective-permute-start.16 = (f32[64,1024]{1,0:T(8,128)S(1)}, f32[64,1024]{1,0:T(8,128)S(1)}, u32[]{:S(2)}, u32[]{:S(2)}) collective-permute-start(f32[64,1024]{1,0:T(8,128)S(1)} %shard_map.103.refs_3_), channel_id=1, source_target_pairs={{0,1},{1,0},{2,3},{3,2},{4,5},{5,4},{6,7},{7,6},{8,9},{9,8},{10,11... | collective-permute-start | bytes 786440 | tf_op jit(solution)/shard_map/ppermute | solution.py:374
  50.9 8.2 %collective-permute-start.13 = (f32[64,1024]{1,0:T(8,128)S(1)}, f32[64,1024]{1,0:T(8,128)S(1)}, u32[]{:S(2)}, u32[]{:S(2)}) collective-permute-start(f32[64,1024]{1,0:T(8,128)S(1)} %shard_map.101.refs_4_), channel_id=1, source_target_pairs={{0,1},{1,0},{2,3},{3,2},{4,5},{5,4},{6,7},{7,6},{8,9},{9,8},{10,11... | collective-permute-start | bytes 786440 | tf_op jit(solution)/shard_map/ppermute | solution.py:374

commit v7 on v6

--- a/solution.py
+++ b/solution.py
@@ -361,9 +361,9 @@
     pick([(6, far, 0, width), (4, far, 0, subs[0])], [])
     sooner = pick([(2, arrived, 0, subs[0])], [])
     pick([(2, second, 0, subs[0])], [])
+    local = pick([(0, {**near, **arrived, **second}, 0, width)], [])
     for start, sub in list(zip(starts, subs))[1:]:
-        pick([(2, everything, start, sub), (4, far, start, sub)], sooner)
-    pick([(0, {**near, **arrived, **second}, 0, width)], [])
+        pick([(2, everything, start, sub), (4, far, start, sub)], sooner + local)
     smoothed = [
         smooth(tuple(plans[c]), table, sources[c], sub, tiles, block_count)
         for c, sub in enumerate(subs)

time: 60.8 us -> 60.8 us (level)
  transfers between devices with their start and end apart: 17 -> 17, of which waited for: 6 -> 7; matrix products, arithmetic and copies ran while one was open for 3% -> 3% of each run, Pallas kernels for 16% -> 16%
where the time goes in v7:
time: 60.8 us; the launch traced here: 60.5 us
  starting transfers between devices  22.7 us (37%)
  waiting for transfers between devices  22.3 us (37%)
  Pallas kernels  10.9 us (18%)
  local copies, waits for them, and re-layouts  3.85 us (6%)
    ppermute x13, starting transfers between devices, swap(): return lax.ppermute(value, 'fix', [(i, i ^ mask) for i in range(fix_count)])  15.4 us
    ppermute x13, waiting for transfers between devices, swap(): return lax.ppermute(value, 'fix', [(i, i ^ mask) for i in range(fix_count)])  13.8 us
    ppermute x2, waiting for transfers between devices, per_device(): parts.extend((lax.ppermute(value, 'subj', pairs) for value in smoothed))  6.04 us
    pallas_call x6, Pallas kernels, pack(): pl.pallas_call(functools.partial(pack_kernel, lists, cap, (len(tables), l...  5.41 us
    ppermute x2, starting transfers between devices, per_device(): parts.extend((lax.ppermute(value, 'subj', pairs) for value in smoothed))  3.17 us
    unnamed x14, local copies, waits for them, and re-layouts  2.84 us
    ppermute x1, starting transfers between devices, per_device(): far_raw[k] = lax.ppermute(raw, 'fix', pairs)  2.59 us
    ppermute x1, waiting for transfers between devices, per_device(): far_raw[k] = lax.ppermute(raw, 'fix', pairs)  2.5 us
  transfers between devices with their start and end apart: 17, of which 7 were waited for; matrix products, arithmetic and copies ran while one was open for 3% of the time, Pallas kernels for 16%

profile of v7, /device:TPU:0, one launch (start us, length us, event | category | flops | bytes accessed | tf_op | source)
XLA Modules:
  0.0 60.5 jit_solution(9447513819761462012)
XLA Ops:
  0.0 3.0 %collective-permute-start.8 = (f32[8,128,128]{2,1,0:T(8,128)}, f32[8,128,128]{2,1,0:T(8,128)S(1)}, u32[]{:S(2)}, u32[]{:S(2)}) collective-permute-start(f32[8,128,128]{2,1,0:T(8,128)} %bitcast.4), channel_id=1, source_target_pairs={{0,8},{2,10},{4,12},{6,14},{8,0},{10,2},{12,4},{14,6},{16,24},{18,... | collective-permute-start | bytes 1572872 | tf_op jit(solution)/shard_map/ppermute | solution.py:259
  3.0 2.6 %collective-permute-start.5 = (f32[8,128,128]{2,1,0:T(8,128)}, f32[8,128,128]{2,1,0:T(8,128)S(1)}, u32[]{:S(2)}, u32[]{:S(2)}) collective-permute-start(f32[8,128,128]{2,1,0:T(8,128)} %bitcast.5), channel_id=1, source_target_pairs={{0,16},{2,18},{4,20},{6,22},{8,24},{10,26},{12,28},{14,30},{16,0},... | collective-permute-start | bytes 1572872 | tf_op jit(solution)/shard_map/ppermute | solution.py:289
  5.8 0.8 %reshape.106 = s32[32]{0:T(128)S(1)} reshape(s32[4,8]{1,0:T(4,128)} %bitcast.13) | data formatting | bytes 256 | tf_op jit(solution)/shard_map/reshape | solution.py:261
  7.1 1.6 %collective-permute-start = (s32[1,32]{1,0:T(1,128)S(1)}, s32[1,32]{1,0:T(1,128)S(1)}, u32[]{:S(2)}, u32[]{:S(2)}) collective-permute-start(s32[1,32]{1,0:T(1,128)S(1)} %bitcast.10), channel_id=1, source_target_pairs={{0,4},{2,6},{4,0},{6,2},{8,12},{10,14},{12,8},{14,10},{16,20},{18,... | collective-permute-start | bytes 392 | tf_op jit(solution)/shard_map/ppermute | solution.py:259
  8.7 1.6 %copy-done.2 = f32[8,4,128,128]{3,2,1,0:T(8,128)S(1)} copy-done((f32[8,4,128,128]{3,2,1,0:T(8,128)S(1)}, f32[8,4,128,128]{3,2,1,0:T(8,128)}, u32[]{:S(2)}) %copy-start.2) | copy-done | bytes 2097176
  10.3 0.6 %shard_map.94.refs_3_.refs_5_.refs_6_ = bf16[32,128,256]{2,1,0:T(8,128)(2,1)S(1)} custom-call(f32[32,128,128]{2,1,0:T(8,128)S(1)} %bitcast.9), custom_call_target="tpu_custom_call" | custom-call | flops 2097152 | bytes 4194304 | tf_op jit(solution)/shard_map/pallas_call | solution.py:70
  11.2 1.6 %collective-permute-start.1 = (f32[72,128]{1,0:T(8,128)S(1)}, f32[72,128]{1,0:T(8,128)S(1)}, u32[]{:S(2)}, u32[]{:S(2)}) collective-permute-start(f32[72,128]{1,0:T(8,128)S(1)} %pad_maximum_fusion.1), channel_id=1, source_target_pairs={{0,1},{1,0},{2,3},{3,2},{4,5},{5,4},{6,7},{7,6},{8,9},{9,8},{10,11... | collective-permute-start | bytes 110600 | tf_op jit(solution)/shard_map/ppermute | solution.py:312
  12.8 1.0 %copy-done = f32[1024,128]{1,0:T(8,128)S(1)} copy-done((f32[1024,128]{1,0:T(8,128)S(1)}, f32[1024,128]{1,0:T(8,128)}, u32[]{:S(2)}) %copy-start) | copy-done | bytes 524312
  13.8 1.2 %shard_map.93 = f32[512,128]{1,0:T(8,128)S(1)} custom-call(s32[16]{0:T(128)S(1)} %mul.38.base_ref, s32[1,32]{1,0:T(1,128)S(1)} %collective-permute-done.refs_0_, f32[8,128,128]{2,1,0:T(8,128)S(1)} %bitcast.7, f32[8,128,128]{2,1,0:T(8,128)} %collective-permute-done.2.refs_2_), custom_call_target="tpu_custom_call" | custom-call | bytes 524288 | tf_op jit(solution)/shard_map/pallas_call | solution.py:101
  15.0 1.2 %collective-permute-start.3 = (f32[512,128]{1,0:T(8,128)S(1)}, f32[512,128]{1,0:T(8,128)S(1)}, u32[]{:S(2)}, u32[]{:S(2)}) collective-permute-start(f32[512,128]{1,0:T(8,128)S(1)} %shard_map.93), channel_id=1, source_target_pairs={{0,4},{2,6},{4,0},{6,2},{8,12},{10,14},{12,8},{14,10},{16,20},{18,... | collective-permute-start | bytes 786440 | tf_op jit(solution)/shard_map/ppermute | solution.py:259
  16.7 0.8 %shard_map.92 = (bf16[256,256]{1,0:T(8,128)(2,1)S(1)}, bf16[256,256]{1,0:T(8,128)(2,1)S(1)}, bf16[256,256]{1,0:T(8,128)(2,1)S(1)}, bf16[256,256]{1,0:T(8,128)(2,1)S(1)}) custom-call(f32[64,256]{1,0:T(8,128)S(1)} %slice.12.perm_ref, f32[4,256]{1,0:T(4,128)S(1)} %copy-done.4, f32[4,256]{1,0:T(4,128)S(1)} %get-tuple-element.24.nuisance_ref, ...), custom_call_target="tpu_custom_call" | custom-call | flops 2097152 | bytes 524288 | tf_op jit(solution)/shard_map/pallas_call | solution.py:184
  17.5 8.8 %collective-permute-done.4.refs_4_.refs_0_.refs_1_ = s32[2,32]{1,0:T(2,128)S(1)} collective-permute-done((s32[2,32]{1,0:T(2,128)S(1)}, s32[2,32]{1,0:T(2,128)S(1)}, u32[]{:S(2)}, u32[]{:S(2)}) %collective-permute-start.4) | collective-permute-done | bytes 288 | tf_op jit(solution)/shard_map/ppermute | solution.py:259
  26.3 2.5 %collective-permute-done.5.refs_0_ = f32[8,128,128]{2,1,0:T(8,128)S(1)} collective-permute-done((f32[8,128,128]{2,1,0:T(8,128)}, f32[8,128,128]{2,1,0:T(8,128)S(1)}, u32[]{:S(2)}, u32[]{:S(2)}) %collective-permute-start.5) | collective-permute-done | bytes 524320 | tf_op jit(solution)/shard_map/ppermute | solution.py:289
  29.3 0.7 %shard_map.99 = f32[256,128]{1,0:T(8,128)S(1)} custom-call(s32[16]{0:T(128)S(1)} %mul.38.base_ref, s32[1,32]{1,0:T(1,128)S(1)} %collective-permute-done.refs_0_, f32[8,128,128]{2,1,0:T(8,128)S(1)} %shard_map.97.refs_3_.refs_1_.refs_2_, f32[8,128,128]{2,1,0:T(8,128)S(1)} %shard_map.95.refs_2_.refs_4_.refs_3_.refs_6_), custom_call_target="tpu_custom_call" | custom-call | bytes 262144 | tf_op jit(solution)/shard_map/pallas_call | solution.py:101
  30.0 1.6 %collective-permute-start.10 = (f32[256,128]{1,0:T(8,128)S(1)}, f32[256,128]{1,0:T(8,128)S(1)}, u32[]{:S(2)}, u32[]{:S(2)}) collective-permute-start(f32[256,128]{1,0:T(8,128)S(1)} %shard_map.99), channel_id=1, source_target_pairs={{0,4},{2,6},{4,0},{6,2},{8,12},{10,14},{12,8},{14,10},{16,20},{18,... | collective-permute-start | bytes 393224 | tf_op jit(solution)/shard_map/ppermute | solution.py:259
  31.6 0.8 %shard_map.96 = (f32[512,128]{1,0:T(8,128)S(1)}, f32[256,128]{1,0:T(8,128)S(1)}) custom-call(s32[16]{0:T(128)S(1)} %mul.38.base_ref, s32[2,32]{1,0:T(2,128)S(1)} %collective-permute-done.4.refs_4_.refs_0_.refs_1_, s32[2,32]{1,0:T(2,128)S(1)} %collective-permute-done.4.refs_4_.refs_0_.refs_1_, f32[8,128,128]{2,1,0:T(8,128)S(1)} %shard_map.95.refs_2_.refs_4_.refs_3_.refs_6_, ...), custom_call_target="tpu_custom_call" | custom-call | bytes 786432 | tf_op jit(solution)/shard_map/pallas_call | solution.py:101
  32.9 0.7 %shard_map.102 = f32[256,128]{1,0:T(8,128)S(1)} custom-call(s32[16]{0:T(128)S(1)} %mul.38.base_ref, s32[1,32]{1,0:T(1,128)S(1)} %collective-permute-done.refs_0_, f32[8,128,128]{2,1,0:T(8,128)S(1)} %collective-permute-done.9.refs_5_.refs_4_.refs_1_, f32[8,128,128]{2,1,0:T(8,128)S(1)} %collective-permute-done.6.refs_3_.refs_5_.refs_6_.refs_7_.refs_2_), custom_call_target="tpu_custom_call" | custom-call | bytes 262144 | tf_op jit(solution)/shard_map/pallas_call | solution.py:101
  33.6 1.4 %collective-permute-start.15 = (f32[256,128]{1,0:T(8,128)S(1)}, f32[256,128]{1,0:T(8,128)S(1)}, u32[]{:S(2)}, u32[]{:S(2)}) collective-permute-start(f32[256,128]{1,0:T(8,128)S(1)} %shard_map.102), channel_id=1, source_target_pairs={{0,4},{2,6},{4,0},{6,2},{8,12},{10,14},{12,8},{14,10},{16,20},{18,... | collective-permute-start | bytes 393224 | tf_op jit(solution)/shard_map/ppermute | solution.py:259
  35.0 1.3 %shard_map.98.refs_9_.refs_2_.refs_5_ = f32[1536,128]{1,0:T(8,128)S(1)} custom-call(s32[16]{0:T(128)S(1)} %mul.38.base_ref, s32[1,32]{1,0:T(1,128)S(1)} %bitcast.12, f32[8,128,128]{2,1,0:T(8,128)S(1)} %bitcast.8, f32[8,128,128]{2,1,0:T(8,128)} %collective-permute-done.2.refs_2_, f32[8,128,128]{2,1,0:T(8,128)S(1)} %shard_map.97.refs_3_.refs_1_.refs_2_, ...), custom_call_target="tpu_custom_call" | custom-call | bytes 1572864 | tf_op jit(solution)/shard_map/pallas_call | solution.py:101
  36.4 3.3 %collective-permute-done.10.refs_8_.refs_3_ = f32[256,128]{1,0:T(8,128)S(1)} collective-permute-done((f32[256,128]{1,0:T(8,128)S(1)}, f32[256,128]{1,0:T(8,128)S(1)}, u32[]{:S(2)}, u32[]{:S(2)}) %collective-permute-start.10) | collective-permute-done | bytes 131104 | tf_op jit(solution)/shard_map/ppermute | solution.py:259
  39.6 0.8 %shard_map.100 = (f32[512,128]{1,0:T(8,128)S(1)}, f32[256,128]{1,0:T(8,128)S(1)}) custom-call(s32[16]{0:T(128)S(1)} %mul.38.base_ref, s32[1,32]{1,0:T(1,128)S(1)} %collective-permute-done.refs_0_, s32[2,32]{1,0:T(2,128)S(1)} %collective-permute-done.4.refs_4_.refs_0_.refs_1_, f32[8,128,128]{2,1,0:T(8,128)S(1)} %shard_map.97.refs_3_.refs_1_.refs_2_, ...), custom_call_target="tpu_custom_call" | custom-call | bytes 786432 | tf_op jit(solution)/shard_map/pallas_call | solution.py:101
  40.5 0.8 %collective-permute-start.12 = (f32[256,128]{1,0:T(8,128)S(1)}, f32[256,128]{1,0:T(8,128)S(1)}, u32[]{:S(2)}, u32[]{:S(2)}) collective-permute-start(f32[256,128]{1,0:T(8,128)S(1)} %get-tuple-element.17), channel_id=1, source_target_pairs={{0,8},{2,10},{4,12},{6,14},{8,0},{10,2},{12,4},{14,6},{16,24},{18,... | collective-permute-start | bytes 393224 | tf_op jit(solution)/shard_map/ppermute | solution.py:259
  41.2 1.3 %collective-permute-start.14 = (f32[256,128]{1,0:T(8,128)S(1)}, f32[256,128]{1,0:T(8,128)S(1)}, u32[]{:S(2)}, u32[]{:S(2)}) collective-permute-start(f32[256,128]{1,0:T(8,128)S(1)} %get-tuple-element.20), channel_id=1, source_target_pairs={{0,8},{2,10},{4,12},{6,14},{8,0},{10,2},{12,4},{14,6},{16,24},{18,... | collective-permute-start | bytes 393224 | tf_op jit(solution)/shard_map/ppermute | solution.py:259
  42.6 3.0 %collective-permute-start.11 = (f32[512,128]{1,0:T(8,128)S(1)}, f32[512,128]{1,0:T(8,128)S(1)}, u32[]{:S(2)}, u32[]{:S(2)}) collective-permute-start(f32[512,128]{1,0:T(8,128)S(1)} %get-tuple-element.16), channel_id=1, source_target_pairs={{0,4},{2,6},{4,0},{6,2},{8,12},{10,14},{12,8},{14,10},{16,20},{18,... | collective-permute-start | bytes 786440 | tf_op jit(solution)/shard_map/ppermute | solution.py:259
  45.5 1.4 %collective-permute-done.14.refs_2_ = f32[256,128]{1,0:T(8,128)S(1)} collective-permute-done((f32[256,128]{1,0:T(8,128)S(1)}, f32[256,128]{1,0:T(8,128)S(1)}, u32[]{:S(2)}, u32[]{:S(2)}) %collective-permute-start.14) | collective-permute-done | bytes 131104 | tf_op jit(solution)/shard_map/ppermute | solution.py:259
  46.9 1.1 %shard_map.103.refs_3_ = f32[64,1024]{1,0:T(8,128)S(1)} custom-call(s32[32]{0:T(128)S(1)} %broadcast_add_fusion.table_ref, f32[512,128]{1,0:T(8,128)S(1)} %collective-permute-done.3.refs_1_.refs_0_, f32[512,128]{1,0:T(8,128)S(1)} %collective-permute-done.7.refs_1_, f32[256,128]{1,0:T(8,128)S(1)} %collective-permute-done.14.refs_2_, ...), custom_call_target="tpu_custom_call" | custom-call | flops 268435456 | bytes 3145728 | tf_op jit(solution)/shard_map/pallas_call | solution.py:139
  48.0 1.6 %collective-permute-start.16 = (f32[64,1024]{1,0:T(8,128)S(1)}, f32[64,1024]{1,0:T(8,128)S(1)}, u32[]{:S(2)}, u32[]{:S(2)}) collective-permute-start(f32[64,1024]{1,0:T(8,128)S(1)} %shard_map.103.refs_3_), channel_id=1, source_target_pairs={{0,1},{1,0},{2,3},{3,2},{4,5},{5,4},{6,7},{7,6},{8,9},{9,8},{10,11... | collective-permute-start | bytes 786440 | tf_op jit(solution)/shard_map/ppermute | solution.py:374
  49.9 1.1 %shard_map.101.refs_4_ = f32[64,1024]{1,0:T(8,128)S(1)} custom-call(s32[32]{0:T(128)S(1)} %broadcast_add_fusion.table_ref, f32[512,128]{1,0:T(8,128)S(1)} %collective-permute-done.3.refs_1_.refs_0_, f32[512,128]{1,0:T(8,128)S(1)} %collective-permute-done.7.refs_1_, f32[1536,128]{1,0:T(8,128)S(1)} %shard_map.98.refs_9_.refs_2_.refs_5_, ...), custom_call_target="tpu_custom_call" | custom-call | flops 268435456 | bytes 3145728 | tf_op jit(solution)/shard_map/pallas_call | solution.py:139
  51.0 1.6 %collective-permute-start.13 = (f32[64,1024]{1,0:T(8,128)S(1)}, f32[64,1024]{1,0:T(8,128)S(1)}, u32[]{:S(2)}, u32[]{:S(2)}) collective-permute-start(f32[64,1024]{1,0:T(8,128)S(1)} %shard_map.101.refs_4_), channel_id=1, source_target_pairs={{0,1},{1,0},{2,3},{3,2},{4,5},{5,4},{6,7},{7,6},{8,9},{9,8},{10,11... | collective-permute-start | bytes 786440 | tf_op jit(solution)/shard_map/ppermute | solution.py:374
  52.6 3.8 %collective-permute-done.16.refs_5_ = f32[64,1024]{1,0:T(8,128)S(1)} collective-permute-done((f32[64,1024]{1,0:T(8,128)S(1)}, f32[64,1024]{1,0:T(8,128)S(1)}, u32[]{:S(2)}, u32[]{:S(2)}) %collective-permute-start.16) | collective-permute-done | bytes 262176 | tf_op jit(solution)/shard_map/ppermute | solution.py:374
  57.0 2.2 %collective-permute-done.13.refs_1_ = f32[64,1024]{1,0:T(8,128)S(1)} collective-permute-done((f32[64,1024]{1,0:T(8,128)S(1)}, f32[64,1024]{1,0:T(8,128)S(1)}, u32[]{:S(2)}, u32[]{:S(2)}) %collective-permute-start.13) | collective-permute-done | bytes 262176 | tf_op jit(solution)/shard_map/ppermute | solution.py:374
  59.2 1.2 %shard_map.105 = f32[256,1024]{1,0:T(8,128)} custom-call(bf16[256,256]{1,0:T(8,128)(2,1)S(1)} %get-tuple-element.13.refs_0_, f32[64,1024]{1,0:T(8,128)S(1)} %collective-permute-done.13.refs_1_, f32[256,1024]{1,0:T(8,128)S(1)} %shard_map.104.refs_2_), custom_call_target="tpu_custom_call" | custom-call | flops 134217728 | bytes 2097152 | tf_op jit(solution)/shard_map/pallas_call | solution.py:230
  (50 shorter events, 3.4 us)
Async XLA Ops:
  0.0 28.8 %collective-permute-start.8 = (f32[8,128,128]{2,1,0:T(8,128)}, f32[8,128,128]{2,1,0:T(8,128)S(1)}, u32[]{:S(2)}, u32[]{:S(2)}) collective-permute-start(f32[8,128,128]{2,1,0:T(8,128)} %bitcast.4), channel_id=1, source_target_pairs={{0,8},{2,10},{4,12},{6,14},{8,0},{10,2},{12,4},{14,6},{16,24},{18,... | collective-permute-start | bytes 1572872 | tf_op jit(solution)/shard_map/ppermute | solution.py:259
  3.0 25.8 %collective-permute-start.5 = (f32[8,128,128]{2,1,0:T(8,128)}, f32[8,128,128]{2,1,0:T(8,128)S(1)}, u32[]{:S(2)}, u32[]{:S(2)}) collective-permute-start(f32[8,128,128]{2,1,0:T(8,128)} %bitcast.5), channel_id=1, source_target_pairs={{0,16},{2,18},{4,20},{6,22},{8,24},{10,26},{12,28},{14,30},{16,0},... | collective-permute-start | bytes 1572872 | tf_op jit(solution)/shard_map/ppermute | solution.py:289
  5.6 7.1 %collective-permute-start.2 = (f32[8,128,128]{2,1,0:T(8,128)}, f32[8,128,128]{2,1,0:T(8,128)}, u32[]{:S(2)}, u32[]{:S(2)}) collective-permute-start(f32[8,128,128]{2,1,0:T(8,128)} %bitcast.6), channel_id=1, source_target_pairs={{0,2},{2,0},{4,6},{6,4},{8,10},{10,8},{12,14},{14,12},{16,18},{18,... | collective-permute-start | bytes 1572872 | tf_op jit(solution)/shard_map/ppermute | solution.py:259
  7.1 3.8 %collective-permute-start = (s32[1,32]{1,0:T(1,128)S(1)}, s32[1,32]{1,0:T(1,128)S(1)}, u32[]{:S(2)}, u32[]{:S(2)}) collective-permute-start(s32[1,32]{1,0:T(1,128)S(1)} %bitcast.10), channel_id=1, source_target_pairs={{0,4},{2,6},{4,0},{6,2},{8,12},{10,14},{12,8},{14,10},{16,20},{18,... | collective-permute-start | bytes 392 | tf_op jit(solution)/shard_map/ppermute | solution.py:259
  8.7 1.6 %copy-start.2 = (f32[8,4,128,128]{3,2,1,0:T(8,128)S(1)}, f32[8,4,128,128]{3,2,1,0:T(8,128)}, u32[]{:S(2)}) copy-start(f32[8,4,128,128]{3,2,1,0:T(8,128)} %param.10) | copy-start | bytes 6291460
  10.3 0.8 %copy-start.3 = (s32[128,128]{1,0:T(8,128)S(1)}, s32[128,128]{1,0:T(8,128)}, u32[]{:S(2)}) copy-start(s32[128,128]{1,0:T(8,128)} %value_ref.1) | copy-start | bytes 196612
  10.3 0.9 %copy-start.5 = (f32[4,128]{1,0:T(4,128)S(1)}, f32[4,128]{1,0:T(4,128)}, u32[]{:S(2)}) copy-start(f32[4,128]{1,0:T(4,128)} %param.13) | copy-start | bytes 6148
  10.3 0.9 %copy-start.6 = (f32[4,128]{1,0:T(4,128)S(1)}, f32[4,128]{1,0:T(4,128)}, u32[]{:S(2)}) copy-start(f32[4,128]{1,0:T(4,128)} %param.12) | copy-start | bytes 6148
  10.3 6.4 %copy-start.4 = (f32[4,256]{1,0:T(4,128)S(1)}, f32[4,256]{1,0:T(4,128)}, u32[]{:S(2)}) copy-start(f32[4,256]{1,0:T(4,128)} %contrast_ref.1) | copy-start | bytes 12292
  11.2 5.5 %collective-permute-start.1 = (f32[72,128]{1,0:T(8,128)S(1)}, f32[72,128]{1,0:T(8,128)S(1)}, u32[]{:S(2)}, u32[]{:S(2)}) collective-permute-start(f32[72,128]{1,0:T(8,128)S(1)} %pad_maximum_fusion.1), channel_id=1, source_target_pairs={{0,1},{1,0},{2,3},{3,2},{4,5},{5,4},{6,7},{7,6},{8,9},{9,8},{10,11... | collective-permute-start | bytes 110600 | tf_op jit(solution)/shard_map/ppermute | solution.py:312
  12.8 1.0 %copy-start = (f32[1024,128]{1,0:T(8,128)S(1)}, f32[1024,128]{1,0:T(8,128)}, u32[]{:S(2)}) copy-start(f32[1024,128]{1,0:T(8,128)} %param.9) | copy-start | bytes 1572868
  15.0 13.8 %collective-permute-start.3 = (f32[512,128]{1,0:T(8,128)S(1)}, f32[512,128]{1,0:T(8,128)S(1)}, u32[]{:S(2)}, u32[]{:S(2)}) collective-permute-start(f32[512,128]{1,0:T(8,128)S(1)} %shard_map.93), channel_id=1, source_target_pairs={{0,4},{2,6},{4,0},{6,2},{8,12},{10,14},{12,8},{14,10},{16,20},{18,... | collective-permute-start | bytes 786440 | tf_op jit(solution)/shard_map/ppermute | solution.py:259
  16.2 10.1 %collective-permute-start.4 = (s32[2,32]{1,0:T(2,128)S(1)}, s32[2,32]{1,0:T(2,128)S(1)}, u32[]{:S(2)}, u32[]{:S(2)}) collective-permute-start(s32[2,32]{1,0:T(2,128)S(1)} %pad_add_fusion), channel_id=1, source_target_pairs={{0,8},{2,10},{4,12},{6,14},{8,0},{10,2},{12,4},{14,6},{16,24},{18,... | collective-permute-start | bytes 776 | tf_op jit(solution)/shard_map/ppermute | solution.py:259
  28.8 2.7 %collective-permute-start.6 = (f32[8,128,128]{2,1,0:T(8,128)S(1)}, f32[8,128,128]{2,1,0:T(8,128)S(1)}, u32[]{:S(2)}, u32[]{:S(2)}) collective-permute-start(f32[8,128,128]{2,1,0:T(8,128)S(1)} %shard_map.95.refs_2_.refs_4_.refs_3_.refs_6_), channel_id=1, source_target_pairs={{0,2},{2,0},{4,6},{6,4},{8,10},{10,8},{12,14},{14,12},{16,18},{18,... | collective-permute-start | bytes 1572872 | tf_op jit(solution)/shard_map/ppermute | solution.py:259
  28.8 6.2 %copy-start.1 = (f32[1024,128]{1,0:T(8,128)S(1)}, f32[1024,128]{1,0:T(8,128)}, u32[]{:S(2)}) copy-start(f32[1024,128]{1,0:T(8,128)} %param.9) | copy-start | bytes 1572868
  28.9 4.1 %collective-permute-start.9 = (f32[8,128,128]{2,1,0:T(8,128)S(1)}, f32[8,128,128]{2,1,0:T(8,128)S(1)}, u32[]{:S(2)}, u32[]{:S(2)}) collective-permute-start(f32[8,128,128]{2,1,0:T(8,128)S(1)} %shard_map.97.refs_3_.refs_1_.refs_2_), channel_id=1, source_target_pairs={{0,2},{2,0},{4,6},{6,4},{8,10},{10,8},{12,14},{14,12},{16,18},{18,... | collective-permute-start | bytes 1572872 | tf_op jit(solution)/shard_map/ppermute | solution.py:259
  30.0 9.6 %collective-permute-start.10 = (f32[256,128]{1,0:T(8,128)S(1)}, f32[256,128]{1,0:T(8,128)S(1)}, u32[]{:S(2)}, u32[]{:S(2)}) collective-permute-start(f32[256,128]{1,0:T(8,128)S(1)} %shard_map.99), channel_id=1, source_target_pairs={{0,4},{2,6},{4,0},{6,2},{8,12},{10,14},{12,8},{14,10},{16,20},{18,... | collective-permute-start | bytes 393224 | tf_op jit(solution)/shard_map/ppermute | solution.py:259
  32.3 14.6 %collective-permute-start.7 = (f32[512,128]{1,0:T(8,128)S(1)}, f32[512,128]{1,0:T(8,128)S(1)}, u32[]{:S(2)}, u32[]{:S(2)}) collective-permute-start(f32[512,128]{1,0:T(8,128)S(1)} %get-tuple-element.15), channel_id=1, source_target_pairs={{0,12},{2,14},{4,8},{6,10},{8,4},{10,6},{12,0},{14,2},{16,28},{18,... | collective-permute-start | bytes 786440 | tf_op jit(solution)/shard_map/ppermute | solution.py:259
  33.6 12.0 %collective-permute-start.15 = (f32[256,128]{1,0:T(8,128)S(1)}, f32[256,128]{1,0:T(8,128)S(1)}, u32[]{:S(2)}, u32[]{:S(2)}) collective-permute-start(f32[256,128]{1,0:T(8,128)S(1)} %shard_map.102), channel_id=1, source_target_pairs={{0,4},{2,6},{4,0},{6,2},{8,12},{10,14},{12,8},{14,10},{16,20},{18,... | collective-permute-start | bytes 393224 | tf_op jit(solution)/shard_map/ppermute | solution.py:259
  40.5 9.1 %collective-permute-start.12 = (f32[256,128]{1,0:T(8,128)S(1)}, f32[256,128]{1,0:T(8,128)S(1)}, u32[]{:S(2)}, u32[]{:S(2)}) collective-permute-start(f32[256,128]{1,0:T(8,128)S(1)} %get-tuple-element.17), channel_id=1, source_target_pairs={{0,8},{2,10},{4,12},{6,14},{8,0},{10,2},{12,4},{14,6},{16,24},{18,... | collective-permute-start | bytes 393224 | tf_op jit(solution)/shard_map/ppermute | solution.py:259
  41.2 5.7 %collective-permute-start.14 = (f32[256,128]{1,0:T(8,128)S(1)}, f32[256,128]{1,0:T(8,128)S(1)}, u32[]{:S(2)}, u32[]{:S(2)}) collective-permute-start(f32[256,128]{1,0:T(8,128)S(1)} %get-tuple-element.20), channel_id=1, source_target_pairs={{0,8},{2,10},{4,12},{6,14},{8,0},{10,2},{12,4},{14,6},{16,24},{18,... | collective-permute-start | bytes 393224 | tf_op jit(solution)/shard_map/ppermute | solution.py:259
  42.6 7.3 %collective-permute-start.11 = (f32[512,128]{1,0:T(8,128)S(1)}, f32[512,128]{1,0:T(8,128)S(1)}, u32[]{:S(2)}, u32[]{:S(2)}) collective-permute-start(f32[512,128]{1,0:T(8,128)S(1)} %get-tuple-element.16), channel_id=1, source_target_pairs={{0,4},{2,6},{4,0},{6,2},{8,12},{10,14},{12,8},{14,10},{16,20},{18,... | collective-permute-start | bytes 786440 | tf_op jit(solution)/shard_map/ppermute | solution.py:259
  48.0 8.4 %collective-permute-start.16 = (f32[64,1024]{1,0:T(8,128)S(1)}, f32[64,1024]{1,0:T(8,128)S(1)}, u32[]{:S(2)}, u32[]{:S(2)}) collective-permute-start(f32[64,1024]{1,0:T(8,128)S(1)} %shard_map.103.refs_3_), channel_id=1, source_target_pairs={{0,1},{1,0},{2,3},{3,2},{4,5},{5,4},{6,7},{7,6},{8,9},{9,8},{10,11... | collective-permute-start | bytes 786440 | tf_op jit(solution)/shard_map/ppermute | solution.py:374
  51.0 8.2 %collective-permute-start.13 = (f32[64,1024]{1,0:T(8,128)S(1)}, f32[64,1024]{1,0:T(8,128)S(1)}, u32[]{:S(2)}, u32[]{:S(2)}) collective-permute-start(f32[64,1024]{1,0:T(8,128)S(1)} %shard_map.101.refs_4_), channel_id=1, source_target_pairs={{0,1},{1,0},{2,3},{3,2},{4,5},{5,4},{6,7},{7,6},{8,9},{9,8},{10,11... | collective-permute-start | bytes 786440 | tf_op jit(solution)/shard_map/ppermute | solution.py:374
